TPU v7x, 32 devices: a whole 2x2x4 slice. The times are simulated.
32 devices in a mesh: dp: 4 (over y, x), row: 2 (over core), col: 4 (over z).
Axes of the slice: x: 2, y: 2, z: 4, core: 2. Of those that a mesh axis runs over, the one named last changes fastest.
Arguments:
- pixels: bfloat16 [2, 6304, 768], P(None, ('dp', 'col'), 'row'), may hold values from -6 to 6
- patch_mask: int32 [2, 6304], P(None, 'dp'), may hold values from 0 to 1
- class_ids: int32 [2, 32], P(None, 'dp'), may hold values from 0 to 999
- class_counts: int32 [1000], replicated, may hold values from 16 to 64
- step_count: int32 [], replicated, may hold values from 1 to 20
- weight_qkv: bfloat16 [2, 768, 2304], P(None, 'col', 'row'), may hold values from -0.21875 to 0.21875
- weight_out: bfloat16 [2, 768, 768], P(None, 'row', 'col'), may hold values from -1 to 1
- weight_up: bfloat16 [2, 768, 3072], P(None, 'col', 'row'), may hold values from -0.21875 to 0.21875
- weight_down: bfloat16 [2, 3072, 768], P(None, 'row', 'col'), may hold values from -0.109375 to 0.109375
- weight_ends: bfloat16 [2, 768, 768], P(None, 'row', 'col'), may hold values from -0.21875 to 0.21875
- vectors: float32 [227, 768], replicated, may hold values from -3 to 3
- vector_moment: float32 [227, 768], replicated, may hold values from -2.861023e-06 to 2.861023e-06
- vector_second: float32 [227, 768], replicated, may hold values from 2.8765455e-15 to 1.1506182e-14
- ends_moment: float32 [2, 768, 768], P(None, 'row', 'col'), may hold values from -9.536743e-07 to 9.536743e-07
- ends_second: float32 [2, 768, 768], P(None, 'row', 'col'), may hold values from 3.1961616e-16 to 1.2784646e-15
- stat_left: float32 [8, 192, 96, 96], P(('row', 'col'), 'dp'), may hold values from -4.602473e-12 to 1.2886924e-10, as said below
- stat_right: float32 [8, 192, 96, 96], P(('row', 'col'), 'dp'), may hold values from -4.602473e-12 to 1.2886924e-10, as said below
- root_left: float32 [8, 192, 96, 96], P(('row', 'col'), 'dp'), may hold values from -42.488853 to 892.2659
- root_right: float32 [8, 192, 96, 96], P(('row', 'col'), 'dp'), may hold values from -42.488853 to 892.2659
- owner_map: int32 [8, 192], P(('row', 'col')), may hold values from 0 to 191, each once within a row
Outputs:
- loss_total: float32 [], replicated
- grad_norm: float32 [], replicated
- vector_next: float32 [227, 768], replicated
- moment_vector: float32 [227, 768], replicated
- second_vector: float32 [227, 768], replicated
- ends_next: float32 [2, 768, 768], P(None, 'row', 'col')
- moment_ends: float32 [2, 768, 768], P(None, 'row', 'col')
- second_ends: float32 [2, 768, 768], P(None, 'row', 'col')
- block_grad: float32 [8, 192, 96, 96], P(('row', 'col'), 'dp')
- left_next: float32 [8, 192, 96, 96], P(('row', 'col'), 'dp')
- right_next: float32 [8, 192, 96, 96], P(('row', 'col'), 'dp')
- block_next: float32 [8, 192, 96, 96], P(('row', 'col'), 'dp')
Inputs may be any that keep to these rules, and one draw needn't show every extreme that they name: `owner_map`: each row names every block once. `stat_left`: symmetric. `stat_right`: symmetric.
All inputs are finite; a program needn't handle non-finite values.
Results may differ from a plain program's by a relative error of at most 0.00074.
Values may be sent and summed in bfloat16 or wider, within the bound.
No kernel may reach another device: no remote copies, remote signals or barrier semaphores. Data moves between devices by JAX's collectives and lax.ppermute only.
A program may use at most 384 MiB of HBM per device.

v0:
```python
from functools import partial
import math

import jax
import jax.numpy as jnp
from jax import lax
from jax.sharding import PartitionSpec as P

HD = 64
PATCH = 768
L = 197
BLK = 96


norm_eps = 1e-06
beta_first = 0.9
beta_second = 0.999
adam_eps = 1e-08
decay_stat = 0.5
rate_matrix = 0.02
rate_vector = 0.2
rate_blocks = 0.1
weight_decay = 0.05
clip_scale = 0.25
highest = lax.Precision.HIGHEST


def matmul(lhs_mat, rhs_mat, lhs_dim, rhs_dim):
    return lax.dot_general(
        lhs_mat, rhs_mat, (((lhs_dim,), (rhs_dim,)), ((), ())), preferred_element_type=jnp.float32
    )


def exact_dot(lhs_mat, rhs_mat, lhs_dim, rhs_dim):
    return lax.dot_general(
        lhs_mat, rhs_mat, (((lhs_dim,), (rhs_dim,)), ((), ())), precision=highest
    )


def gather_rows(value):
    return lax.all_gather(value, "row", axis=0, tiled=True)


def gather_cols(value):
    return lax.all_gather(value, "col", axis=0, tiled=True)


def sum_over_rows(value):
    return lax.psum_scatter(value, "row", scatter_dimension=0, tiled=True)


def sum_over_cols(value):
    return lax.psum_scatter(value, "col", scatter_dimension=0, tiled=True)


def col_totals(pair):
    return lax.psum((pair[0], pair[1]), "col")


def grid_forward(inputs, weight, weight_dim, by_rows):
    if by_rows:
        full_in = gather_rows(inputs)
        return (full_in, sum_over_cols(matmul(full_in, weight, 1, weight_dim)))
    full_in = gather_cols(inputs)
    return (full_in, sum_over_rows(matmul(full_in, weight, 1, weight_dim)))


def grid_backward(full_in, weight, weight_dim, by_rows, grad_low, need_input):
    full_grad = gather_cols(grad_low) if by_rows else gather_rows(grad_low)
    if weight_dim == 0:
        weight_grad = matmul(full_in, full_grad, 0, 0)
    else:
        weight_grad = matmul(full_grad, full_in, 0, 0)
    if not need_input:
        return (weight_grad, None)
    partial_sum = matmul(full_grad, weight, 1, 1 - weight_dim)
    return (weight_grad, sum_over_rows(partial_sum) if by_rows else sum_over_cols(partial_sum))


def norm_forward(residual, gain, shift, model_width):
    totals = col_totals((jnp.sum(residual, axis=1), jnp.sum(residual * residual, axis=1)))
    mean_rows = totals[0] / model_width
    inverse = lax.rsqrt(totals[1] / model_width - mean_rows * mean_rows + norm_eps)
    normed = (residual - mean_rows[:, None]) * inverse[:, None]
    return (normed, inverse, normed * gain + shift)


def norm_backward(grad_normed, normed, inverse, gain, model_width):
    scaled = grad_normed * gain
    totals = col_totals((jnp.sum(scaled, axis=1), jnp.sum(scaled * normed, axis=1)))
    grad_in = inverse[:, None] * (
        scaled - totals[0][:, None] / model_width - normed * totals[1][:, None] / model_width
    )
    return (grad_in, jnp.sum(grad_normed * normed, axis=0), jnp.sum(grad_normed, axis=0))


def attend_forward(mixed_qkv, heads_loc):
    images = mixed_qkv.shape[0] // L
    split_view = mixed_qkv.reshape(images, L, heads_loc, 3, HD)
    queries = (split_view[:, :, :, 0] * 0.125).astype(jnp.bfloat16)
    key_rows = split_view[:, :, :, 1].astype(jnp.bfloat16)
    values = split_view[:, :, :, 2].astype(jnp.bfloat16)
    scores = jnp.einsum("bqhd,bkhd->bhqk", queries, key_rows, preferred_element_type=jnp.float32)
    top_score = jnp.max(scores, axis=-1, keepdims=True)
    exponent = jnp.exp(scores - top_score)
    denominator = jnp.sum(exponent, axis=-1, keepdims=True)
    attend = (exponent / denominator).astype(jnp.bfloat16)
    context = jnp.einsum("bhqk,bkhd->bqhd", attend, values, preferred_element_type=jnp.float32)
    context = context.astype(jnp.bfloat16).reshape(images * L, heads_loc * HD)
    return (context, (queries, key_rows, values, top_score + jnp.log(denominator)))


def attend_backward(grad_context, kept_attend):
    queries, key_rows, values, log_total = kept_attend
    images = queries.shape[0]
    heads_loc = queries.shape[2]
    grad_low = grad_context.astype(jnp.bfloat16).reshape(images, L, heads_loc, HD)
    scores = jnp.einsum("bqhd,bkhd->bhqk", queries, key_rows, preferred_element_type=jnp.float32)
    attend = jnp.exp(scores - log_total)
    grad_values = jnp.einsum(
        "bhqk,bqhd->bkhd", attend.astype(jnp.bfloat16), grad_low, preferred_element_type=jnp.float32
    )
    grad_attend = jnp.einsum(
        "bqhd,bkhd->bhqk", grad_low, values, preferred_element_type=jnp.float32
    )
    grad_scores = attend * (grad_attend - jnp.sum(grad_attend * attend, axis=-1, keepdims=True))
    grad_scores = grad_scores.astype(jnp.bfloat16)
    grad_queries = (
        jnp.einsum("bhqk,bkhd->bqhd", grad_scores, key_rows, preferred_element_type=jnp.float32)
        * 0.125
    )
    grad_keys = jnp.einsum(
        "bhqk,bqhd->bkhd", grad_scores, queries, preferred_element_type=jnp.float32
    )
    stacked = jnp.stack([grad_queries, grad_keys, grad_values], axis=3)
    return stacked.astype(jnp.bfloat16).reshape(images * L, heads_loc * 3 * HD)


def add_into(target, row_start, col_start, additions):
    current = lax.dynamic_slice(target, (row_start, col_start), additions.shape)
    return lax.dynamic_update_slice(target, current + additions, (row_start, col_start))


def cut_blocks(tile_mat):
    shaped = tile_mat.reshape(tile_mat.shape[0] // BLK, BLK, tile_mat.shape[1] // BLK, BLK)
    return shaped.transpose(0, 2, 1, 3).reshape(-1, BLK, BLK)


def all_blocks(stacks):
    pieces = []
    for layer_idx in range(stacks[0].shape[0]):
        for stack_mat in stacks:
            pieces.append(cut_blocks(stack_mat[layer_idx]))
    return jnp.concatenate(pieces, axis=0)


def adam_update(weight, gradient, moment, second, rate, decay, factor, step_value):
    clipped = gradient * factor
    moment_new = beta_first * moment + (1.0 - beta_first) * clipped
    second_new = beta_second * second + (1.0 - beta_second) * clipped * clipped
    corr_first = 1.0 - jnp.power(beta_first, step_value)
    corr_second = 1.0 - jnp.power(beta_second, step_value)
    stride = moment_new / corr_first / (jnp.sqrt(second_new / corr_second) + adam_eps)
    return (weight - rate * (stride + decay * weight), moment_new, second_new)


def shards(
    pixels,
    patch_mask,
    class_ids,
    class_counts,
    step_count,
    weight_qkv,
    weight_out,
    weight_up,
    weight_down,
    weight_ends,
    vectors,
    vector_moment,
    vector_second,
    ends_moment,
    ends_second,
    stat_left,
    stat_right,
    root_left,
    root_right,
    owner_map,
):
    row_count = lax.axis_size("row")
    col_count = lax.axis_size("col")
    data_count = lax.axis_size("dp")
    row_index = lax.axis_index("row")
    col_index = lax.axis_index("col")
    data_index = lax.axis_index("dp")
    micro_count = pixels.shape[0]
    col_tok = pixels.shape[1]
    group_tok = col_tok * col_count
    row_tok = group_tok // row_count
    model_width = vectors.shape[1]
    layer_count = weight_qkv.shape[0]
    use_qkv, use_out, use_up, use_down, use_ends = (
        weight_qkv,
        weight_out,
        weight_up,
        weight_down,
        weight_ends,
    )
    res_start = row_index * row_tok
    col_width = use_qkv.shape[1]
    heads_loc = use_qkv.shape[2] // (3 * HD)
    ff_part = use_up.shape[2]
    patch_part = use_ends.shape[1]
    col_start = col_index * col_width

    def col_part(row_at):
        return lax.dynamic_slice_in_dim(vectors[row_at], col_start, col_width)

    def row_part(flat_vec, span_size):
        return lax.dynamic_slice_in_dim(flat_vec, row_index * span_size, span_size)

    def layer_backward(grad_res, layer_idx, kept_state, grad_vec):
        (
            normed_one,
            inverse_one,
            norm_full_one,
            kept_attend,
            context_full,
            normed_two,
            inverse_two,
            norm_full_two,
            hidden_pre,
            active_full,
        ) = kept_state
        row_base = L + 6 + 12 * layer_idx
        grad_low = grad_res.astype(jnp.bfloat16)
        grad_down, grad_active = grid_backward(
            active_full, use_down[layer_idx], 0, False, grad_low, True
        )
        down_bias = jnp.sum(grad_low.astype(jnp.float32), axis=0)
        gelu_pull = jax.vjp(partial(jax.nn.gelu, approximate=False), hidden_pre)[1]
        grad_hidden = gelu_pull(grad_active)[0].astype(jnp.bfloat16)
        up_bias = jnp.sum(grad_hidden.astype(jnp.float32), axis=0)
        grad_up, grad_norm_two = grid_backward(
            norm_full_two, use_up[layer_idx], 0, True, grad_hidden, True
        )
        grad_in_two, gain_two, shift_two = norm_backward(
            grad_norm_two, normed_two, inverse_two, col_part(row_base + 5), model_width
        )
        grad_mid = grad_res + grad_in_two
        grad_mid_low = grad_mid.astype(jnp.bfloat16)
        grad_proj, grad_context = grid_backward(
            context_full, use_out[layer_idx], 0, False, grad_mid_low, True
        )
        out_bias = jnp.sum(grad_mid_low.astype(jnp.float32), axis=0)
        grad_mixed = attend_backward(grad_context, kept_attend)
        mixed_bias = jnp.sum(grad_mixed.astype(jnp.float32), axis=0).reshape(heads_loc, 3, HD)
        grad_qkv_tile, grad_norm_one = grid_backward(
            norm_full_one, use_qkv[layer_idx], 0, True, grad_mixed, True
        )
        grad_in_one, gain_one, shift_one = norm_backward(
            grad_norm_one, normed_one, inverse_one, col_part(row_base), model_width
        )
        grad_vec = add_into(grad_vec, row_base, col_start, jnp.stack([gain_one, shift_one]))
        grad_vec = add_into(
            grad_vec,
            row_base + 2,
            row_index * heads_loc * HD,
            jnp.stack([mixed_bias[:, 0].reshape(-1), mixed_bias[:, 2].reshape(-1)]),
        )
        grad_vec = add_into(grad_vec, row_base + 4, col_start, out_bias[None])
        grad_vec = add_into(grad_vec, row_base + 5, col_start, jnp.stack([gain_two, shift_two]))
        grad_vec = add_into(
            grad_vec,
            row_base + 7 + row_index * (ff_part // model_width),
            0,
            up_bias.reshape(-1, model_width),
        )
        grad_vec = add_into(grad_vec, row_base + 11, col_start, down_bias[None])
        return (grad_mid + grad_in_one, (grad_qkv_tile, grad_proj, grad_up, grad_down), grad_vec)

    position_group = jnp.arange(group_tok) % L
    live_group = ((patch_mask > 0) & (position_group != 0)[None, :]).astype(jnp.float32)
    count_all = lax.psum(jnp.sum(live_group), "dp")
    class_table = (
        class_ids[:, :, None] == jnp.arange(class_counts.shape[0])[None, None, :]
    ).astype(jnp.float32)
    image_weight = 32.0 / jnp.sum(class_table * class_counts.astype(jnp.float32), axis=2)
    image_col = col_tok // L
    weight_tok = jnp.repeat(
        lax.dynamic_slice_in_dim(image_weight, col_index * image_col, image_col, 1), L, axis=1
    )
    keep_col = weight_tok * lax.dynamic_slice_in_dim(live_group, col_index * col_tok, col_tok, 1)
    mask_res = lax.dynamic_slice_in_dim(patch_mask, res_start, row_tok, 1)
    position_res = (res_start + jnp.arange(row_tok)) % L
    onehot = (position_res[:, None] == jnp.arange(L)[None, :]).astype(jnp.float32)
    first_res = (position_res == 0)[:, None]
    pos_local = lax.dynamic_slice_in_dim(vectors[:L], col_start, col_width, 1)
    loss_scale = 1.0 / (PATCH * count_all)
    grad_qkv = jnp.zeros(use_qkv.shape, jnp.float32)
    grad_outs = jnp.zeros(use_out.shape, jnp.float32)
    grad_ups = jnp.zeros(use_up.shape, jnp.float32)
    grad_downs = jnp.zeros(use_down.shape, jnp.float32)
    grad_ends = jnp.zeros(use_ends.shape, jnp.float32)
    grad_vec = jnp.zeros(vectors.shape, jnp.float32)
    loss_local = jnp.float32(0.0)
    for micro_idx in range(micro_count):
        pix_low = pixels[micro_idx]
        hidden_res = (mask_res[micro_idx] > 0)[:, None]
        pix_full, embedded = grid_forward(pix_low, use_ends[0], 0, False)
        embedded = embedded + col_part(L + 2)
        residual = jnp.where(
            first_res, col_part(L), jnp.where(hidden_res, col_part(L + 1), embedded)
        )
        residual = residual + jnp.dot(onehot, pos_local, precision=highest)
        kept_layers = []
        for layer_idx in range(layer_count):
            layer_row_base = L + 6 + 12 * layer_idx
            layer_normed_one, layer_inverse_one, scaled_one = norm_forward(
                residual, col_part(layer_row_base), col_part(layer_row_base + 1), model_width
            )
            layer_norm_full_one, mixed_qkv = grid_forward(
                scaled_one.astype(jnp.bfloat16), use_qkv[layer_idx], 0, True
            )
            qkv_span_size = heads_loc * HD
            query_bias = row_part(vectors[layer_row_base + 2], qkv_span_size).reshape(
                heads_loc, 1, HD
            )
            value_bias = row_part(vectors[layer_row_base + 3], qkv_span_size).reshape(
                heads_loc, 1, HD
            )
            context, layer_kept_attend = attend_forward(
                mixed_qkv
                + jnp.concatenate(
                    [query_bias, jnp.zeros_like(query_bias), value_bias], axis=1
                ).reshape(-1),
                heads_loc,
            )
            layer_context_full, branch = grid_forward(context, use_out[layer_idx], 0, False)
            residual_mid = residual + (branch + col_part(layer_row_base + 4))
            layer_normed_two, layer_inverse_two, scaled_two = norm_forward(
                residual_mid,
                col_part(layer_row_base + 5),
                col_part(layer_row_base + 6),
                model_width,
            )
            layer_norm_full_two, layer_hidden_pre = grid_forward(
                scaled_two.astype(jnp.bfloat16), use_up[layer_idx], 0, True
            )
            layer_hidden_pre = layer_hidden_pre + row_part(
                vectors[layer_row_base + 7 : layer_row_base + 11].reshape(-1), ff_part
            )
            active = jax.nn.gelu(layer_hidden_pre, approximate=False).astype(jnp.bfloat16)
            layer_active_full, branch_two = grid_forward(active, use_down[layer_idx], 0, False)
            residual_out = residual_mid + (branch_two + col_part(layer_row_base + 11))
            layer_kept_state = (
                layer_normed_one,
                layer_inverse_one,
                layer_norm_full_one,
                layer_kept_attend,
                layer_context_full,
                layer_normed_two,
                layer_inverse_two,
                layer_norm_full_two,
                layer_hidden_pre,
                layer_active_full,
            )
            residual = residual_out
            kept_state = layer_kept_state
            kept_layers.append(kept_state)
        normed_fin, inverse_fin, scaled_fin = norm_forward(
            residual, col_part(L + 3), col_part(L + 4), model_width
        )
        final_full, predict = grid_forward(scaled_fin.astype(jnp.bfloat16), use_ends[1], 1, True)
        pred_error = predict + row_part(vectors[L + 5], patch_part) - pix_low.astype(jnp.float32)
        keep_rows = keep_col[micro_idx][:, None]
        loss_local = loss_local + jnp.sum(keep_rows * pred_error * pred_error) * loss_scale
        grad_pred = (2.0 * loss_scale * keep_rows * pred_error).astype(jnp.bfloat16)
        grad_vec = add_into(
            grad_vec,
            L + 5,
            row_index * patch_part,
            jnp.sum(grad_pred.astype(jnp.float32), axis=0)[None],
        )
        head_grad, grad_final = grid_backward(final_full, use_ends[1], 1, True, grad_pred, True)
        grad_ends = grad_ends.at[1].add(head_grad)
        grad_res, gain_fin, shift_fin = norm_backward(
            grad_final, normed_fin, inverse_fin, col_part(L + 3), model_width
        )
        grad_vec = add_into(grad_vec, L + 3, col_start, jnp.stack([gain_fin, shift_fin]))
        for layer_idx in reversed(range(layer_count)):
            grad_res, layer_grads, grad_vec = layer_backward(
                grad_res, layer_idx, kept_layers[layer_idx], grad_vec
            )
            grad_qkv = grad_qkv.at[layer_idx].add(layer_grads[0])
            grad_outs = grad_outs.at[layer_idx].add(layer_grads[1])
            grad_ups = grad_ups.at[layer_idx].add(layer_grads[2])
            grad_downs = grad_downs.at[layer_idx].add(layer_grads[3])
        grad_vec = add_into(grad_vec, 0, col_start, exact_dot(onehot, grad_res, 0, 0))
        patch_rows = jnp.logical_not(first_res) & jnp.logical_not(hidden_res)
        mask_rows = jnp.logical_not(first_res) & hidden_res
        class_grad = jnp.sum(jnp.where(first_res, grad_res, 0.0), axis=0)
        token_grad = jnp.sum(jnp.where(mask_rows, grad_res, 0.0), axis=0)
        grad_embed = jnp.where(patch_rows, grad_res, 0.0).astype(jnp.bfloat16)
        embed_bias = jnp.sum(grad_embed.astype(jnp.float32), axis=0)
        grad_vec = add_into(grad_vec, L, col_start, jnp.stack([class_grad, token_grad, embed_bias]))
        embed_grad, unused = grid_backward(pix_full, use_ends[0], 0, False, grad_embed, False)
        grad_ends = grad_ends.at[0].add(embed_grad)
    slot_order = owner_map[0]
    per_owner = slot_order.shape[0] // data_count
    summed = lax.psum((grad_qkv, grad_outs, grad_ups, grad_downs, grad_ends), "dp")
    slot_blocks = jnp.take(all_blocks(summed[:4]), slot_order, axis=0)
    own_grad = lax.dynamic_slice_in_dim(slot_blocks, data_index * per_owner, per_owner, 0)
    ends_grad = summed[4]
    weight_slots = jnp.take(
        all_blocks((weight_qkv, weight_out, weight_up, weight_down)), slot_order, axis=0
    )
    own_weight = lax.dynamic_slice_in_dim(
        weight_slots, data_index * per_owner, per_owner, 0
    ).astype(jnp.float32)
    vec_sum, loss_total = lax.psum((grad_vec, loss_local), ("dp", "row", "col"))
    ends_square = jnp.where(data_index == 0, jnp.sum(ends_grad * ends_grad), 0.0)
    norm_square = lax.psum(jnp.sum(own_grad * own_grad) + ends_square, ("dp", "row", "col"))
    grad_norm = jnp.sqrt(norm_square + jnp.sum(vec_sum * vec_sum))
    total_tokens = micro_count * data_count * group_tok
    factor = jnp.minimum(1.0, clip_scale / math.sqrt(total_tokens) / grad_norm)
    step_value = step_count.astype(jnp.float32)
    vector_next, moment_vector, second_vector = adam_update(
        vectors, vec_sum, vector_moment, vector_second, rate_vector, 0.0, factor, step_value
    )
    ends_next, moment_ends, second_ends = adam_update(
        weight_ends.astype(jnp.float32),
        ends_grad,
        ends_moment,
        ends_second,
        rate_matrix,
        weight_decay,
        factor,
        step_value,
    )
    block_grad = own_grad * factor
    left_next = decay_stat * stat_left[0] + (1.0 - decay_stat) * jnp.einsum(
        "sij,skj->sik", block_grad, block_grad, precision=highest
    )
    right_next = decay_stat * stat_right[0] + (1.0 - decay_stat) * jnp.einsum(
        "sji,sjk->sik", block_grad, block_grad, precision=highest
    )
    inner_prod = jnp.einsum("sij,sjk->sik", block_grad, root_right[0], precision=highest)
    precond = jnp.einsum("sij,sjk->sik", root_left[0], inner_prod, precision=highest)
    block_next = own_weight - rate_blocks * (precond + weight_decay * own_weight)
    return (
        loss_total,
        grad_norm,
        vector_next,
        moment_vector,
        second_vector,
        ends_next,
        moment_ends,
        second_ends,
        block_grad[None],
        left_next[None],
        right_next[None],
        block_next[None],
    )


def solution(mesh):
    return jax.shard_map(
        shards,
        mesh=mesh,
        in_specs=(
            P(None, ("dp", "col"), "row"),
            P(None, "dp"),
            P(None, "dp"),
            P(),
            P(),
            P(None, "col", "row"),
            P(None, "row", "col"),
            P(None, "col", "row"),
            P(None, "row", "col"),
            P(None, "row", "col"),
            P(),
            P(),
            P(),
            P(None, "row", "col"),
            P(None, "row", "col"),
            P(("row", "col"), "dp", None, None),
            P(("row", "col"), "dp", None, None),
            P(("row", "col"), "dp", None, None),
            P(("row", "col"), "dp", None, None),
            P(("row", "col"), None),
        ),
        out_specs=(
            P(),
            P(),
            P(),
            P(),
            P(),
            P(None, "row", "col"),
            P(None, "row", "col"),
            P(None, "row", "col"),
            P(("row", "col"), "dp", None, None),
            P(("row", "col"), "dp", None, None),
            P(("row", "col"), "dp", None, None),
            P(("row", "col"), "dp", None, None),
        ),
        check_vma=False,
    )
```

profile of v0, /device:TPU:0, one launch (start us, length us, event | category | flops | bytes accessed | tf_op | source)
XLA Modules:
  0.0 4894.7 jit_solution(8518428075347837108)
XLA Ops:
  12.1 53.6 %all-gather.63.cloned.1.call-done = bf16[1,1576,384]{2,0,1:T(2,128)(2,1)} async-done(((bf16[1,394,384]{2,0,1:T(2,128)(2,1)}), bf16[1,1576,384]{2,0,1:T(2,128)(2,1)}) %all-gather.63.cloned.1.call-update) | async-done | bytes 1210384 | tf_op jit(solution)/shard_map/all_gather | solution.py:45
  69.0 49.1 %all-gather.61.cloned.1.call-done = bf16[1,1576,384]{2,0,1:T(2,128)(2,1)} async-done(((bf16[1,394,384]{2,0,1:T(2,128)(2,1)}), bf16[1,1576,384]{2,0,1:T(2,128)(2,1)}) %all-gather.61.cloned.1.call-update) | async-done | bytes 1210384 | tf_op jit(solution)/shard_map/all_gather | solution.py:45
  125.2 17.4 all-reduce.122.cloned.1.call-done
  146.1 18.9 all-reduce.66
  190.5 248.3 %fusion.345 = (f32[400,1152]{1,0:T(8,128)}, f32[400,1152]{1,0:T(8,128)}) fusion(f32[1576,1152]{1,0:T(8,128)} %fusion.197, f32[1576,1152]{1,0:T(8,128)} %fusion.199), kind=kCustom, calls=%all-reduce-scatter.26 | all-reduce-scatter fusion | flops 3686401 | bytes 18211328
  520.4 26.8 all-gather.65.cloned.1.call-done
  554.3 19.8 all-reduce.120.cloned.1.call-done
  577.2 18.9 all-reduce.65
  624.0 328.2 %fusion.344 = (f32[400,1536]{1,0:T(8,128)}, f32[400,1536]{1,0:T(8,128)}) fusion(f32[1576,1536]{1,0:T(8,128)} %fusion.177, f32[1576,1536]{1,0:T(8,128)} %fusion.179), kind=kCustom, calls=%all-reduce-scatter.25 | all-reduce-scatter fusion | flops 4915201 | bytes 24281600
  978.9 13.6 fusion.84
  993.5 90.0 %all-gather.75.cloned.1.call-done = bf16[4,394,1536]{2,1,0:T(8,128)(2,1)} async-done(((bf16[1,394,1536]{2,1,0:T(8,128)(2,1)}), bf16[4,394,1536]{2,1,0:T(8,128)(2,1)}) %all-gather.75.cloned.1.call-update) | async-done | bytes 4841488 | tf_op jit(solution)/shard_map/all_gather | solution.py:45
  1095.2 81.5 %all-gather.67.cloned.1.call-done = bf16[4,394,1536]{2,1,0:T(8,128)(2,1)} async-done(((bf16[1,394,1536]{2,1,0:T(8,128)(2,1)}), bf16[4,394,1536]{2,1,0:T(8,128)(2,1)}) %all-gather.67.cloned.1.call-update) | async-done | bytes 4841488 | tf_op jit(solution)/shard_map/all_gather | solution.py:45
  1189.4 19.3 all-reduce.118.cloned.1.call-done
  1211.8 18.9 all-reduce.64
  1257.4 248.0 %fusion.343 = (f32[400,1152]{1,0:T(8,128)}, f32[400,1152]{1,0:T(8,128)}) fusion(f32[1576,1152]{1,0:T(8,128)} %fusion.189, f32[1576,1152]{1,0:T(8,128)} %fusion.191), kind=kCustom, calls=%all-reduce-scatter.24 | all-reduce-scatter fusion | flops 3686401 | bytes 18211328
  1586.2 27.0 all-gather.69.cloned.1.call-done
  1620.6 19.8 all-reduce.116.cloned.1.call-done
  1643.4 18.9 all-reduce.63
  1690.9 328.3 %fusion.342 = (f32[400,1536]{1,0:T(8,128)}, f32[400,1536]{1,0:T(8,128)}) fusion(f32[1576,1536]{1,0:T(8,128)} %fusion.161, f32[1576,1536]{1,0:T(8,128)} %fusion.163), kind=kCustom, calls=%all-reduce-scatter.23 | all-reduce-scatter fusion | flops 4915201 | bytes 24281600
  2046.3 13.7 fusion.85
  2060.6 90.3 %all-gather.79.cloned.1.call-done = bf16[4,394,1536]{2,1,0:T(8,128)(2,1)} async-done(((bf16[1,394,1536]{2,1,0:T(8,128)(2,1)}), bf16[4,394,1536]{2,1,0:T(8,128)(2,1)}) %all-gather.79.cloned.1.call-update) | async-done | bytes 4841488 | tf_op jit(solution)/shard_map/all_gather | solution.py:45
  2162.8 80.7 %all-gather.71.cloned.1.call-done = bf16[4,394,1536]{2,1,0:T(8,128)(2,1)} async-done(((bf16[1,394,1536]{2,1,0:T(8,128)(2,1)}), bf16[4,394,1536]{2,1,0:T(8,128)(2,1)}) %all-gather.71.cloned.1.call-update) | async-done | bytes 4841488 | tf_op jit(solution)/shard_map/all_gather | solution.py:45
  2278.8 18.9 all-reduce.62
  2320.0 87.5 %fusion.341 = (f32[400,384]{1,0:T(8,128)}, f32[400,384]{1,0:T(8,128)}) fusion(f32[1576,384]{1,0:T(8,128)} %fusion.231, f32[1576,384]{1,0:T(8,128)} %fusion.233), kind=kCustom, calls=%all-reduce-scatter.22 | all-reduce-scatter fusion | flops 1228801 | bytes 6070784
  2426.1 29.0 all-gather.81.cloned.1.call-done
  2460.6 26.8 all-gather.91.cloned.1.call-done
  2493.1 21.3 all-reduce.112.cloned.1.call-done
  2517.7 18.9 all-reduce.61
  2568.1 328.2 %fusion.340 = (f32[400,1536]{1,0:T(8,128)}, f32[400,1536]{1,0:T(8,128)}) fusion(f32[1576,1536]{1,0:T(8,128)} %fusion.151, f32[1576,1536]{1,0:T(8,128)} %fusion.149), kind=kCustom, calls=%all-reduce-scatter.21 | all-reduce-scatter fusion | flops 4915201 | bytes 24281600
  2931.6 90.3 %all-gather.83.cloned.1.call-done = bf16[4,394,1536]{2,1,0:T(8,128)(2,1)} async-done(((bf16[1,394,1536]{2,1,0:T(8,128)(2,1)}), bf16[4,394,1536]{2,1,0:T(8,128)(2,1)}) %all-gather.83.cloned.1.call-update) | async-done | bytes 4841488 | tf_op jit(solution)/shard_map/all_gather | solution.py:45
  3033.8 80.6 %all-gather.93.cloned.1.call-done = bf16[4,394,1536]{2,1,0:T(8,128)(2,1)} async-done(((bf16[1,394,1536]{2,1,0:T(8,128)(2,1)}), bf16[4,394,1536]{2,1,0:T(8,128)(2,1)}) %all-gather.93.cloned.1.call-update) | async-done | bytes 4841488 | tf_op jit(solution)/shard_map/all_gather | solution.py:45
  3125.7 20.6 all-reduce.110.cloned.1.call-done
  3149.6 19.3 all-reduce.60
  3193.8 87.5 %fusion.339 = (f32[400,384]{1,0:T(8,128)}, f32[400,384]{1,0:T(8,128)}) fusion(f32[1576,384]{1,0:T(8,128)} %fusion.237, f32[1576,384]{1,0:T(8,128)} %fusion.235), kind=kCustom, calls=%all-reduce-scatter.20 | all-reduce-scatter fusion | flops 1228801 | bytes 6070784
  3342.2 41.1 all-gather.85.cloned.1.call-done
  3392.8 63.2 %all-gather.95.cloned.1.call-done = bf16[4,394,1152]{2,1,0:T(8,128)(2,1)} async-done(((bf16[1,394,1152]{2,1,0:T(8,128)(2,1)}), bf16[4,394,1152]{2,1,0:T(8,128)(2,1)}) %all-gather.95.cloned.1.call-update) | async-done | bytes 3631120 | tf_op jit(solution)/shard_map/all_gather | solution.py:45
  3465.5 20.8 all-reduce.108.cloned.1.call-done
  3489.4 18.9 all-reduce.59
  3539.6 328.2 %fusion.338 = (f32[400,1536]{1,0:T(8,128)}, f32[400,1536]{1,0:T(8,128)}) fusion(f32[1576,1536]{1,0:T(8,128)} %fusion.167, f32[1576,1536]{1,0:T(8,128)} %fusion.165), kind=kCustom, calls=%all-reduce-scatter.19 | all-reduce-scatter fusion | flops 4915201 | bytes 24281600
  3900.1 91.6 %all-gather.87.cloned.1.call-done = bf16[4,394,1536]{2,1,0:T(8,128)(2,1)} async-done(((bf16[1,394,1536]{2,1,0:T(8,128)(2,1)}), bf16[4,394,1536]{2,1,0:T(8,128)(2,1)}) %all-gather.87.cloned.1.call-update) | async-done | bytes 4841488 | tf_op jit(solution)/shard_map/all_gather | solution.py:45
  4003.4 81.5 %all-gather.97.cloned.1.call-done = bf16[4,394,1536]{2,1,0:T(8,128)(2,1)} async-done(((bf16[1,394,1536]{2,1,0:T(8,128)(2,1)}), bf16[4,394,1536]{2,1,0:T(8,128)(2,1)}) %all-gather.97.cloned.1.call-update) | async-done | bytes 4841488 | tf_op jit(solution)/shard_map/all_gather | solution.py:45
  4121.2 17.5 all-reduce.58
  4160.9 87.7 %fusion.337 = (f32[400,384]{1,0:T(8,128)}, f32[400,384]{1,0:T(8,128)}) fusion(f32[1576,384]{1,0:T(8,128)} %fusion.245, f32[1576,384]{1,0:T(8,128)} %fusion.243), kind=kCustom, calls=%all-reduce-scatter.18 | all-reduce-scatter fusion | flops 1228801 | bytes 6070784
  4409.4 15.1 all-gather.99.cloned.1.call-done
  4458.0 18.9 all-reduce.57
  4641.7 22.0 all-reduce.102.cloned.1.call-done
  4733.8 64.2 %all-reduce.100.cloned.1.call-done = f32[227,768]{0,1:T(8,128)} async-done(((f32[227,768]{0,1:T(8,128)}), f32[227,768]{0,1:T(8,128)}) %all-reduce.100.cloned.1.call-update) | async-done | bytes 697360 | tf_op jit(solution)/shard_map/psum | solution.py:420
  4799.9 39.3 all-reduce.56
  (1074 shorter events, 1299.5 us)
Async XLA Ops:
  7.2 58.4 %all-gather.63.cloned.1.call-start = ((), (), s32[]{:S(2)}) async-start(), calls=%async_computation.2 | async-start | bytes 3025920 | tf_op jit(solution)/shard_map/all_gather | solution.py:45
  11.3 106.8 %all-gather.61.cloned.1.call-start = ((), (), s32[]{:S(2)}) async-start(), calls=%async_computation.1 | async-start | bytes 3025920 | tf_op jit(solution)/shard_map/all_gather | solution.py:45
  12.0 130.5 %all-reduce.122.cloned.1.call-start = ((), (), s32[]{:S(2)}) async-start(), calls=%async_computation.31 | async-start | bytes 5111808
  121.5 393.3 %all-gather.73.cloned.1.call-start = ((), (), s32[]{:S(2)}) async-start(), calls=%async_computation.7 | async-start | bytes 1536000 | tf_op jit(solution)/shard_map/all_gather | solution.py:45
  439.7 6.3 collective-permute-start
  441.9 10.9 collective-permute-start.5
  485.2 62.0 %all-gather.65.cloned.1.call-start = ((), (), s32[]{:S(2)}) async-start(), calls=%async_computation.3 | async-start | bytes 1536000 | tf_op jit(solution)/shard_map/all_gather | solution.py:45
  506.5 67.7 %all-reduce.120.cloned.1.call-start = ((), (), s32[]{:S(2)}) async-start(), calls=%async_computation.30 | async-start | bytes 5111808
  552.8 530.7 %all-gather.75.cloned.1.call-start = ((), (), s32[]{:S(2)}) async-start(), calls=%async_computation.8 | async-start | bytes 6144000 | tf_op jit(solution)/shard_map/all_gather | solution.py:45
  953.7 7.0 collective-permute-start.1
  957.3 13.0 collective-permute-start.6
  992.5 184.2 %all-gather.67.cloned.1.call-start = ((), (), s32[]{:S(2)}) async-start(), calls=%async_computation.4 | async-start | bytes 6144000 | tf_op jit(solution)/shard_map/all_gather | solution.py:45
  993.3 215.4 %all-reduce.118.cloned.1.call-start = ((), (), s32[]{:S(2)}) async-start(), calls=%async_computation.29 | async-start | bytes 5111808
  1188.0 392.7 %all-gather.77.cloned.1.call-start = ((), (), s32[]{:S(2)}) async-start(), calls=%async_computation.9 | async-start | bytes 1536000 | tf_op jit(solution)/shard_map/all_gather | solution.py:45
  1506.3 5.0 collective-permute-start.2
  1508.5 9.6 collective-permute-start.7
  1550.4 62.9 %all-gather.69.cloned.1.call-start = ((), (), s32[]{:S(2)}) async-start(), calls=%async_computation.5 | async-start | bytes 1536000 | tf_op jit(solution)/shard_map/all_gather | solution.py:45
  1571.0 69.4 %all-reduce.116.cloned.1.call-start = ((), (), s32[]{:S(2)}) async-start(), calls=%async_computation.28 | async-start | bytes 5111808
  1619.0 531.9 %all-gather.79.cloned.1.call-start = ((), (), s32[]{:S(2)}) async-start(), calls=%async_computation.10 | async-start | bytes 6144000 | tf_op jit(solution)/shard_map/all_gather | solution.py:45
  2020.8 6.5 collective-permute-start.3
  2024.3 12.5 collective-permute-start.8
  2060.0 183.5 %all-gather.71.cloned.1.call-start = ((), (), s32[]{:S(2)}) async-start(), calls=%async_computation.6 | async-start | bytes 6144000 | tf_op jit(solution)/shard_map/all_gather | solution.py:45
  2060.5 214.9 %all-reduce.114.cloned.1.call-start = ((), (), s32[]{:S(2)}) async-start(), calls=%async_computation.27 | async-start | bytes 5111808
  2254.8 200.2 %all-gather.81.cloned.1.call-start = ((), (), s32[]{:S(2)}) async-start(), calls=%async_computation.11 | async-start | bytes 1536000 | tf_op jit(solution)/shard_map/all_gather | solution.py:45
  2408.3 6.6 collective-permute-start.9
  2410.4 8.0 collective-permute-start.4
  2425.4 62.1 %all-gather.91.cloned.1.call-start = ((), (), s32[]{:S(2)}) async-start(), calls=%async_computation.16 | async-start | bytes 1536000 | tf_op jit(solution)/shard_map/all_gather | solution.py:45
  2426.0 88.4 %all-reduce.112.cloned.1.call-start = ((), (), s32[]{:S(2)}) async-start(), calls=%async_computation.26 | async-start | bytes 5111808
  2493.1 528.8 %all-gather.83.cloned.1.call-start = ((), (), s32[]{:S(2)}) async-start(), calls=%async_computation.12 | async-start | bytes 6144000 | tf_op jit(solution)/shard_map/all_gather | solution.py:45
  2897.2 6.2 collective-permute-start.14
  2900.7 12.2 collective-permute-start.10
  2931.0 183.5 %all-gather.93.cloned.1.call-start = ((), (), s32[]{:S(2)}) async-start(), calls=%async_computation.17 | async-start | bytes 6144000 | tf_op jit(solution)/shard_map/all_gather | solution.py:45
  2931.5 214.8 %all-reduce.110.cloned.1.call-start = ((), (), s32[]{:S(2)}) async-start(), calls=%async_computation.25 | async-start | bytes 5111808
  3125.7 257.7 %all-gather.85.cloned.1.call-start = ((), (), s32[]{:S(2)}) async-start(), calls=%async_computation.13 | async-start | bytes 4608000 | tf_op jit(solution)/shard_map/all_gather | solution.py:45
  3310.7 145.4 %all-gather.95.cloned.1.call-start = ((), (), s32[]{:S(2)}) async-start(), calls=%async_computation.18 | async-start | bytes 4608000 | tf_op jit(solution)/shard_map/all_gather | solution.py:45
  3311.5 5.6 collective-permute-start.15
  3342.2 144.1 %all-reduce.108.cloned.1.call-start = ((), (), s32[]{:S(2)}) async-start(), calls=%async_computation.24 | async-start | bytes 5111808
  3465.4 526.3 %all-gather.87.cloned.1.call-start = ((), (), s32[]{:S(2)}) async-start(), calls=%async_computation.14 | async-start | bytes 6144000 | tf_op jit(solution)/shard_map/all_gather | solution.py:45
  3868.7 4.9 collective-permute-start.16
  3870.9 11.4 collective-permute-start.12
  3899.3 185.6 %all-gather.97.cloned.1.call-start = ((), (), s32[]{:S(2)}) async-start(), calls=%async_computation.19 | async-start | bytes 6144000 | tf_op jit(solution)/shard_map/all_gather | solution.py:45
  3899.9 218.2 %all-reduce.106.cloned.1.call-start = ((), (), s32[]{:S(2)}) async-start(), calls=%async_computation.23 | async-start | bytes 5111808
  4096.0 303.8 %all-gather.89.cloned.1.call-start = ((), (), s32[]{:S(2)}) async-start(), calls=%async_computation.15 | async-start | bytes 4608000 | tf_op jit(solution)/shard_map/all_gather | solution.py:45
  4272.9 151.5 %all-gather.99.cloned.1.call-start = ((), (), s32[]{:S(2)}) async-start(), calls=%async_computation.20 | async-start | bytes 4608000 | tf_op jit(solution)/shard_map/all_gather | solution.py:45
  4317.8 10.9 collective-permute-start.17
  4353.6 101.1 %all-reduce.104.cloned.1.call-start = ((), (), s32[]{:S(2)}) async-start(), calls=%async_computation.22 | async-start | bytes 5111808
  4433.8 229.8 %all-reduce.102.cloned.1.call-start = ((), (), s32[]{:S(2)}) async-start(), calls=%async_computation.21 | async-start | bytes 15335424 | tf_op jit(solution)/shard_map/psum | solution.py:410
  4502.8 295.3 %all-reduce.100.cloned.1.call-start = ((), (), s32[]{:S(2)}) async-start(), calls=%async_computation | async-start | bytes 1572864 | tf_op jit(solution)/shard_map/psum | solution.py:420
  (199 other events, 8294.0 us)
Sparse Core Ops, SparseCore 0:
  11.4 54.1 all-gather.62
  67.8 50.2 all-gather.60
  121.6 20.9 all-reduce.121
  485.3 29.4 all-gather.72
  516.8 30.3 all-gather.64
  552.9 21.1 all-reduce.119
  992.6 90.7 all-gather.74
  1085.6 91.0 all-gather.66
  1188.1 20.5 all-reduce.117
  1550.5 30.1 all-gather.76
  1582.9 30.3 all-gather.68
  1619.1 21.1 all-reduce.115
  2060.1 90.7 all-gather.78
  2152.4 91.0 all-gather.70
  2254.9 20.4 all-reduce.113
  2425.5 29.4 all-gather.80
  2457.1 30.3 all-gather.90
  2493.2 21.1 all-reduce.111
  2931.1 90.7 all-gather.82
  3023.3 91.0 all-gather.92
  3125.8 20.5 all-reduce.109
  3310.8 72.5 all-gather.84
  3385.0 70.9 all-gather.94
  3465.5 20.6 all-reduce.107
  3899.4 92.2 all-gather.86
  3993.8 91.0 all-gather.96
  4096.1 20.5 all-reduce.105
  4273.0 72.5 all-gather.88
  4353.6 70.7 all-gather.98
  4433.9 20.6 all-reduce.103
  4502.9 160.7 all-reduce.101
  4668.9 129.1 all-reduce.99
where the time goes:
time: 4920 us; the launch traced here: 4890 us
  blocking collectives  2360 us (48%)
  waiting for transfers between devices  1280 us (26%)
  local copies, waits for them, and re-layouts  677 us (14%)
  matrix products  312 us (6%)
  other arithmetic  203 us (4%)
    unnamed x9, blocking collectives  2070 us
    all_gather x20, waiting for transfers between devices, gather_cols(): return lax.all_gather(value, 'col', axis=0, tiled=True)  1040 us
    unnamed x506, local copies, waits for them, and re-layouts  367 us
    dot_general x58, matrix products, matmul(): lax.dot_general(lhs_mat, rhs_mat, (((lhs_dim,), (rhs_dim,)), ((), ())), p...  234 us
    psum x10, blocking collectives, col_totals(): return lax.psum((pair[0], pair[1]), 'col')  188 us
    unnamed x60, waiting for transfers between devices  154 us
  transfers between devices with their start and end apart: 50, of which 33 were waited for; matrix products, arithmetic and copies ran while one was open for 12% of the time, Pallas kernels for 0%

commit v1 on v0

v1 whole, which is shorter than its diff:
```python
import math

import jax
import jax.numpy as jnp
from jax import lax
from jax.experimental import pallas as pl
from jax.experimental.pallas import tpu as pltpu
from jax.sharding import PartitionSpec as P

HD = 64
PATCH = 768
L = 197
LP = 208
BLK = 96

norm_eps = 1e-06
beta_first = 0.9
beta_second = 0.999
adam_eps = 1e-08
decay_stat = 0.5
rate_matrix = 0.02
rate_vector = 0.2
rate_blocks = 0.1
weight_decay = 0.05
clip_scale = 0.25
highest = lax.Precision.HIGHEST
bf16 = jnp.bfloat16
f16 = jnp.float16
f32 = jnp.float32


COST = 16
VMEM = pl.BlockSpec(memory_space=pltpu.VMEM)
SMEM = pl.BlockSpec(memory_space=pltpu.SMEM)


def whole_call(body, outs, name, flops, scratch=()):
    return pl.pallas_call(
        body,
        out_shape=[jax.ShapeDtypeStruct(shape, dtype) for shape, dtype in outs],
        scratch_shapes=list(scratch),
        compiler_params=pltpu.CompilerParams(vmem_limit_bytes=52 * 2**20),
        cost_estimate=pl.CostEstimate(flops=flops // COST, bytes_accessed=2**16, transcendentals=0),
        name=name,
    )


def dot(lhs_mat, rhs_mat, lhs_dim, rhs_dim):
    return lax.dot_general(
        lhs_mat, rhs_mat, (((lhs_dim,), (rhs_dim,)), ((), ())), preferred_element_type=f32
    )


def exact(lhs_mat, rhs_mat, lhs_dim, rhs_dim):
    return lax.dot_general(
        lhs_mat,
        rhs_mat,
        (((lhs_dim,), (rhs_dim,)), ((), ())),
        precision=highest,
        preferred_element_type=f32,
    )


def swap(value, axis, mask):
    size = lax.axis_size(axis)
    return lax.ppermute(value, axis, [(i, i ^ mask) for i in range(size)])


def bits_of(axis):
    return [1 << b for b in range(lax.axis_size(axis).bit_length() - 1)]


def butterfly(value, axes, op=jnp.add):
    for axis in axes:
        for mask in bits_of(axis):
            value = op(value, swap(value, axis, mask))
    return value


def softmax_scores(queries, key_rows):
    scores = dot(queries, key_rows, 1, 1)
    spot = lax.broadcasted_iota(jnp.int32, scores.shape, 1)
    scores = jnp.where(spot < L, scores, -1e30)
    top = jnp.max(scores, axis=1, keepdims=True)
    exponent = jnp.exp(scores - top)
    return exponent / jnp.sum(exponent, axis=1, keepdims=True)


def attend_forward(qkv_ref, ctx_ref):
    rows, wide = qkv_ref.shape
    for image in range(rows // LP):
        span = slice(image * LP, (image + 1) * LP)
        for pair in range(wide // (6 * HD)):
            made = []
            for head in (2 * pair, 2 * pair + 1):
                base = head * 3 * HD
                queries = qkv_ref[span, base : base + HD]
                key_rows = qkv_ref[span, base + HD : base + 2 * HD]
                values = qkv_ref[span, base + 2 * HD : base + 3 * HD]
                attend = softmax_scores(queries, key_rows).astype(bf16)
                made.append(dot(attend, values, 1, 0).astype(bf16))
            ctx_ref[span, pair * 2 * HD : (pair + 1) * 2 * HD] = jnp.concatenate(made, axis=1)


def attend_backward(qkv_ref, grad_ref, out_ref):
    rows, wide = qkv_ref.shape
    for image in range(rows // LP):
        span = slice(image * LP, (image + 1) * LP)
        for pair in range(wide // (6 * HD)):
            made = []
            for head in (2 * pair, 2 * pair + 1):
                base = head * 3 * HD
                queries = qkv_ref[span, base : base + HD]
                key_rows = qkv_ref[span, base + HD : base + 2 * HD]
                values = qkv_ref[span, base + 2 * HD : base + 3 * HD]
                grad = grad_ref[span, head * HD : (head + 1) * HD].astype(bf16)
                attend = softmax_scores(queries, key_rows)
                grad_values = dot(attend.astype(bf16), grad, 0, 0)
                grad_attend = dot(grad, values, 1, 1)
                inner = jnp.sum(grad_attend * attend, axis=1, keepdims=True)
                grad_scores = (attend * (grad_attend - inner)).astype(bf16)
                made.append((dot(grad_scores, key_rows, 1, 0) * 0.125).astype(bf16))
                made.append(dot(grad_scores, queries, 0, 0).astype(bf16))
                made.append(grad_values.astype(bf16))
            out_ref[span, pair * 6 * HD : (pair + 1) * 6 * HD] = jnp.concatenate(made, axis=1)


def normed_of(residual):
    center = residual - jnp.mean(residual, axis=1, keepdims=True)
    inverse = lax.rsqrt(jnp.mean(center * center, axis=1, keepdims=True) + norm_eps)
    return center * inverse, inverse


def norm_backward(grad_normed, residual, gain):
    normed, inverse = normed_of(residual)
    scaled = grad_normed * gain
    mean_one = jnp.mean(scaled, axis=1, keepdims=True)
    mean_two = jnp.mean(scaled * normed, axis=1, keepdims=True)
    grad_in = inverse * (scaled - mean_one - normed * mean_two)
    gain_sum = jnp.sum(grad_normed * normed, axis=0, keepdims=True)
    return grad_in, gain_sum, jnp.sum(grad_normed, axis=0, keepdims=True)


def rows_sum(value):
    return jnp.sum(value.astype(f32), axis=0, keepdims=True)


def put_rows(ref, rows):
    ref[...] = jnp.zeros(ref.shape, f32)
    for i, row in enumerate(rows):
        ref[i : i + 1, :] = row


def own_first(row, core):
    half = row.shape[1] // 2
    return jnp.where(core == 1, jnp.concatenate([row[:, half:], row[:, :half]], axis=1), row)


def qkv_part(base, places, vec, vectors, residual, weights, low_one, qkv, context):
    normed, _ = normed_of(residual)
    low_one[...] = (normed * vec[base : base + 1, :] + vec[base + 1 : base + 2, :]).astype(bf16)
    query_bias = own_first(vectors[base + 2 : base + 3, :], places[1])
    value_bias = own_first(vectors[base + 3 : base + 4, :], places[1])
    for half in range(2):
        heads = qkv[half].shape[1] // (3 * HD)
        parts = []
        for head in range(heads):
            at = (half * heads + head) * HD
            parts += [query_bias[:, at : at + HD], jnp.zeros((1, HD), f32), value_bias[:, at : at + HD]]
        bias = jnp.concatenate(parts, axis=1)
        kind = (lax.broadcasted_iota(jnp.int32, bias.shape, 1) // HD) % 3
        factor = jnp.where(kind == 0, 0.125, 1.0)
        step = 6 * HD
        for at in range(0, heads * 3 * HD, step):
            span = slice(at, at + step)
            mixed = dot(low_one[...], weights[half][:, span], 1, 0)
            qkv[half][:, span] = ((mixed + bias[:, span]) * factor[:, span]).astype(bf16)
        attend_forward(qkv[half], context[half])


def embed_qkv_body(
    places, vec, vectors, pix_a, pix_b, flags, ends_a, ends_b, qkv_a, qkv_b,
    residual, low_one, out_a, out_b, ctx_a, ctx_b,
):
    embedded = dot(pix_a[...], ends_a[...], 1, 1) + dot(pix_b[...], ends_b[...], 1, 1)
    embedded = embedded + vec[L + 2 : L + 3, :]
    spots = vec[0:LP, :]
    spots = jnp.concatenate([spots] * (embedded.shape[0] // LP), axis=0)
    picked = jnp.where(flags[:, 1:2] > 0, vec[L + 1 : L + 2, :], embedded)
    picked = jnp.where(flags[:, 0:1] > 0, vec[L : L + 1, :], picked)
    residual[...] = jnp.where(flags[:, 2:3] > 0, picked + spots, 0.0)
    qkv_part(
        L + 6, places, vec, vectors, residual[...], (qkv_a, qkv_b), low_one, (out_a, out_b), (ctx_a, ctx_b)
    )


def up_body(
    base, places, vec, vectors, residual, ctx_a, ctx_b, out_a, out_b, up_a, up_b,
    mid, low_two, act_a, act_b, slope_a, slope_b,
):
    branch = dot(ctx_a[...], out_a[...], 1, 1) + dot(ctx_b[...], out_b[...], 1, 1)
    mid[...] = residual[...] + (branch + vec[base + 4 : base + 5, :])
    normed, _ = normed_of(mid[...])
    low_two[...] = (normed * vec[base + 5 : base + 6, :] + vec[base + 6 : base + 7, :]).astype(bf16)
    wide = vec.shape[1]
    for half, (weight, active, slope) in enumerate(((up_a, act_a, slope_a), (up_b, act_b, slope_b))):
        for k in range(weight.shape[1] // wide):
            row = base + 7 + (weight.shape[1] // wide) * jnp.bitwise_xor(places[1], half) + k
            span = slice(k * wide, (k + 1) * wide)
            pre = dot(low_two[...], weight[:, span], 1, 0) + vectors[pl.ds(row, 1), :]
            phi = 0.5 * (1.0 + lax.erf(pre * math.sqrt(0.5)))
            active[:, span] = (pre * phi).astype(bf16)
            slope[:, span] = phi + pre * (jnp.exp(-0.5 * pre * pre) * (1.0 / math.sqrt(2.0 * math.pi)))


def down_qkv_body(
    base, places, vec, vectors, mid, act_a, act_b, down_a, down_b, qkv_a, qkv_b,
    residual, low_one, out_a, out_b, ctx_a, ctx_b,
):
    branch = dot(act_a[...], down_a[...], 1, 1) + dot(act_b[...], down_b[...], 1, 1)
    residual[...] = mid[...] + (branch + vec[base - 1 : base, :])
    qkv_part(
        base, places, vec, vectors, residual[...], (qkv_a, qkv_b), low_one, (out_a, out_b), (ctx_a, ctx_b)
    )


def down_head_body(
    base, places, vec, vectors, scale, mid, act_a, act_b, down_a, down_b, ends_a, ends_b, pix_a, pix_b, flags,
    low_fin, pred_a, pred_b, grad_res, grad_low, wide, flat, loss,
):
    branch = dot(act_a[...], down_a[...], 1, 1) + dot(act_b[...], down_b[...], 1, 1)
    residual = mid[...] + (branch + vec[base + 11 : base + 12, :])
    normed, _ = normed_of(residual)
    low_fin[...] = (normed * vec[L + 3 : L + 4, :] + vec[L + 4 : L + 5, :]).astype(bf16)
    bias = own_first(vectors[L + 5 : L + 6, :], places[1])
    keep = flags[:, 3:4]
    total = jnp.zeros((1, 1), f32)
    sums = []
    for half, (ends, pix, pred) in enumerate(((ends_a, pix_a, pred_a), (ends_b, pix_b, pred_b))):
        span = ends.shape[1]
        error = dot(low_fin[...], ends[...], 1, 0) + bias[:, half * span : (half + 1) * span]
        error = error - pix[...].astype(f32)
        total = total + jnp.sum(jnp.sum(keep * error * error, axis=1, keepdims=True), axis=0, keepdims=True)
        pred[...] = (2.0 * scale[0] * keep * error).astype(bf16)
        sums.append(rows_sum(pred[...]))
    loss[...] = jnp.broadcast_to(total * scale[0], loss.shape)
    grad_fin = dot(pred_a[...], ends_a[...], 1, 1) + dot(pred_b[...], ends_b[...], 1, 1)
    grad, gain_sum, shift_sum = norm_backward(grad_fin, residual, vec[L + 3 : L + 4, :])
    grad_res[...] = grad
    grad_low[...] = grad.astype(bf16)
    put_rows(wide, [gain_sum, shift_sum])
    put_rows(flat, [jnp.concatenate(sums, axis=1)])


def back_mlp_body(
    base, vec, grad_res, grad_low, down_a, down_b, slope_a, slope_b, up_a, up_b, mid,
    grad_mid, mid_low, hid_a, hid_b, wide, flat,
):
    span = vec.shape[1]
    sums = []
    total = None
    for down, slope, up, hid in ((down_a, slope_a, up_a, hid_a), (down_b, slope_b, up_b, hid_b)):
        for at in range(0, down.shape[1], span):
            cols = slice(at, at + span)
            hid[:, cols] = (dot(grad_low[...], down[:, cols], 1, 0) * slope[:, cols]).astype(bf16)
            sums.append(rows_sum(hid[:, cols]))
        part = dot(hid[...], up[...], 1, 1)
        total = part if total is None else total + part
    grad, gain_sum, shift_sum = norm_backward(total, mid[...], vec[base + 5 : base + 6, :])
    grad = grad_res[...] + grad
    grad_mid[...] = grad
    mid_low[...] = grad.astype(bf16)
    put_rows(wide, [rows_sum(grad_low[...]), gain_sum, shift_sum])
    put_rows(flat, sums)


def back_attend_body(
    base, vec, grad_mid, mid_low, out_a, out_b, qkv_a, qkv_b, wqkv_a, wqkv_b, residual,
    grad_res, grad_low, mix_a, mix_b, wide, flat, ctx,
):
    total = None
    query_sums, value_sums = [], []
    for out, qkv, wqkv, mix in ((out_a, qkv_a, wqkv_a, mix_a), (out_b, qkv_b, wqkv_b, mix_b)):
        ctx[...] = dot(mid_low[...], out[...], 1, 0)
        attend_backward(qkv, ctx, mix)
        part = dot(mix[...], wqkv[...], 1, 1)
        total = part if total is None else total + part
        sums = rows_sum(mix[...])
        for head in range(mix.shape[1] // (3 * HD)):
            at = head * 3 * HD
            query_sums.append(sums[:, at : at + HD])
            value_sums.append(sums[:, at + 2 * HD : at + 3 * HD])
    grad, gain_sum, shift_sum = norm_backward(total, residual[...], vec[base : base + 1, :])
    grad = grad_mid[...] + grad
    grad_res[...] = grad
    grad_low[...] = grad.astype(bf16)
    put_rows(wide, [rows_sum(mid_low[...]), gain_sum, shift_sum])
    put_rows(flat, [jnp.concatenate(query_sums, axis=1), jnp.concatenate(value_sums, axis=1)])


def back_embed_body(grad_res, flags, grad_low, place, wide):
    grad = grad_res[...]
    low = jnp.where(flags[:, 4:5] > 0, grad, 0.0).astype(bf16)
    grad_low[...] = low
    total = grad[0:LP]
    for image in range(1, grad.shape[0] // LP):
        total = total + grad[image * LP : (image + 1) * LP]
    place[...] = total
    class_sum = rows_sum(jnp.where(flags[:, 0:1] > 0, grad, 0.0))
    mask_sum = rows_sum(jnp.where(flags[:, 1:2] > 0, grad, 0.0))
    put_rows(wide, [class_sum, mask_sum, rows_sum(low)])


def tie(*trees):
    leaves, shape = jax.tree.flatten(trees)
    return jax.tree.unflatten(shape, lax.optimization_barrier(leaves))


def prepare_body(plan, cuts, places, qkv, out, up, down, ends, *rest):
    outs, turned = rest[:-1], rest[-1]
    whole, owns, firsts = outs[0], outs[1::2], outs[2::2]
    sub_at = places[0]
    part = whole.shape[1]
    refs = {"qkv": qkv, "out": out, "up": up, "down": down, "ends": ends}
    for chunk in range(len(cuts) - 1):
        begin = plan[cuts[chunk]][2]
        for name, layer, start, width in plan[cuts[chunk] : cuts[chunk + 1]]:
            ref = refs[name]
            plain = name in ("qkv", "up")
            if not plain:
                turned[:, :width] = ref[layer].T.astype(f32)
            for k in range(4):
                rows = pl.ds(pl.multiple_of(jnp.bitwise_xor(sub_at, k) * part, 16), part)
                piece = ref[layer, rows, :] if plain else turned[rows, :width].astype(bf16)
                whole[k, :, start : start + width] = piece
                owns[chunk][k, :, start - begin : start - begin + width] = piece
                if k == 0:
                    firsts[chunk][:, start - begin : start - begin + width] = piece


def prepare_tiles(plan, cuts, places, qkv, out, up, down, ends):
    height = qkv.shape[1]
    part = height // 4
    outs = [((4, part, plan[-1][2] + plan[-1][3]), bf16)]
    for j, k in zip(cuts[:-1], cuts[1:]):
        width = plan[k - 1][2] + plan[k - 1][3] - plan[j][2]
        outs += [((4, part, width), bf16), ((part, width), bf16)]
    widest = max(entry[3] for entry in plan)
    got = whole_call_smem(
        lambda *refs: prepare_body(plan, cuts, *refs), 1, 5, outs, "prepare_tiles", 10**8,
        [pltpu.VMEM((height, widest), f32)],
    )(places, qkv, out, up, down, ends)
    return got[0], got[1::2], got[2::2]


def whole_call_smem(body, scalars, arrays, outs, name, flops, scratch=()):
    return pl.pallas_call(
        body,
        in_specs=[SMEM] * scalars + [VMEM] * arrays,
        out_specs=[VMEM] * len(outs),
        out_shape=[jax.ShapeDtypeStruct(shape, dtype) for shape, dtype in outs],
        scratch_shapes=list(scratch),
        compiler_params=pltpu.CompilerParams(vmem_limit_bytes=52 * 2**20),
        cost_estimate=pl.CostEstimate(flops=flops // COST, bytes_accessed=2**16, transcendentals=0),
        name=name,
    )


def assemble_body(widths, own, stack, from_x, from_y, left, right, *outs):
    part = own.shape[1]
    half = left.shape[1]
    start = 0
    for out, width in zip(outs, widths):
        stop = start + width
        for k in range(4):
            out[4 * k * part : (4 * k + 1) * part, :] = own[k, :, start:stop]
            rows = slice((4 * k + 1) * part, 4 * (k + 1) * part)
            if k < 3:
                out[rows, :] = (stack, from_x, from_y)[k][:, start:stop]
                continue
            middle = min(max(half, start), stop)
            if middle > start:
                out[rows, : middle - start] = left[:, start:middle]
            if stop > middle:
                out[rows, middle - start :] = right[:, middle - half : stop - half]
        start = stop


class Gather:
    def __init__(self, own, first, widths):
        self.own, self.first, self.widths = own, first, widths
        self.state = []

    def along(self):
        self.state = [jnp.concatenate([swap(self.first, "col", k) for k in (1, 2, 3)], axis=0)]

    def across(self):
        stack = self.state[0]
        self.state = [stack, swap(stack, "dp", 1), swap(stack, "dp", 2)]

    def diagonal(self):
        stack, from_x, from_y = self.state
        half = stack.shape[1] // 256 * 128
        left = swap(from_x[:, :half], "dp", 2)
        right = swap(from_y[:, half:], "dp", 1)
        self.state = [stack, from_x, from_y, left, right]

    def weights(self):
        height = 16 * self.own.shape[1]
        mine = whole_call(
            lambda *refs: assemble_body(self.widths, *refs),
            [((height, w), bf16) for w in self.widths],
            "assemble",
            10**8,
        )(self.own, *self.state)
        return [(w, swap(w, "row", 1)) for w in mine]


DIMS = ("y", "x", "c1", "c0")
WHERE = {"c1": ("col", 2), "c0": ("col", 1), "y": ("dp", 2), "x": ("dp", 1)}


def row_runs(name, part):
    block = part << (3 - DIMS.index(name))
    count = 16 * part // block
    return [(i * block, block) for i in range(0, count, 2)], [(i * block, block) for i in range(1, count, 2)]


def product_body(runs, left, left_got, right, right_got, keep, send, power, total):
    total[...] = dot(left[...], right[...], 0, 0) + dot(left_got[...], right_got[...], 0, 0)
    top = jnp.max(jnp.abs(total[...]), axis=0, keepdims=True)
    exponent = jnp.clip(jnp.ceil(jnp.log2(top)) + 1.0, -100.0, 120.0)
    scale = jnp.exp2(14.0 - exponent)
    power[...] = exponent
    for out, spans, factor in ((keep, runs[0], None), (send, runs[1], scale)):
        at = 0
        for start, size in spans:
            piece = total[start : start + size, :]
            out[at : at + size, :] = piece if factor is None else piece * factor
            at += size
    send[at:, :] = jnp.broadcast_to(exponent, (16, exponent.shape[1]))


def product_sum(name, left, left_got, right, right_got, block, blocks):
    rows, height = left.shape
    width = block * len(blocks)
    first = blocks[0]
    runs = row_runs(name, height // 16)
    whole = pl.BlockSpec((rows, height), lambda i: (0, 0))
    part = pl.BlockSpec((rows, block), lambda i: (0, i + first))
    half = pl.BlockSpec((height // 2, block), lambda i: (0, i))
    return pl.pallas_call(
        lambda *refs: product_body(runs, *refs),
        grid=(len(blocks),),
        in_specs=[whole, whole, part, part],
        out_specs=[
            half,
            pl.BlockSpec((height // 2 + 16, block), lambda i: (0, i)),
            pl.BlockSpec((1, block), lambda i: (0, i)),
        ],
        out_shape=[
            jax.ShapeDtypeStruct((height // 2, width), f32),
            jax.ShapeDtypeStruct((height // 2 + 16, width), f32),
            jax.ShapeDtypeStruct((1, width), f32),
        ],
        scratch_shapes=[pltpu.VMEM((height, block), f32)],
        compiler_params=pltpu.CompilerParams(vmem_limit_bytes=32 * 2**20),
        cost_estimate=pl.CostEstimate(
            flops=4 * rows * height * width // COST, bytes_accessed=2**16, transcendentals=0
        ),
        name="product_sum",
    )(left, left_got, right, right_got)


def lowered(rows, exponent):
    tail = jnp.broadcast_to(exponent, (16, exponent.shape[1]))
    return jnp.concatenate([rows * jnp.exp2(14.0 - exponent), tail], axis=0).astype(f16)


def tail_of(payload):
    return jnp.max(payload[-16:].astype(f32), axis=0, keepdims=True)


def decoded(rows, exponent):
    return rows.astype(f32) * jnp.exp2(exponent - 14.0)


def halves(rows, block):
    shaped = rows.reshape(-1, 2, block, rows.shape[1])
    return shaped[:, 0].reshape(-1, rows.shape[1]), shaped[:, 1].reshape(-1, rows.shape[1])


class Reduce:
    def __init__(self, first_x, first_y):
        self.parts = []
        for products in (first_x, first_y):
            keep, send, exponent = (jnp.concatenate(list(p), axis=1) for p in zip(*products))
            self.parts.append([keep, send.astype(f16), exponent])
        self.stage = 0

    def send(self):
        ways = ((("dp", 1), ("dp", 2)), (("dp", 2), ("dp", 1)), (("col", 1),), (("col", 2),))[self.stage]
        self.got = [swap(part[1], axis, mask) for part, (axis, mask) in zip(self.parts, ways)]

    def absorb(self):
        part = self.parts[0][0].shape[0] * 2 // (16 >> self.stage)
        if self.stage == 0:
            blocks = (8 * part // 2, 4 * part)
        elif self.stage == 1:
            blocks = (part, part)
        elif self.stage == 2:
            blocks = (part,)
        made = []
        for i, ((keep, _, exponent), got) in enumerate(zip(self.parts, self.got)):
            theirs = tail_of(got)
            after = jnp.maximum(exponent, theirs) + 1.0
            if self.stage == 3:
                made.append([keep + decoded(got[:-16], theirs), None, after])
                continue
            stay, leave = halves(keep, blocks[i])
            got_stay, got_leave = halves(got[:-16], blocks[i])
            stay = stay + decoded(got_stay, theirs)
            leave = leave + decoded(got_leave, theirs)
            made.append([stay, leave, after])
        if self.stage == 1:
            made = [[jnp.concatenate(list(p), axis=1) for p in zip(*made)]]
        self.stage += 1
        if self.stage < 4:
            self.parts = [[stay, lowered(leave, after), after] for stay, leave, after in made]
            return
        keep, _, after = made[0]
        for mask in bits_of("dp")[2:]:
            keep = keep + swap(keep, "dp", mask)
            after = after + 1.0
        self.parts = []
        self.keep, self.exponent = keep, after


def shampoo_body(
    group, layout, info, weight, *rest
):
    pieces, (rl, rr, grad_out, left, right, precond, weight_out), grads = rest[:-8], rest[-8:-1], rest[-1]
    step = pl.program_id(0)

    @pl.when(step == 0)
    def _():
        for ref, (sub, spans) in zip(pieces, layout):
            for source, target, size in spans:
                grads[sub, :, target : target + size] = ref[:, source : source + size]

    window = 2 * 128

    def block_of(ref, slot):
        start = pl.multiple_of(info[2, slot] * 128, 128)
        tops = [ref[info[k, slot], :, pl.ds(start, window)].astype(f32) for k in range(2)]
        both = jnp.concatenate(tops, axis=0)
        both = pltpu.roll(both, info[3, slot], 1)[:, :BLK]
        return jnp.where(info[4, slot] == 1, both.T, both)

    for j in range(group):
        slot = step * group + j
        g = block_of(grads, slot)
        grad_out[j] = g
        weight_out[j] = block_of(weight, slot)
        left[j] = exact(g, g, 1, 1)
        right[j] = exact(g, g, 0, 0)
        precond[j] = exact(rl[j], exact(g, rr[j], 1, 0), 1, 0)


def shampoo(info, weight, pieces, layout, root_left, root_right):
    count = root_left.shape[0]
    group = next(g for g in (8, 6, 4, 3, 2, 1) if count % g == 0)
    plain = pl.BlockSpec((group, BLK, BLK), lambda i: (i, 0, 0))
    return pl.pallas_call(
        lambda *refs: shampoo_body(group, layout, *refs),
        grid=(count // group,),
        in_specs=[SMEM] + [VMEM] * (1 + len(pieces)) + [plain] * 2,
        out_specs=[plain] * 5,
        out_shape=[jax.ShapeDtypeStruct((count, BLK, BLK), f32)] * 5,
        scratch_shapes=[pltpu.VMEM(weight.shape, f32)],
        compiler_params=pltpu.CompilerParams(vmem_limit_bytes=52 * 2**20),
        cost_estimate=pl.CostEstimate(
            flops=count * 48 * BLK**3 // COST, bytes_accessed=2**16, transcendentals=0
        ),
        name="shampoo",
    )(info, weight, *pieces, root_left, root_right)


def ends_body(places, *refs):
    out = refs[-1]
    part = refs[0].shape[0]
    for end in range(2):
        for k in range(4):
            sub = jnp.bitwise_xor(places[0], k)
            out[end, pl.ds(pl.multiple_of(sub * part, 8), part), :] = refs[4 * end + k][...]


def adam_update(weight, gradient, moment, second, rate, decay, factor, step_value):
    clipped = gradient * factor
    moment_new = beta_first * moment + (1.0 - beta_first) * clipped
    second_new = beta_second * second + (1.0 - beta_second) * clipped * clipped
    corr_first = 1.0 - jnp.power(beta_first, step_value)
    corr_second = 1.0 - jnp.power(beta_second, step_value)
    stride = moment_new / corr_first / (jnp.sqrt(second_new / corr_second) + adam_eps)
    return (weight - rate * (stride + decay * weight), moment_new, second_new)


def shards(
    pixels,
    patch_mask,
    class_ids,
    class_counts,
    step_count,
    weight_qkv,
    weight_out,
    weight_up,
    weight_down,
    weight_ends,
    vectors,
    vector_moment,
    vector_second,
    ends_moment,
    ends_second,
    stat_left,
    stat_right,
    root_left,
    root_right,
    owner_map,
):
    data_count = lax.axis_size("dp")
    row_index = lax.axis_index("row")
    col_index = lax.axis_index("col")
    data_index = lax.axis_index("dp")
    sub_index = data_index & 3
    layer_count = weight_qkv.shape[0]
    width = vectors.shape[1]
    images = pixels.shape[1] // L
    total_tokens = pixels.shape[0] * pixels.shape[1] * lax.axis_size("col") * data_count
    places = jnp.stack([sub_index, row_index]).astype(jnp.int32)
    swapped = row_index == 1

    names = [("ends", 0)]
    for i in range(layer_count):
        names += [("qkv", i), ("out", i), ("up", i), ("down", i)]
    names.append(("ends", 1))
    sizes = {
        "qkv": weight_qkv.shape[2],
        "out": weight_out.shape[1],
        "up": weight_up.shape[2],
        "down": weight_down.shape[1],
        "ends": weight_ends.shape[1],
    }
    plan, at = [], 0
    for name, i in names:
        plan.append((name, i, at, sizes[name]))
        at += sizes[name]
    start_of = {entry[:2]: entry[2] for entry in plan}
    cuts = [0]
    for i in range(layer_count):
        cuts += [2 + 4 * i, 4 + 4 * i]
    cuts.append(len(plan))
    tiles_own, owns, firsts = prepare_tiles(
        plan, cuts, places, weight_qkv, weight_out, weight_up, weight_down, weight_ends
    )
    chunks = [
        Gather(own, first, [entry[3] for entry in plan[j:k]])
        for own, first, j, k in zip(owns, firsts, cuts[:-1], cuts[1:])
    ]

    part = weight_qkv.shape[1] // 4
    column = jnp.arange(width)
    piece, inner = column // part, column % part
    source = ((piece & 3) ^ col_index) * (4 * part) + ((piece >> 2) ^ sub_index) * part + inner
    turn = (column[:, None] == source[None, :]).astype(f32)
    vec = exact(vectors, turn, 1, 0)

    def pad_rows(value):
        shaped = value.reshape(images, L, -1)
        return jnp.pad(shaped, ((0, 0), (0, LP - L), (0, 0))).reshape(images * LP, -1)

    pix_mine = lax.dynamic_index_in_dim(pixels, row_index, 0, keepdims=False)
    pix_give = lax.dynamic_index_in_dim(pixels, 1 - row_index, 0, keepdims=False)
    pix_got = swap(pix_give, "row", 1)
    pix_half = [pad_rows(pix_mine), pad_rows(pix_got)]
    pix_other = pad_rows(pix_give)

    live_group = (patch_mask > 0) & ((jnp.arange(patch_mask.shape[1]) % L) != 0)[None, :]
    count_all = butterfly(jnp.sum(live_group.astype(f32)), ("dp",))
    mask_mine = lax.dynamic_slice(
        patch_mask, (row_index, col_index * images * L), (1, images * L)
    ).reshape(images, L)
    ids_mine = lax.dynamic_slice(class_ids, (row_index, col_index * images), (1, images))[0]
    chosen = ids_mine[:, None] == jnp.arange(class_counts.shape[0])[None, :]
    image_weight = 32.0 / jnp.sum(jnp.where(chosen, class_counts[None, :], 0), axis=1).astype(f32)
    position = jnp.broadcast_to(jnp.arange(LP)[None, :], (images, LP))
    hidden = jnp.pad(mask_mine, ((0, 0), (0, LP - L))) > 0
    first_rows = position == 0
    real_rows = position < L
    live = hidden & (position != 0)
    keep_rows = jnp.where(live, image_weight[:, None], 0.0)
    patch_rows = real_rows & jnp.logical_not(first_rows) & jnp.logical_not(live)
    columns = [first_rows, live, real_rows, keep_rows, patch_rows]
    flags = jnp.stack([c.astype(f32).reshape(-1) for c in columns] + [jnp.zeros((images * LP,), f32)] * 3, axis=1)
    tokens = images * LP

    def activations(*widths):
        return [((tokens, w), bf16) for w in widths]

    weights, values = {}, {}
    qkv_outs = [((tokens, width), f32)] + activations(width, *[sizes["qkv"]] * 2, *[sizes["out"]] * 2)
    full = 2 * tokens * width
    loss_scale = 1.0 / (PATCH * count_all)

    def across_core(value):
        return swap(value, "row", 1)

    def keep_qkv(i, got):
        values["residual", i], values["low_one", i] = got[0], got[1]
        values["qkv", i], values["context", i] = got[2:4], got[4:6]
        values["got_one", i], values["got_context", i] = across_core(got[1]), across_core(got[5])

    def forward_stage(index, pairs):
        layer, odd = divmod(index, 2)
        for entry, pair in zip(plan[cuts[index] : cuts[index + 1]], pairs):
            weights[entry[:2]] = pair
        base = L + 6 + 12 * layer
        if index == 0:
            got = whole_call_smem(
                embed_qkv_body, 1, 9, qkv_outs, "embed_qkv", full * (width + 3 * width)
            )(places, vec, vectors, *pix_half, flags, *weights["ends", 0], *weights["qkv", 0])
            keep_qkv(0, got)
        elif odd:
            outs = [((tokens, width), f32)] + activations(width, *[sizes["up"]] * 2)
            outs += [((tokens, sizes["up"]), f32)] * 2
            got = whole_call_smem(
                lambda *refs: up_body(base, *refs), 1, 9, outs, "out_up", full * 5 * width
            )(
                places, vec, vectors, values["residual", layer], *values["context", layer],
                *weights["out", layer], *weights["up", layer],
            )
            values["mid", layer], values["low_two", layer] = got[0], got[1]
            values["active", layer], values["slope", layer] = got[2:4], got[4:6]
            values["got_two", layer], values["got_active", layer] = across_core(got[1]), across_core(got[3])
        elif layer < layer_count:
            got = whole_call_smem(
                lambda *refs: down_qkv_body(base, *refs), 1, 9, qkv_outs, "down_qkv", full * 7 * width
            )(
                places, vec, vectors, values["mid", layer - 1], *values["active", layer - 1],
                *weights["down", layer - 1], *weights["qkv", layer],
            )
            keep_qkv(layer, got)
        else:
            outs = activations(width, *[sizes["ends"]] * 2) + [((tokens, width), f32)] + activations(width)
            outs += [((8, width), f32), ((8, width), f32), ((8, 128), f32)]
            got = whole_call_smem(
                lambda *refs: down_head_body(base - 12, refs[0], refs[2], refs[3], refs[1], *refs[4:]),
                2, 12, outs, "down_head", full * 6 * width,
            )(
                places, loss_scale.reshape(1), vec, vectors, values["mid", layer - 1],
                *values["active", layer - 1], *weights["down", layer - 1], *weights["ends", 1],
                *pix_half, flags,
            )
            values["low_fin"], values["pred"] = got[0], got[1:3]
            values["grad_res"], values["grad_low"] = got[3], got[4]
            values["wide", "head"], values["flat", "head"], values["loss"] = got[5:]
            values["got_fin"], values["got_pred"] = across_core(got[0]), across_core(got[2])
            values["got_low"] = across_core(got[4])

    count = len(chunks)
    for step in range(count + 3):
        begun = list(values)
        if step < count:
            chunks[step].along()
        if 0 <= step - 1 < count:
            chunks[step - 1].across()
        if 0 <= step - 2 < count:
            chunks[step - 2].diagonal()
        if 0 <= step - 3 < count:
            forward_stage(step - 3, chunks[step - 3].weights())
        if step == count + 2:
            break
        moving = chunks[max(0, step - 2) : step + 1]
        later = chunks[step + 1 :]
        keys = [k for k in values if k in begun or not (isinstance(k, tuple) and k[0][:3] == "got")]
        states, waiting, kept = tie(
            [c.state for c in moving], [c.first for c in later], [values[k] for k in keys]
        )
        values.update(zip(keys, kept))
        for c, s in zip(moving, states):
            c.state = s
        for c, w in zip(later, waiting):
            c.first = w

    flying, done = [], []

    def step_on(value, fresh):
        value, landed, ready = tie(value, [r.got for r in flying], [r.parts for r in fresh])
        for r, got in zip(flying, landed):
            r.got = got
            r.absorb()
        for r, parts in zip(fresh, ready):
            r.parts = parts
        done.extend(r for r in flying if r.stage == 4)
        flying[:] = [r for r in flying if r.stage < 4] + list(fresh)
        for r in flying:
            r.send()
        return value

    wides = {"head": values["wide", "head"]}
    flats = {"head": values["flat", "head"]}
    grad_res, grad_low, got_low = values["grad_res"], values["grad_low"], values["got_low"]
    small = sizes["out"]
    blocks_of = {name: range(sizes[name] // small) for name in sizes}
    big = 2 * small
    groups = []

    def product(way, left, left_got, right, right_got, name, part=None):
        blocks = list(part if part is not None else blocks_of[name])
        block = small
        if len(blocks) % 2 == 0 and blocks[0] % 2 == 0:
            block, blocks = big, list(range(blocks[0] // 2, blocks[0] // 2 + len(blocks) // 2))
        return product_sum(way, left, left_got, right, right_got, block, blocks)

    for i in reversed(range(layer_count)):
        base = L + 6 + 12 * i
        outs = [((tokens, width), f32)] + activations(width, *[sizes["up"]] * 2) + [((8, width), f32)] * 2
        grad_mid, mid_low, hid_a, hid_b, wides["mlp", i], flats["mlp", i] = whole_call(
            lambda *refs: back_mlp_body(base, *refs), outs, "back_mlp", full * 8 * width
        )(
            vec, grad_res, grad_low, *weights["down", i], *values["slope", i], *weights["up", i],
            values["mid", i],
        )
        got_mid, got_hid = across_core(mid_low), across_core(hid_b)
        active = values["active", i]
        first_x = [product("x", grad_low, got_low, active[0], values["got_active", i], "down")]
        names_x = [("down", i)]
        if i == layer_count - 1:
            first_x.append(
                product("x", values["low_fin"], values["got_fin"], values["pred"][0], values["got_pred"], "ends")
            )
            names_x.append(("ends", 1))
        first_y = [product("y", values["low_two", i], values["got_two", i], hid_a, got_hid, "up")]
        group = Reduce(first_x, first_y)
        groups.append((group, names_x + [("up", i)]))
        grad_mid, mid_low, got_mid = step_on((grad_mid, mid_low, got_mid), [group])
        outs = [((tokens, width), f32)] + activations(width, *[sizes["qkv"]] * 2) + [((8, width), f32)] * 2
        grad_res, grad_low, mix_a, mix_b, wides["mix", i], flats["mix", i] = whole_call(
            lambda *refs: back_attend_body(base, *refs), outs, "back_attend", full * 8 * width,
            [pltpu.VMEM((tokens, sizes["out"]), f32)],
        )(
            vec, grad_mid, mid_low, *weights["out", i], *values["qkv", i], *weights["qkv", i],
            values["residual", i],
        )
        got_mix = across_core(mix_b)
        if i > 0:
            got_low = across_core(grad_low)
        else:
            outs = activations(width) + [((LP, width), f32), ((8, width), f32)]
            embed_low, place_sum, wides["embed"] = whole_call(back_embed_body, outs, "back_embed", full)(
                grad_res, flags
            )
            got_embed = across_core(embed_low)
        low_one, got_one = values["low_one", i], values["got_one", i]
        out_args = (mid_low, got_mid, values["context", i][0], values["got_context", i], "out")
        if i > 0:
            first_x = [product("x", low_one, got_one, mix_a, got_mix, "qkv", range(0, 2))]
            first_y = [product("y", low_one, got_one, mix_a, got_mix, "qkv", range(2, 3)), product("y", *out_args)]
            group_names = [("qkv", i), ("out", i)]
        else:
            first_x = [product("x", low_one, got_one, mix_a, got_mix, "qkv")]
            first_y = [
                product("y", *out_args),
                product("y", embed_low, got_embed, pix_half[0], pix_other, "ends"),
            ]
            group_names = [("qkv", i), ("out", i), ("ends", 0)]
        group = Reduce(first_x, first_y)
        groups.append((group, group_names))
        grad_res, grad_low, got_low = step_on((grad_res, grad_low, got_low), [group])

    raw_wide = [place_sum, wides["embed"], wides["head"]]
    raw_flat = [flats["head"]]
    source_wide = list(range(L)) + [LP, LP + 1, LP + 2, LP + 8, LP + 9, -1]
    source_flat = [-1] * (L + 5) + [0]
    rolled = [1] * 8
    for i in range(layer_count):
        at, low = LP + 16 * (i + 1), 8 + 16 * i
        raw_wide += [wides["mlp", i], wides["mix", i]]
        raw_flat += [flats["mlp", i], flats["mix", i]]
        source_wide += [at + 9, at + 10, -1, -1, at + 8, at + 1, at + 2, -1, -1, -1, -1, at]
        source_flat += [-1, -1, low + 8, low + 9, -1, -1, -1, low, low + 1, low + 2, low + 3, -1]
        rolled += [0] * 8 + [1] * 8
    rows_all = -(-vectors.shape[0] // 256) * 256
    spare = [-1] * (rows_all - vectors.shape[0])
    source_wide, source_flat = jnp.array(source_wide + spare), jnp.array(source_flat + spare)
    raw_wide = jnp.concatenate(raw_wide, axis=0)
    raw_flat = jnp.concatenate(raw_flat, axis=0)
    other = jnp.concatenate([raw_flat[:, width // 2 :], raw_flat[:, : width // 2]], axis=1)
    raw_flat = jnp.where(swapped & (jnp.array(rolled)[:, None] == 1), other, raw_flat)
    is_up = (source_flat >= 0) & (source_flat % 16 >= 8) & (source_flat % 16 < 12)
    turned_row = source_flat // 4 * 4 + (source_flat % 4 + 2 * row_index) % 4
    source_flat = jnp.where(is_up, turned_row, source_flat)
    pick_wide = (source_wide[:, None] == jnp.arange(raw_wide.shape[0])[None, :]).astype(f32)
    pick_flat = (source_flat[:, None] == jnp.arange(raw_flat.shape[0])[None, :]).astype(f32)
    grad_vec = exact(exact(pick_wide, raw_wide, 1, 0), turn, 1, 1) + exact(pick_flat, raw_flat, 1, 0)

    def rows_at(value, index, size):
        return lax.dynamic_slice_in_dim(value, index * size, size)

    half_rows, sub_rows, end_rows = rows_all // 2, rows_all // 8, rows_all // 32
    value = rows_at(grad_vec, row_index, half_rows) + across_core(rows_at(grad_vec, 1 - row_index, half_rows))
    value = rows_at(value, sub_index, sub_rows) + sum(
        swap(rows_at(value, sub_index ^ k, sub_rows), "dp", k) for k in (1, 2, 3)
    )
    value = rows_at(value, col_index, end_rows) + sum(
        swap(rows_at(value, col_index ^ k, end_rows), "col", k) for k in (1, 2, 3)
    )
    for mask in bits_of("dp")[2:]:
        value = value + swap(value, "dp", mask)
    vec_square = jnp.sum(value * value)
    value = jnp.concatenate([value] + [swap(value, "col", k) for k in (1, 2, 3)], axis=0)
    value = jnp.concatenate([value] + [swap(value, "dp", k) for k in (1, 2, 3)], axis=0)
    value = jnp.concatenate([value, across_core(value)], axis=0)
    spot = jnp.arange(rows_all)
    native = (
        ((spot // half_rows) ^ row_index) * half_rows
        + (((spot // sub_rows) & 3) ^ sub_index) * sub_rows
        + (((spot // end_rows) & 3) ^ col_index) * end_rows
        + spot % end_rows
    )
    pick = (jnp.arange(vectors.shape[0])[:, None] == native[None, :]).astype(f32)
    vec_sum = exact(pick, value, 1, 0)

    def spread(members):
        value = jnp.concatenate([g.keep for g in members], axis=1)
        exponent = jnp.concatenate([g.exponent for g in members], axis=1)
        payload = lowered(value, exponent)
        return [payload] + [swap(payload, "dp", k) for k in (1, 2, 3)]

    spreads = []
    ready = 0

    def spread_ready(size):
        nonlocal ready
        spreads.append((spread([g for g, _ in groups[ready : ready + size]]), groups[ready : ready + size]))
        ready += size

    marker = grad_res
    while flying:
        marker = step_on(marker, [])
        finished = sum(1 for g, _ in groups if g.stage == 4)
        if ready == 0 and finished >= 2:
            spread_ready(2)
    spread_ready(len(groups) - ready)
    axes = ("row", "dp", "col")
    copies = max(1, data_count // 4)
    square = sum(jnp.sum(g.keep * g.keep) for g, _ in groups) + vec_square
    pair = butterfly(jnp.stack([square / copies, values["loss"][0, 0]]), axes)
    loss_total = pair[1]
    grad_norm = jnp.sqrt(pair[0])
    factor = jnp.minimum(1.0, clip_scale / math.sqrt(total_tokens) / grad_norm)

    pieces, layout, ends_parts = [], [], {}
    for payloads, members in spreads:
        names_in = [name for _, group_names in members for name in group_names]
        spans, at = [], 0
        for name in names_in:
            size = sizes[name[0]]
            spans.append((at, start_of[name], size))
            if name[0] == "ends":
                ends_parts[name[1]] = (len(pieces), at)
            at += size
        for k, payload in enumerate(payloads):
            pieces.append(decoded(payload[:-16], tail_of(payload)))
            layout.append((k, spans))
    per_owner = owner_map.shape[1] // data_count
    slots = lax.dynamic_slice_in_dim(owner_map[0], data_index * per_owner, per_owner)
    edge = part * 4 // BLK
    firsts_of, kinds = [], []
    at = 0
    for i in range(layer_count):
        for name in ("qkv", "out", "up", "down"):
            firsts_of.append(at)
            kinds.append((start_of[name, i], sizes[name] // BLK, name in ("out", "down")))
            at += edge * sizes[name] // BLK
    top = jnp.zeros_like(slots)
    left_at = jnp.zeros_like(slots)
    turned = jnp.zeros_like(slots)
    for begin, (start, across, is_turned) in zip(firsts_of, kinds):
        inside = slots >= begin
        local = slots - begin
        top = jnp.where(inside, local % edge if is_turned else local // across, top)
        left_at = jnp.where(inside, start + BLK * (local // edge if is_turned else local % across), left_at)
        turned = jnp.where(inside, int(is_turned), turned)
    upper = (2 * top) ^ sub_index
    shift = left_at % 128
    info = jnp.stack([upper, (2 * top + 1) ^ sub_index, left_at // 128, (256 - shift) % 256, turned]).astype(jnp.int32)
    raw_grad, raw_left, raw_right, raw_precond, own_weight = shampoo(
        info, tiles_own, pieces, layout, root_left[0], root_right[0]
    )
    block_grad = raw_grad * factor
    square_factor = (1.0 - decay_stat) * factor * factor
    left_next = decay_stat * stat_left[0] + square_factor * raw_left
    right_next = decay_stat * stat_right[0] + square_factor * raw_right
    block_next = own_weight - rate_blocks * (factor * raw_precond + weight_decay * own_weight)

    ends_refs = []
    for end in range(2):
        index, at = ends_parts[end]
        ends_refs += [pieces[index + k][:, at : at + sizes["ends"]] for k in range(4)]
    ends_flat = whole_call_smem(
        ends_body, 1, 8, [((2, 4 * part, sizes["ends"]), f32)], "ends_order", 10**7
    )(places, *ends_refs)[0]
    ends_grad = ends_flat.transpose(0, 2, 1)
    step_value = step_count.astype(f32)
    vector_next, moment_vector, second_vector = adam_update(
        vectors, vec_sum, vector_moment, vector_second, rate_vector, 0.0, factor, step_value
    )
    ends_next, moment_ends, second_ends = adam_update(
        weight_ends.astype(f32),
        ends_grad,
        ends_moment,
        ends_second,
        rate_matrix,
        weight_decay,
        factor,
        step_value,
    )
    return (
        loss_total,
        grad_norm,
        vector_next,
        moment_vector,
        second_vector,
        ends_next,
        moment_ends,
        second_ends,
        block_grad[None],
        left_next[None],
        right_next[None],
        block_next[None],
    )


def solution(mesh):
    grid = P(None, "row", "col")
    slots = P(("row", "col"), "dp", None, None)
    return jax.shard_map(
        shards,
        mesh=mesh,
        in_specs=(
            P(None, ("dp", "col"), "row"),
            P(None, "dp"),
            P(None, "dp"),
            P(),
            P(),
            P(None, "col", "row"),
            grid,
            P(None, "col", "row"),
            grid,
            grid,
            P(),
            P(),
            P(),
            grid,
            grid,
            slots,
            slots,
            slots,
            slots,
            P(("row", "col"), None),
        ),
        out_specs=(P(), P(), P(), P(), P(), grid, grid, grid, slots, slots, slots, slots),
        check_vma=False,
    )
```

time: 4920 us -> 720 us (0.15)
  blocking collectives: 2360 us -> 0 us
  waiting for transfers between devices: 1280 us -> 228 us
  local copies, waits for them, and re-layouts: 677 us -> 74.1 us
  matrix products: 312 us -> 9.55 us
  Pallas kernels: 0 us -> 207 us
  other arithmetic: 203 us -> 74.4 us
  starting transfers between devices: 43.9 us -> 103 us
    unnamed x9 -> x0, blocking collectives: 2070 us -> none
    all_gather x20 -> x0, waiting for transfers between devices: 1040 us -> none  [gather_cols(): return lax.all_gather(value, 'col', axis=0, tiled=True)]
    unnamed x506 -> x332, local copies, waits for them, and re-layouts: 367 us -> 34.1 us
    dot_general x89 -> x5, matrix products: 312 us -> 9.55 us  [exact(): lax.dot_general(lhs_mat, rhs_mat, (((lhs_dim,), (rhs_dim,)), ((), ())), p...]
    psum x12 -> x0, blocking collectives: 238 us -> none  [the longest x10 188 us: col_totals(): return lax.psum((pair[0], pair[1]), 'col')]
    ppermute x0 -> x116, waiting for transfers between devices: none -> 228 us  [swap(): return lax.ppermute(value, axis, [(i, i ^ mask) for i in range(size)])]
    pallas_call x0 -> x29, Pallas kernels: none -> 207 us  [the longest x2 43.5 us: shards(): whole_call(lambda *refs: back_attend_body(base, *refs), outs, 'back_atten...]
    unnamed x60 -> x0, waiting for transfers between devices: 154 us -> none
  transfers between devices with their start and end apart: 50 -> 116, of which waited for: 33 -> 51; matrix products, arithmetic and copies ran while one was open for 12% -> 13% of each run, Pallas kernels for 0% -> 21%
where the time goes in v1:
time: 720 us; the launch traced here: 708 us
  waiting for transfers between devices  228 us (32%)
  Pallas kernels  207 us (29%)
  starting transfers between devices  103 us (14%)
  other arithmetic  74.4 us (10%)
  local copies, waits for them, and re-layouts  74.1 us (10%)
  between operations  12.5 us (2%)
  matrix products  9.55 us (1%)
    ppermute x116, waiting for transfers between devices, swap(): return lax.ppermute(value, axis, [(i, i ^ mask) for i in range(size)])  228 us
    ppermute x116, starting transfers between devices, swap(): return lax.ppermute(value, axis, [(i, i ^ mask) for i in range(size)])  103 us
    pallas_call x2, Pallas kernels, shards(): whole_call(lambda *refs: back_attend_body(base, *refs), outs, 'back_atten...  43.5 us
    unnamed x332, local copies, waits for them, and re-layouts  34.1 us
    pallas_call x11, Pallas kernels, product_sum(): pl.pallas_call(lambda *refs: product_body(runs, *refs), grid=(len(blocks)...  27.9 us
    pallas_call x2, Pallas kernels, shards(): whole_call(lambda *refs: back_mlp_body(base, *refs), outs, 'back_mlp', fu...  25.4 us
    pallas_call x1, Pallas kernels, shampoo(): pl.pallas_call(lambda *refs: shampoo_body(group, layout, *refs), grid=(co...  25.2 us
    pallas_call x2, Pallas kernels, forward_stage(): whole_call_smem(lambda *refs: up_body(base, *refs), 1, 9, outs, 'out_up',...  21.6 us
  transfers between devices with their start and end apart: 116, of which 51 were waited for; matrix products, arithmetic and copies ran while one was open for 13% of the time, Pallas kernels for 21%

profile of v1, /device:TPU:0, one launch (start us, length us, event | category | flops | bytes accessed | tf_op | source)
XLA Modules:
  0.0 708.3 jit_solution(16026789958730978502)
XLA Ops:
  4.6 6.0 prepare_tiles.1
  10.7 5.1 collective-permute-start.4
  16.4 4.1 collective-permute-done.4
  20.5 7.7 %collective-permute-done.3 = bf16[48,1536]{1,0:T(8,128)(2,1)S(1)} collective-permute-done((bf16[48,1536]{1,0:T(8,128)(2,1)S(1)}, bf16[48,1536]{1,0:T(8,128)(2,1)S(1)}, u32[]{:S(2)}, u32[]{:S(2)}) %collective-permute-start.3) | collective-permute-done | bytes 147488 | tf_op jit(solution)/shard_map/ppermute | solution.py:66
  35.7 5.0 collective-permute-done.9
  40.7 7.1 %collective-permute-done.8 = bf16[48,1920]{1,0:T(8,128)(2,1)S(1)} collective-permute-done((bf16[48,1920]{1,0:T(8,128)(2,1)S(1)}, bf16[48,1920]{1,0:T(8,128)(2,1)S(1)}, u32[]{:S(2)}, u32[]{:S(2)}) %collective-permute-start.8) | collective-permute-done | bytes 184352 | tf_op jit(solution)/shard_map/ppermute | solution.py:66
  53.4 4.4 constant_dynamic-slice_fusion.8
  59.0 11.2 %collective-permute-done.15 = bf16[48,2688]{1,0:T(8,128)(2,1)S(1)} collective-permute-done((bf16[48,2688]{1,0:T(8,128)(2,1)S(1)}, bf16[48,2688]{1,0:T(8,128)(2,1)S(1)}, u32[]{:S(2)}, u32[]{:S(2)}) %collective-permute-start.15) | collective-permute-done | bytes 258080 | tf_op jit(solution)/shard_map/ppermute | solution.py:66
  72.7 3.4 collective-permute-done.10.refs_4_
  86.8 5.0 collective-permute-done.23
  93.4 8.5 %collective-permute-done.22 = bf16[48,1920]{1,0:T(8,128)(2,1)S(1)} collective-permute-done((bf16[48,1920]{1,0:T(8,128)(2,1)S(1)}, bf16[48,1920]{1,0:T(8,128)(2,1)S(1)}, u32[]{:S(2)}, u32[]{:S(2)}) %collective-permute-start.22) | collective-permute-done | bytes 184352 | tf_op jit(solution)/shard_map/ppermute | solution.py:66
  116.4 12.4 %embed_qkv.1 = (f32[416,768]{1,0:T(8,128)}, bf16[416,768]{1,0:T(8,128)(2,1)}, bf16[416,1152]{1,0:T(8,128)(2,1)}, bf16[416,1152]{1,0:T(8,128)(2,1)}, bf16[416,384...) custom-call(s32[2]{0:T(128)S(1)} %pad_add_fusion.refs_0_.places, f32[227,768]{1,0:T(8,128)} %fusion.8.vec.refs_1_.refs_2_.refs_0_, ...), custom_call_target="tpu_custom_call" | custom-call | flops 122683392 | bytes 65536 | tf_op jit(solution)/shard_map/embed_qkv/pallas_call | solution.py:728
  134.2 7.7 %collective-permute-done.33 = bf16[48,1920]{1,0:T(8,128)(2,1)S(1)} collective-permute-done((bf16[48,1920]{1,0:T(8,128)(2,1)S(1)}, bf16[48,1920]{1,0:T(8,128)(2,1)S(1)}, u32[]{:S(2)}, u32[]{:S(2)}) %collective-permute-start.33) | collective-permute-done | bytes 184352 | tf_op jit(solution)/shard_map/ppermute | solution.py:66
  141.8 6.3 collective-permute-start.31
  150.7 3.7 collective-permute-done.31
  160.8 10.8 %out_up.2 = (f32[416,768]{1,0:T(8,128)}, bf16[416,768]{1,0:T(8,128)(2,1)}, bf16[416,1536]{1,0:T(8,128)(2,1)}, bf16[416,1536]{1,0:T(8,128)(2,1)}, f32[416,1536]{1,0:T(8,128)}, /*index=5*/f32[416,1536]{1,0:T(8,128)}) custom-call(s32[2]{0:T(128)S(1)} %pad_add_fusion.refs_0_.places, f32[227,768]{1,0:T(8,128)} %fusion.8.vec.refs_1_.refs_2_.refs_0_, ...), custom_call_target="tpu_custom_call" | custom-call | flops 153354240 | bytes 65536 | tf_op jit(solution)/shard_map/out_up/pallas_call | solution.py:735
  171.6 6.3 collective-permute-done.27.refs_4_
  177.9 4.2 assemble.7
  183.6 7.8 %collective-permute-done.38.refs_4_ = bf16[144,896]{1,0:T(8,128)(2,1)S(1)} collective-permute-done((bf16[144,896]{1,0:T(8,128)(2,1)S(1)}, bf16[144,896]{1,0:T(8,128)(2,1)S(1)}, u32[]{:S(2)}, u32[]{:S(2)}) %collective-permute-start.38) | collective-permute-done | bytes 258080 | tf_op jit(solution)/shard_map/ppermute | solution.py:66
  194.5 14.4 %down_qkv.1 = (f32[416,768]{1,0:T(8,128)}, bf16[416,768]{1,0:T(8,128)(2,1)S(1)}, bf16[416,1152]{1,0:T(8,128)(2,1)}, bf16[416,1152]{1,0:T(8,128)(2,1)}, bf16[416,...) custom-call(s32[2]{0:T(128)S(1)} %pad_add_fusion.refs_0_.places, f32[227,768]{1,0:T(8,128)S(1)} %copy-done.2, ...), custom_call_target="tpu_custom_call" | custom-call | flops 214695936 | bytes 65536 | tf_op jit(solution)/shard_map/down_qkv/pallas_call | solution.py:745
  211.9 3.8 assemble.8
  224.2 10.8 %out_up.3 = (f32[416,768]{1,0:T(8,128)}, bf16[416,768]{1,0:T(8,128)(2,1)}, bf16[416,1536]{1,0:T(8,128)(2,1)}, bf16[416,1536]{1,0:T(8,128)(2,1)}, f32[416,1536]{1,0:T(8,128)}, /*index=5*/f32[416,1536]{1,0:T(8,128)}) custom-call(s32[2]{0:T(128)S(1)} %pad_add_fusion.refs_0_.places, f32[227,768]{1,0:T(8,128)} %fusion.8.vec.refs_1_.refs_2_.refs_0_, ...), custom_call_target="tpu_custom_call" | custom-call | flops 153354240 | bytes 65536 | tf_op jit(solution)/shard_map/out_up/pallas_call | solution.py:735
  248.9 11.1 %down_head.1 = (bf16[416,768]{1,0:T(8,128)(2,1)}, bf16[416,384]{1,0:T(8,128)(2,1)S(1)}, bf16[416,384]{1,0:T(8,128)(2,1)S(1)}, f32[416,768]{1,0:T(8,128)}, bf16[4...) custom-call(s32[2]{0:T(128)S(1)} %pad_add_fusion.refs_0_.places, ...), custom_call_target="tpu_custom_call" | custom-call | flops 184025088 | bytes 65536 | tf_op jit(solution)/shard_map/down_head/pallas_call | solution.py:755
  262.2 12.6 %back_mlp.2 = (f32[416,768]{1,0:T(8,128)}, bf16[416,768]{1,0:T(8,128)(2,1)S(1)}, bf16[416,1536]{1,0:T(8,128)(2,1)}, bf16[416,1536]{1,0:T(8,128)(2,1)}, f32[8,768]{1,0:T(8,128)S(1)}, /*index=5*/f32[8,768]{1,0:T(8,128)S(1)}) custom-call(f32[227,768]{1,0:T(8,128)} %fusion.8.vec.refs_1_.refs_2_.refs_0_, f32[416,768]{1,0:T(8,128)} %get-tuple-element.447.refs_1_, ...), custom_call_target="tpu_custom_call" | custom-call | flops 245366784 | bytes 65536 | tf_op jit(solution)/shard_map/back_mlp/pallas_call | solution.py:827
  281.5 4.6 product_sum.11
  290.3 4.1 product_sum.13
  298.1 21.7 %back_attend.2 = (f32[416,768]{1,0:T(8,128)}, bf16[416,768]{1,0:T(8,128)(2,1)S(1)}, bf16[416,1152]{1,0:T(8,128)(2,1)}, bf16[416,1152]{1,0:T(8,128)(2,1)}, f32[8,768]{1,0:T(8,128)S(1)}, /*index=5*/f32[8,768]{1,0:T(8,128)S(1)}) custom-call(f32[227,768]{1,0:T(8,128)} %fusion.8.vec.refs_1_.refs_2_.refs_0_, f32[416,768]{1,0:T(8,128)} %get-tuple-element.469.refs_1_, ...), custom_call_target="tpu_custom_call" | custom-call | flops 245366784 | bytes 65536 | tf_op jit(solution)/shard_map/back_attend/pallas_call | solution.py:847
  355.1 12.8 %back_mlp.3 = (f32[416,768]{1,0:T(8,128)}, bf16[416,768]{1,0:T(8,128)(2,1)S(1)}, bf16[416,1536]{1,0:T(8,128)(2,1)}, bf16[416,1536]{1,0:T(8,128)(2,1)}, f32[8,768]{1,0:T(8,128)S(1)}, /*index=5*/f32[8,768]{1,0:T(8,128)S(1)}) custom-call(f32[227,768]{1,0:T(8,128)} %fusion.8.vec.refs_1_.refs_2_.refs_0_, f32[416,768]{1,0:T(8,128)} %get-tuple-element.495.refs_1_, ...), custom_call_target="tpu_custom_call" | custom-call | flops 245366784 | bytes 65536 | tf_op jit(solution)/shard_map/back_mlp/pallas_call | solution.py:827
  374.9 4.6 product_sum.17
  385.8 3.7 product_sum.18
  390.7 12.1 %collective-permute-done.68 = f16[400,768]{1,0:T(8,128)(2,1)S(1)} collective-permute-done((f16[400,768]{1,0:T(8,128)(2,1)S(1)}, f16[400,768]{1,0:T(8,128)(2,1)S(1)}, u32[]{:S(2)}, u32[]{:S(2)}) %collective-permute-start.68) | collective-permute-done | bytes 614432 | tf_op jit(solution)/shard_map/ppermute | solution.py:66
  406.1 21.8 %back_attend.3 = (f32[416,768]{1,0:T(8,128)}, bf16[416,768]{1,0:T(8,128)(2,1)}, bf16[416,1152]{1,0:T(8,128)(2,1)}, bf16[416,1152]{1,0:T(8,128)(2,1)}, f32[8,768]{1,0:T(8,128)S(1)}, /*index=5*/f32[8,768]{1,0:T(8,128)S(1)}) custom-call(f32[227,768]{1,0:T(8,128)} %fusion.8.vec.refs_1_.refs_2_.refs_0_, f32[416,768]{1,0:T(8,128)} %get-tuple-element.523.refs_1_, ...), custom_call_target="tpu_custom_call" | custom-call | flops 245366784 | bytes 65536 | tf_op jit(solution)/shard_map/back_attend/pallas_call | solution.py:847
  462.5 3.5 collective-permute-done.106
  467.2 4.5 collective-permute-done.107
  473.4 3.8 collective-permute-done.108
  484.9 3.9 product_sum.19
  489.0 3.5 collective-permute-done.72
  510.1 20.4 %collective-permute-done.78 = f16[64,3456]{1,0:T(8,128)(2,1)S(1)} collective-permute-done((f16[64,3456]{1,0:T(8,128)(2,1)S(1)}, f16[64,3456]{1,0:T(8,128)(2,1)S(1)}, u32[]{:S(2)}, u32[]{:S(2)}) %collective-permute-start.78) | collective-permute-done | bytes 442400 | tf_op jit(solution)/shard_map/ppermute | solution.py:66
  531.0 7.8 %collective-permute-done.82 = f16[400,1152]{1,0:T(8,128)(2,1)S(1)} collective-permute-done((f16[400,1152]{1,0:T(8,128)(2,1)S(1)}, f16[400,1152]{1,0:T(8,128)(2,1)S(1)}, u32[]{:S(2)}, u32[]{:S(2)}) %collective-permute-start.82) | collective-permute-done | bytes 921632 | tf_op jit(solution)/shard_map/ppermute | solution.py:66
  553.6 7.6 %collective-permute-done.85 = f16[112,3072]{1,0:T(8,128)(2,1)S(1)} collective-permute-done((f16[112,3072]{1,0:T(8,128)(2,1)S(1)}, f16[112,3072]{1,0:T(8,128)(2,1)S(1)}, u32[]{:S(2)}, u32[]{:S(2)}) %collective-permute-start.85) | collective-permute-done | bytes 688160 | tf_op jit(solution)/shard_map/ppermute | solution.py:66
  574.1 11.6 %collective-permute-done.88 = f16[64,3072]{1,0:T(8,128)(2,1)} collective-permute-done((f16[64,3072]{1,0:T(8,128)(2,1)}, f16[64,3072]{1,0:T(8,128)(2,1)}, u32[]{:S(2)}, u32[]{:S(2)}) %collective-permute-start.88) | collective-permute-done | bytes 393248 | tf_op jit(solution)/shard_map/ppermute | solution.py:66
  603.5 3.6 collective-permute-done.90
  620.7 21.2 %collective-permute-done.99 = f32[2]{0:T(128)S(1)} collective-permute-done((f32[2]{0:T(128)S(1)}, f32[2]{0:T(128)S(1)}, u32[]{:S(2)}, u32[]{:S(2)}) %collective-permute-start.99) | collective-permute-done | bytes 40 | tf_op jit(solution)/shard_map/ppermute | solution.py:66
  646.1 3.5 collective-permute-done.101
  649.8 4.3 collective-permute-done.102
  655.5 3.9 multiply_subtract_fusion
  667.1 25.2 %shampoo.1 = (f32[48,96,96]{2,1,0:T(8,128)}, f32[48,96,96]{2,1,0:T(8,128)}, f32[48,96,96]{2,1,0:T(8,128)}, f32[48,96,96]{2,1,0:T(8,128)}, f32[48,96,96]{2,1,0:T(8,128)}) custom-call(s32[5,48]{1,0:T(8,128)S(1)} %stack.36.refs_0_, bf16[4,48,9984]{2,1,0:T(8,128)(2,1)} %get-tuple-element.594.refs_1_, f32[48,4992]{1,0:T(8,128)S(1)} %get-tuple-element.607.refs_2_, ...), custom_call_target="tpu_custom_call" | custom-call | flops 127401984 | bytes 65536 | tf_op jit(solution)/shard_map/shampoo/pallas_call | solution.py:574
  692.3 3.4 multiply_bitcast_fusion
  (913 shorter events, 299.3 us)
Async XLA Ops:
  28.2 19.7 %collective-permute-start.5 = (bf16[144,1536]{1,0:T(8,128)(2,1)S(1)}, bf16[144,1536]{1,0:T(8,128)(2,1)S(1)}, u32[]{:S(2)}, u32[]{:S(2)}) collective-permute-start(bf16[144,1536]{1,0:T(8,128)(2,1)S(1)} %pad_maximum_fusion.21.refs_1_), channel_id=1, source_target_pairs={{0,8},{8,0},{16,24},{24,16},{1,9},{9,1},{17,25},{25,17},{2,10},{10... | collective-permute-start | bytes 1327112 | tf_op jit(solution)/shard_map/ppermute | solution.py:66
  49.4 20.9 %collective-permute-start.15 = (bf16[48,2688]{1,0:T(8,128)(2,1)S(1)}, bf16[48,2688]{1,0:T(8,128)(2,1)S(1)}, u32[]{:S(2)}, u32[]{:S(2)}) collective-permute-start(bf16[48,2688]{1,0:T(8,128)(2,1)S(1)} %get-tuple-element.320), channel_id=1, source_target_pairs={{0,2},{1,3},{2,0},{3,1},{4,6},{5,7},{6,4},{7,5},{8,10},{9,11},{10,... | collective-permute-start | bytes 774152 | tf_op jit(solution)/shard_map/ppermute | solution.py:66
  49.4 21.4 %collective-permute-start.14 = (bf16[48,2688]{1,0:T(8,128)(2,1)S(1)}, bf16[48,2688]{1,0:T(8,128)(2,1)}, u32[]{:S(2)}, u32[]{:S(2)}) collective-permute-start(bf16[48,2688]{1,0:T(8,128)(2,1)S(1)} %get-tuple-element.320), channel_id=1, source_target_pairs={{0,1},{1,0},{2,3},{3,2},{4,5},{5,4},{6,7},{7,6},{8,9},{9,8},{10,11... | collective-permute-start | bytes 774152 | tf_op jit(solution)/shard_map/ppermute | solution.py:66
  52.4 24.5 %collective-permute-start.12 = (bf16[144,1920]{1,0:T(8,128)(2,1)S(1)}, bf16[144,1920]{1,0:T(8,128)(2,1)S(1)}, u32[]{:S(2)}, u32[]{:S(2)}) collective-permute-start(bf16[144,1920]{1,0:T(8,128)(2,1)S(1)} %pad_maximum_fusion.17.refs_1_), channel_id=1, source_target_pairs={{0,8},{8,0},{16,24},{24,16},{1,9},{9,1},{17,25},{25,17},{2,10},{10... | collective-permute-start | bytes 1658888 | tf_op jit(solution)/shard_map/ppermute | solution.py:66
  52.9 24.0 %collective-permute-start.13 = (bf16[144,1920]{1,0:T(8,128)(2,1)S(1)}, bf16[144,1920]{1,0:T(8,128)(2,1)}, u32[]{:S(2)}, u32[]{:S(2)}) collective-permute-start(bf16[144,1920]{1,0:T(8,128)(2,1)S(1)} %pad_maximum_fusion.17.refs_1_), channel_id=1, source_target_pairs={{0,16},{8,24},{16,0},{24,8},{1,17},{9,25},{17,1},{25,9},{2,18},{10... | collective-permute-start | bytes 1658888 | tf_op jit(solution)/shard_map/ppermute | solution.py:66
  59.0 26.4 %collective-permute-start.24 = (bf16[394,384]{1,0:T(8,128)(2,1)}, bf16[394,384]{1,0:T(8,128)(2,1)}, u32[]{:S(2)}, u32[]{:S(2)}) collective-permute-start(bf16[394,384]{1,0:T(8,128)(2,1)} %bitcast.435), channel_id=1, source_target_pairs={{0,4},{4,0},{1,5},{5,1},{2,6},{6,2},{3,7},{7,3},{8,12},{12,8},{9,1... | collective-permute-start | bytes 907784 | tf_op jit(solution)/shard_map/ppermute | solution.py:66
  79.4 37.0 %collective-permute-start.26 = (bf16[768,1152]{1,0:T(8,128)(2,1)}, bf16[768,1152]{1,0:T(8,128)(2,1)}, u32[]{:S(2)}, u32[]{:S(2)}) collective-permute-start(bf16[768,1152]{1,0:T(8,128)(2,1)} %get-tuple-element.336.qkv_a.refs_7_), channel_id=1, source_target_pairs={{0,4},{4,0},{1,5},{5,1},{2,6},{6,2},{3,7},{7,3},{8,12},{12,8},{9,1... | collective-permute-start | bytes 5308424 | tf_op jit(solution)/shard_map/ppermute | solution.py:66
  84.3 25.3 %collective-permute-start.25 = (bf16[768,384]{1,0:T(8,128)(2,1)}, bf16[768,384]{1,0:T(8,128)(2,1)}, u32[]{:S(2)}, u32[]{:S(2)}) collective-permute-start(bf16[768,384]{1,0:T(8,128)(2,1)} %get-tuple-element.335.ends_a), channel_id=1, source_target_pairs={{0,4},{4,0},{1,5},{5,1},{2,6},{6,2},{3,7},{7,3},{8,12},{12,8},{9,1... | collective-permute-start | bytes 1769480 | tf_op jit(solution)/shard_map/ppermute | solution.py:66
  84.8 44.0 %collective-permute-start.19 = (bf16[144,2688]{1,0:T(8,128)(2,1)S(1)}, bf16[144,2688]{1,0:T(8,128)(2,1)}, u32[]{:S(2)}, u32[]{:S(2)}) collective-permute-start(bf16[144,2688]{1,0:T(8,128)(2,1)S(1)} %pad_maximum_fusion.5.refs_1_), channel_id=1, source_target_pairs={{0,8},{8,0},{16,24},{24,16},{1,9},{9,1},{17,25},{25,17},{2,10},{10... | collective-permute-start | bytes 2322440 | tf_op jit(solution)/shard_map/ppermute | solution.py:66
  85.4 43.4 %collective-permute-start.20 = (bf16[144,2688]{1,0:T(8,128)(2,1)S(1)}, bf16[144,2688]{1,0:T(8,128)(2,1)}, u32[]{:S(2)}, u32[]{:S(2)}) collective-permute-start(bf16[144,2688]{1,0:T(8,128)(2,1)S(1)} %pad_maximum_fusion.5.refs_1_), channel_id=1, source_target_pairs={{0,16},{8,24},{16,0},{24,8},{1,17},{9,25},{17,1},{25,9},{2,18},{10... | collective-permute-start | bytes 2322440 | tf_op jit(solution)/shard_map/ppermute | solution.py:66
  108.2 20.6 %collective-permute-start.17 = (bf16[144,896]{1,0:T(8,128)(2,1)}, bf16[144,896]{1,0:T(8,128)(2,1)S(1)}, u32[]{:S(2)}, u32[]{:S(2)}) collective-permute-start(bf16[144,896]{1,0:T(8,128)(2,1)} %slice.499), channel_id=1, source_target_pairs={{0,16},{8,24},{16,0},{24,8},{1,17},{9,25},{17,1},{25,9},{2,18},{10... | collective-permute-start | bytes 774152 | tf_op jit(solution)/shard_map/ppermute | solution.py:66
  131.9 27.3 %collective-permute-start.37 = (bf16[768,1536]{1,0:T(8,128)(2,1)}, bf16[768,1536]{1,0:T(8,128)(2,1)S(1)}, u32[]{:S(2)}, u32[]{:S(2)}) collective-permute-start(bf16[768,1536]{1,0:T(8,128)(2,1)} %get-tuple-element.361.refs_8_.refs_7_), channel_id=1, source_target_pairs={{0,4},{4,0},{1,5},{5,1},{2,6},{6,2},{3,7},{7,3},{8,12},{12,8},{9,1... | collective-permute-start | bytes 7077896 | tf_op jit(solution)/shard_map/ppermute | solution.py:66
  131.9 25.6 %collective-permute-start.36 = (bf16[768,384]{1,0:T(8,128)(2,1)}, bf16[768,384]{1,0:T(8,128)(2,1)S(1)}, u32[]{:S(2)}, u32[]{:S(2)}) collective-permute-start(bf16[768,384]{1,0:T(8,128)(2,1)} %get-tuple-element.360.refs_6_.refs_3_), channel_id=1, source_target_pairs={{0,4},{4,0},{1,5},{5,1},{2,6},{6,2},{3,7},{7,3},{8,12},{12,8},{9,1... | collective-permute-start | bytes 1769480 | tf_op jit(solution)/shard_map/ppermute | solution.py:66
  134.1 21.8 %collective-permute-start.35 = (bf16[416,384]{1,0:T(8,128)(2,1)S(1)}, bf16[416,384]{1,0:T(8,128)(2,1)S(1)}, u32[]{:S(2)}, u32[]{:S(2)}) collective-permute-start(bf16[416,384]{1,0:T(8,128)(2,1)S(1)} %get-tuple-element.353.refs_5_), channel_id=1, source_target_pairs={{0,4},{4,0},{1,5},{5,1},{2,6},{6,2},{3,7},{7,3},{8,12},{12,8},{9,1... | collective-permute-start | bytes 958472 | tf_op jit(solution)/shard_map/ppermute | solution.py:66
  150.7 27.2 %collective-permute-start.34 = (bf16[416,768]{1,0:T(8,128)(2,1)S(1)}, bf16[416,768]{1,0:T(8,128)(2,1)S(1)}, u32[]{:S(2)}, u32[]{:S(2)}) collective-permute-start(bf16[416,768]{1,0:T(8,128)(2,1)S(1)} %copy-done.35), channel_id=1, source_target_pairs={{0,4},{4,0},{1,5},{5,1},{2,6},{6,2},{3,7},{7,3},{8,12},{12,8},{9,1... | collective-permute-start | bytes 1916936 | tf_op jit(solution)/shard_map/ppermute | solution.py:66
  154.4 23.5 %collective-permute-start.29 = (bf16[144,1920]{1,0:T(8,128)(2,1)S(1)}, bf16[144,1920]{1,0:T(8,128)(2,1)S(1)}, u32[]{:S(2)}, u32[]{:S(2)}) collective-permute-start(bf16[144,1920]{1,0:T(8,128)(2,1)S(1)} %pad_maximum_fusion.18.refs_1_), channel_id=1, source_target_pairs={{0,8},{8,0},{16,24},{24,16},{1,9},{9,1},{17,25},{25,17},{2,10},{10... | collective-permute-start | bytes 1658888 | tf_op jit(solution)/shard_map/ppermute | solution.py:66
  155.9 22.0 %collective-permute-start.30 = (bf16[144,1920]{1,0:T(8,128)(2,1)S(1)}, bf16[144,1920]{1,0:T(8,128)(2,1)S(1)}, u32[]{:S(2)}, u32[]{:S(2)}) collective-permute-start(bf16[144,1920]{1,0:T(8,128)(2,1)S(1)} %pad_maximum_fusion.18.refs_1_), channel_id=1, source_target_pairs={{0,16},{8,24},{16,0},{24,8},{1,17},{9,25},{17,1},{25,9},{2,18},{10... | collective-permute-start | bytes 1658888 | tf_op jit(solution)/shard_map/ppermute | solution.py:66
  157.6 20.3 %collective-permute-start.28 = (bf16[144,1408]{1,0:T(8,128)(2,1)S(1)}, bf16[144,1408]{1,0:T(8,128)(2,1)S(1)}, u32[]{:S(2)}, u32[]{:S(2)}) collective-permute-start(bf16[144,1408]{1,0:T(8,128)(2,1)S(1)} %slice.502), channel_id=1, source_target_pairs={{0,8},{8,0},{16,24},{24,16},{1,9},{9,1},{17,25},{25,17},{2,10},{10... | collective-permute-start | bytes 1216520 | tf_op jit(solution)/shard_map/ppermute | solution.py:66
  182.7 29.2 %collective-permute-start.43 = (bf16[416,1536]{1,0:T(8,128)(2,1)}, bf16[416,1536]{1,0:T(8,128)(2,1)S(1)}, u32[]{:S(2)}, u32[]{:S(2)}) collective-permute-start(bf16[416,1536]{1,0:T(8,128)(2,1)} %get-tuple-element.382.refs_5_), channel_id=1, source_target_pairs={{0,4},{4,0},{1,5},{5,1},{2,6},{6,2},{3,7},{7,3},{8,12},{12,8},{9,1... | collective-permute-start | bytes 3833864 | tf_op jit(solution)/shard_map/ppermute | solution.py:66
  183.5 28.4 %collective-permute-start.42 = (bf16[416,768]{1,0:T(8,128)(2,1)S(1)}, bf16[416,768]{1,0:T(8,128)(2,1)S(1)}, u32[]{:S(2)}, u32[]{:S(2)}) collective-permute-start(bf16[416,768]{1,0:T(8,128)(2,1)S(1)} %copy-done.42), channel_id=1, source_target_pairs={{0,4},{4,0},{1,5},{5,1},{2,6},{6,2},{3,7},{7,3},{8,12},{12,8},{9,1... | collective-permute-start | bytes 1916936 | tf_op jit(solution)/shard_map/ppermute | solution.py:66
  191.4 20.4 %collective-permute-start.40 = (bf16[144,1920]{1,0:T(8,128)(2,1)S(1)}, bf16[144,1920]{1,0:T(8,128)(2,1)S(1)}, u32[]{:S(2)}, u32[]{:S(2)}) collective-permute-start(bf16[144,1920]{1,0:T(8,128)(2,1)S(1)} %pad_maximum_fusion.19.refs_1_), channel_id=1, source_target_pairs={{0,8},{8,0},{16,24},{24,16},{1,9},{9,1},{17,25},{25,17},{2,10},{10... | collective-permute-start | bytes 1658888 | tf_op jit(solution)/shard_map/ppermute | solution.py:66
  192.5 19.4 %collective-permute-start.41 = (bf16[144,1920]{1,0:T(8,128)(2,1)S(1)}, bf16[144,1920]{1,0:T(8,128)(2,1)S(1)}, u32[]{:S(2)}, u32[]{:S(2)}) collective-permute-start(bf16[144,1920]{1,0:T(8,128)(2,1)S(1)} %pad_maximum_fusion.19.refs_1_), channel_id=1, source_target_pairs={{0,16},{8,24},{16,0},{24,8},{1,17},{9,25},{17,1},{25,9},{2,18},{10... | collective-permute-start | bytes 1658888 | tf_op jit(solution)/shard_map/ppermute | solution.py:66
  238.4 41.1 %collective-permute-start.56 = (bf16[416,1536]{1,0:T(8,128)(2,1)}, bf16[416,1536]{1,0:T(8,128)(2,1)}, u32[]{:S(2)}, u32[]{:S(2)}) collective-permute-start(bf16[416,1536]{1,0:T(8,128)(2,1)} %get-tuple-element.438.refs_6_), channel_id=1, source_target_pairs={{0,4},{4,0},{1,5},{5,1},{2,6},{6,2},{3,7},{7,3},{8,12},{12,8},{9,1... | collective-permute-start | bytes 3833864 | tf_op jit(solution)/shard_map/ppermute | solution.py:66
  297.0 53.2 %collective-permute-start.62 = (f16[400,1920]{1,0:T(8,128)(2,1)}, f16[400,1920]{1,0:T(8,128)(2,1)}, u32[]{:S(2)}, u32[]{:S(2)}) collective-permute-start(f16[400,1920]{1,0:T(8,128)(2,1)} %pad_maximum_fusion.1), channel_id=1, source_target_pairs={{0,8},{8,0},{16,24},{24,16},{1,9},{9,1},{17,25},{25,17},{2,10},{10... | collective-permute-start | bytes 4608008 | tf_op jit(solution)/shard_map/ppermute | solution.py:66
  319.8 23.1 %collective-permute-start.64 = (bf16[416,1152]{1,0:T(8,128)(2,1)}, bf16[416,1152]{1,0:T(8,128)(2,1)S(1)}, u32[]{:S(2)}, u32[]{:S(2)}) collective-permute-start(bf16[416,1152]{1,0:T(8,128)(2,1)} %get-tuple-element.481), channel_id=1, source_target_pairs={{0,4},{4,0},{1,5},{5,1},{2,6},{6,2},{3,7},{7,3},{8,12},{12,8},{9,1... | collective-permute-start | bytes 2875400 | tf_op jit(solution)/shard_map/ppermute | solution.py:66
  320.6 29.7 %collective-permute-start.63 = (f16[400,1536]{1,0:T(8,128)(2,1)}, f16[400,1536]{1,0:T(8,128)(2,1)}, u32[]{:S(2)}, u32[]{:S(2)}) collective-permute-start(f16[400,1536]{1,0:T(8,128)(2,1)} %convert_element_type.512), channel_id=1, source_target_pairs={{0,16},{8,24},{16,0},{24,8},{1,17},{9,25},{17,1},{25,9},{2,18},{10... | collective-permute-start | bytes 3686408 | tf_op jit(solution)/shard_map/ppermute | solution.py:66
  324.5 24.3 %collective-permute-start.61 = (bf16[416,768]{1,0:T(8,128)(2,1)S(1)}, bf16[416,768]{1,0:T(8,128)(2,1)}, u32[]{:S(2)}, u32[]{:S(2)}) collective-permute-start(bf16[416,768]{1,0:T(8,128)(2,1)S(1)} %get-tuple-element.496.refs_2_.refs_0_), channel_id=1, source_target_pairs={{0,4},{4,0},{1,5},{5,1},{2,6},{6,2},{3,7},{7,3},{8,12},{12,8},{9,1... | collective-permute-start | bytes 1916936 | tf_op jit(solution)/shard_map/ppermute | solution.py:66
  367.9 34.9 %collective-permute-start.65 = (bf16[416,768]{1,0:T(8,128)(2,1)S(1)}, bf16[416,768]{1,0:T(8,128)(2,1)S(1)}, u32[]{:S(2)}, u32[]{:S(2)}) collective-permute-start(bf16[416,768]{1,0:T(8,128)(2,1)S(1)} %get-tuple-element.524.refs_2_.refs_0_), channel_id=1, source_target_pairs={{0,4},{4,0},{1,5},{5,1},{2,6},{6,2},{3,7},{7,3},{8,12},{12,8},{9,1... | collective-permute-start | bytes 1916936 | tf_op jit(solution)/shard_map/ppermute | solution.py:66
  369.0 33.8 %collective-permute-start.66 = (f16[208,1920]{1,0:T(8,128)(2,1)S(1)}, f16[208,1920]{1,0:T(8,128)(2,1)S(1)}, u32[]{:S(2)}, u32[]{:S(2)}) collective-permute-start(f16[208,1920]{1,0:T(8,128)(2,1)S(1)} %pad_maximum_fusion.4), channel_id=1, source_target_pairs={{0,16},{8,24},{16,0},{24,8},{1,17},{9,25},{17,1},{25,9},{2,18},{10... | collective-permute-start | bytes 2396168 | tf_op jit(solution)/shard_map/ppermute | solution.py:66
  372.8 30.0 %collective-permute-start.67 = (f16[208,1536]{1,0:T(8,128)(2,1)S(1)}, f16[208,1536]{1,0:T(8,128)(2,1)S(1)}, u32[]{:S(2)}, u32[]{:S(2)}) collective-permute-start(f16[208,1536]{1,0:T(8,128)(2,1)S(1)} %pad_maximum_fusion.9), channel_id=1, source_target_pairs={{0,8},{8,0},{16,24},{24,16},{1,9},{9,1},{17,25},{25,17},{2,10},{10... | collective-permute-start | bytes 1916936 | tf_op jit(solution)/shard_map/ppermute | solution.py:66
  373.8 29.0 %collective-permute-start.68 = (f16[400,768]{1,0:T(8,128)(2,1)S(1)}, f16[400,768]{1,0:T(8,128)(2,1)S(1)}, u32[]{:S(2)}, u32[]{:S(2)}) collective-permute-start(f16[400,768]{1,0:T(8,128)(2,1)S(1)} %copy-done.105), channel_id=1, source_target_pairs={{0,8},{8,0},{16,24},{24,16},{1,9},{9,1},{17,25},{25,17},{2,10},{10... | collective-permute-start | bytes 1843208 | tf_op jit(solution)/shard_map/ppermute | solution.py:66
  381.3 21.4 %collective-permute-start.69 = (f16[400,768]{1,0:T(8,128)(2,1)S(1)}, f16[400,768]{1,0:T(8,128)(2,1)S(1)}, u32[]{:S(2)}, u32[]{:S(2)}) collective-permute-start(f16[400,768]{1,0:T(8,128)(2,1)S(1)} %copy-done.106), channel_id=1, source_target_pairs={{0,16},{8,24},{16,0},{24,8},{1,17},{9,25},{17,1},{25,9},{2,18},{10... | collective-permute-start | bytes 1843208 | tf_op jit(solution)/shard_map/ppermute | solution.py:66
  404.3 89.1 %collective-permute-start.74 = (f16[400,1536]{1,0:T(8,128)(2,1)}, f16[400,1536]{1,0:T(8,128)(2,1)}, u32[]{:S(2)}, u32[]{:S(2)}) collective-permute-start(f16[400,1536]{1,0:T(8,128)(2,1)} %convert_element_type.522), channel_id=1, source_target_pairs={{0,8},{8,0},{16,24},{24,16},{1,9},{9,1},{17,25},{25,17},{2,10},{10... | collective-permute-start | bytes 3686408 | tf_op jit(solution)/shard_map/ppermute | solution.py:66
  405.2 88.1 %collective-permute-start.75 = (f16[400,1536]{1,0:T(8,128)(2,1)}, f16[400,1536]{1,0:T(8,128)(2,1)}, u32[]{:S(2)}, u32[]{:S(2)}) collective-permute-start(f16[400,1536]{1,0:T(8,128)(2,1)} %convert_element_type.523), channel_id=1, source_target_pairs={{0,16},{8,24},{16,0},{24,8},{1,17},{9,25},{17,1},{25,9},{2,18},{10... | collective-permute-start | bytes 3686408 | tf_op jit(solution)/shard_map/ppermute | solution.py:66
  457.8 24.7 %collective-permute-start.76 = (bf16[416,1152]{1,0:T(8,128)(2,1)S(1)}, bf16[416,1152]{1,0:T(8,128)(2,1)S(1)}, u32[]{:S(2)}, u32[]{:S(2)}) collective-permute-start(bf16[416,1152]{1,0:T(8,128)(2,1)S(1)} %copy-done.155), channel_id=1, source_target_pairs={{0,4},{4,0},{1,5},{5,1},{2,6},{6,2},{3,7},{7,3},{8,12},{12,8},{9,1... | collective-permute-start | bytes 2875400 | tf_op jit(solution)/shard_map/ppermute | solution.py:66
  502.3 28.6 %collective-permute-start.80 = (f16[208,1536]{1,0:T(8,128)(2,1)S(1)}, f16[208,1536]{1,0:T(8,128)(2,1)S(1)}, u32[]{:S(2)}, u32[]{:S(2)}) collective-permute-start(f16[208,1536]{1,0:T(8,128)(2,1)S(1)} %pad_maximum_fusion.10), channel_id=1, source_target_pairs={{0,16},{8,24},{16,0},{24,8},{1,17},{9,25},{17,1},{25,9},{2,18},{10... | collective-permute-start | bytes 1916936 | tf_op jit(solution)/shard_map/ppermute | solution.py:66
  503.9 27.1 %collective-permute-start.81 = (f16[208,1536]{1,0:T(8,128)(2,1)S(1)}, f16[208,1536]{1,0:T(8,128)(2,1)S(1)}, u32[]{:S(2)}, u32[]{:S(2)}) collective-permute-start(f16[208,1536]{1,0:T(8,128)(2,1)S(1)} %pad_maximum_fusion.11), channel_id=1, source_target_pairs={{0,8},{8,0},{16,24},{24,16},{1,9},{9,1},{17,25},{25,17},{2,10},{10... | collective-permute-start | bytes 1916936 | tf_op jit(solution)/shard_map/ppermute | solution.py:66
  505.0 33.8 %collective-permute-start.82 = (f16[400,1152]{1,0:T(8,128)(2,1)S(1)}, f16[400,1152]{1,0:T(8,128)(2,1)S(1)}, u32[]{:S(2)}, u32[]{:S(2)}) collective-permute-start(f16[400,1152]{1,0:T(8,128)(2,1)S(1)} %convert_element_type.542), channel_id=1, source_target_pairs={{0,8},{8,0},{16,24},{24,16},{1,9},{9,1},{17,25},{25,17},{2,10},{10... | collective-permute-start | bytes 2764808 | tf_op jit(solution)/shard_map/ppermute | solution.py:66
  505.9 25.0 %collective-permute-start.83 = (f16[400,768]{1,0:T(8,128)(2,1)S(1)}, f16[400,768]{1,0:T(8,128)(2,1)S(1)}, u32[]{:S(2)}, u32[]{:S(2)}) collective-permute-start(f16[400,768]{1,0:T(8,128)(2,1)S(1)} %pad_maximum_fusion.15), channel_id=1, source_target_pairs={{0,16},{8,24},{16,0},{24,8},{1,17},{9,25},{17,1},{25,9},{2,18},{10... | collective-permute-start | bytes 1843208 | tf_op jit(solution)/shard_map/ppermute | solution.py:66
  509.3 21.2 %collective-permute-start.78 = (f16[64,3456]{1,0:T(8,128)(2,1)S(1)}, f16[64,3456]{1,0:T(8,128)(2,1)S(1)}, u32[]{:S(2)}, u32[]{:S(2)}) collective-permute-start(f16[64,3456]{1,0:T(8,128)(2,1)S(1)} %pad_maximum_fusion.22), channel_id=1, source_target_pairs={{0,2},{1,3},{2,0},{3,1},{4,6},{5,7},{6,4},{7,5},{8,10},{9,11},{10,... | collective-permute-start | bytes 1327112 | tf_op jit(solution)/shard_map/ppermute | solution.py:66
  541.8 19.4 %collective-permute-start.85 = (f16[112,3072]{1,0:T(8,128)(2,1)S(1)}, f16[112,3072]{1,0:T(8,128)(2,1)S(1)}, u32[]{:S(2)}, u32[]{:S(2)}) collective-permute-start(f16[112,3072]{1,0:T(8,128)(2,1)S(1)} %pad_maximum_fusion.7), channel_id=1, source_target_pairs={{0,1},{1,0},{2,3},{3,2},{4,5},{5,4},{6,7},{7,6},{8,9},{9,8},{10,11... | collective-permute-start | bytes 2064392 | tf_op jit(solution)/shard_map/ppermute | solution.py:66
  563.7 32.9 %collective-permute-start.113 = (f16[64,4992]{1,0:T(8,128)(2,1)}, f16[64,4992]{1,0:T(8,128)(2,1)}, u32[]{:S(2)}, u32[]{:S(2)}) collective-permute-start(f16[64,4992]{1,0:T(8,128)(2,1)} %pad_maximum_fusion.13), channel_id=1, source_target_pairs={{0,8},{8,0},{16,24},{24,16},{1,9},{9,1},{17,25},{25,17},{2,10},{10... | collective-permute-start | bytes 1916936 | tf_op jit(solution)/shard_map/ppermute | solution.py:66
  564.8 32.8 %collective-permute-start.114 = (f16[64,4992]{1,0:T(8,128)(2,1)}, f16[64,4992]{1,0:T(8,128)(2,1)}, u32[]{:S(2)}, u32[]{:S(2)}) collective-permute-start(f16[64,4992]{1,0:T(8,128)(2,1)} %pad_maximum_fusion.13), channel_id=1, source_target_pairs={{0,16},{8,24},{16,0},{24,8},{1,17},{9,25},{17,1},{25,9},{2,18},{10... | collective-permute-start | bytes 1916936 | tf_op jit(solution)/shard_map/ppermute | solution.py:66
  566.0 32.7 %collective-permute-start.115 = (f16[64,4992]{1,0:T(8,128)(2,1)}, f16[64,4992]{1,0:T(8,128)(2,1)}, u32[]{:S(2)}, u32[]{:S(2)}) collective-permute-start(f16[64,4992]{1,0:T(8,128)(2,1)} %pad_maximum_fusion.13), channel_id=1, source_target_pairs={{0,24},{8,16},{16,8},{24,0},{1,25},{9,17},{17,9},{25,1},{2,26},{10... | collective-permute-start | bytes 1916936 | tf_op jit(solution)/shard_map/ppermute | solution.py:66
  612.0 47.3 %collective-permute-start.110 = (f16[64,4992]{1,0:T(8,128)(2,1)}, f16[64,4992]{1,0:T(8,128)(2,1)}, u32[]{:S(2)}, u32[]{:S(2)}) collective-permute-start(f16[64,4992]{1,0:T(8,128)(2,1)} %pad_maximum_fusion.12), channel_id=1, source_target_pairs={{0,8},{8,0},{16,24},{24,16},{1,9},{9,1},{17,25},{25,17},{2,10},{10... | collective-permute-start | bytes 1916936 | tf_op jit(solution)/shard_map/ppermute | solution.py:66
  613.1 48.4 %collective-permute-start.111 = (f16[64,4992]{1,0:T(8,128)(2,1)}, f16[64,4992]{1,0:T(8,128)(2,1)}, u32[]{:S(2)}, u32[]{:S(2)}) collective-permute-start(f16[64,4992]{1,0:T(8,128)(2,1)} %pad_maximum_fusion.12), channel_id=1, source_target_pairs={{0,16},{8,24},{16,0},{24,8},{1,17},{9,25},{17,1},{25,9},{2,18},{10... | collective-permute-start | bytes 1916936 | tf_op jit(solution)/shard_map/ppermute | solution.py:66
  614.2 49.6 %collective-permute-start.112 = (f16[64,4992]{1,0:T(8,128)(2,1)}, f16[64,4992]{1,0:T(8,128)(2,1)}, u32[]{:S(2)}, u32[]{:S(2)}) collective-permute-start(f16[64,4992]{1,0:T(8,128)(2,1)} %pad_maximum_fusion.12), channel_id=1, source_target_pairs={{0,24},{8,16},{16,8},{24,0},{1,25},{9,17},{17,9},{25,1},{2,26},{10... | collective-permute-start | bytes 1916936 | tf_op jit(solution)/shard_map/ppermute | solution.py:66
  619.6 22.2 %collective-permute-start.99 = (f32[2]{0:T(128)S(1)}, f32[2]{0:T(128)S(1)}, u32[]{:S(2)}, u32[]{:S(2)}) collective-permute-start(f32[2]{0:T(128)S(1)} %fusion.188), channel_id=1, source_target_pairs={{0,8},{8,0},{16,24},{24,16},{1,9},{9,1},{17,25},{25,17},{2,10},{10... | collective-permute-start | bytes 32 | tf_op jit(solution)/shard_map/ppermute | solution.py:66
  (231 other events, 2045.2 us)

commit v2 on v1

--- a/solution.py
+++ b/solution.py
@@ -178,9 +178,16 @@
         attend_forward(qkv[half], context[half])
 
 
+def give(ref, parts):
+    at = 0
+    for part in parts:
+        ref[:, at : at + part.shape[1]] = part[...]
+        at += part.shape[1]
+
+
 def embed_qkv_body(
     places, vec, vectors, pix_a, pix_b, flags, ends_a, ends_b, qkv_a, qkv_b,
-    residual, low_one, out_a, out_b, ctx_a, ctx_b,
+    residual, low_one, out_a, out_b, ctx_a, ctx_b, gift,
 ):
     embedded = dot(pix_a[...], ends_a[...], 1, 1) + dot(pix_b[...], ends_b[...], 1, 1)
     embedded = embedded + vec[L + 2 : L + 3, :]
@@ -192,11 +199,12 @@
     qkv_part(
         L + 6, places, vec, vectors, residual[...], (qkv_a, qkv_b), low_one, (out_a, out_b), (ctx_a, ctx_b)
     )
+    give(gift, (low_one, ctx_b))
 
 
 def up_body(
     base, places, vec, vectors, residual, ctx_a, ctx_b, out_a, out_b, up_a, up_b,
-    mid, low_two, act_a, act_b, slope_a, slope_b,
+    mid, low_two, act_a, act_b, slope_a, slope_b, gift,
 ):
     branch = dot(ctx_a[...], out_a[...], 1, 1) + dot(ctx_b[...], out_b[...], 1, 1)
     mid[...] = residual[...] + (branch + vec[base + 4 : base + 5, :])
@@ -211,22 +219,24 @@
             phi = 0.5 * (1.0 + lax.erf(pre * math.sqrt(0.5)))
             active[:, span] = (pre * phi).astype(bf16)
             slope[:, span] = phi + pre * (jnp.exp(-0.5 * pre * pre) * (1.0 / math.sqrt(2.0 * math.pi)))
+    give(gift, (low_two, act_b))
 
 
 def down_qkv_body(
     base, places, vec, vectors, mid, act_a, act_b, down_a, down_b, qkv_a, qkv_b,
-    residual, low_one, out_a, out_b, ctx_a, ctx_b,
+    residual, low_one, out_a, out_b, ctx_a, ctx_b, gift,
 ):
     branch = dot(act_a[...], down_a[...], 1, 1) + dot(act_b[...], down_b[...], 1, 1)
     residual[...] = mid[...] + (branch + vec[base - 1 : base, :])
     qkv_part(
         base, places, vec, vectors, residual[...], (qkv_a, qkv_b), low_one, (out_a, out_b), (ctx_a, ctx_b)
     )
+    give(gift, (low_one, ctx_b))
 
 
 def down_head_body(
     base, places, vec, vectors, scale, mid, act_a, act_b, down_a, down_b, ends_a, ends_b, pix_a, pix_b, flags,
-    low_fin, pred_a, pred_b, grad_res, grad_low, wide, flat, loss,
+    low_fin, pred_a, pred_b, grad_res, grad_low, wide, flat, loss, gift,
 ):
     branch = dot(act_a[...], down_a[...], 1, 1) + dot(act_b[...], down_b[...], 1, 1)
     residual = mid[...] + (branch + vec[base + 11 : base + 12, :])
@@ -250,11 +260,12 @@
     grad_low[...] = grad.astype(bf16)
     put_rows(wide, [gain_sum, shift_sum])
     put_rows(flat, [jnp.concatenate(sums, axis=1)])
+    give(gift, (low_fin, grad_low, pred_b))
 
 
 def back_mlp_body(
     base, vec, grad_res, grad_low, down_a, down_b, slope_a, slope_b, up_a, up_b, mid,
-    grad_mid, mid_low, hid_a, hid_b, wide, flat,
+    grad_mid, mid_low, hid_a, hid_b, wide, flat, gift,
 ):
     span = vec.shape[1]
     sums = []
@@ -272,11 +283,12 @@
     mid_low[...] = grad.astype(bf16)
     put_rows(wide, [rows_sum(grad_low[...]), gain_sum, shift_sum])
     put_rows(flat, sums)
+    give(gift, (mid_low, hid_b))
 
 
 def back_attend_body(
     base, vec, grad_mid, mid_low, out_a, out_b, qkv_a, qkv_b, wqkv_a, wqkv_b, residual,
-    grad_res, grad_low, mix_a, mix_b, wide, flat, ctx,
+    grad_res, grad_low, mix_a, mix_b, wide, flat, gift, ctx,
 ):
     total = None
     query_sums, value_sums = [], []
@@ -296,6 +308,7 @@
     grad_low[...] = grad.astype(bf16)
     put_rows(wide, [rows_sum(mid_low[...]), gain_sum, shift_sum])
     put_rows(flat, [jnp.concatenate(query_sums, axis=1), jnp.concatenate(value_sums, axis=1)])
+    give(gift, (grad_low, mix_b))
 
 
 def back_embed_body(grad_res, flags, grad_low, place, wide):
@@ -366,9 +379,8 @@
     )
 
 
-def assemble_body(widths, own, stack, from_x, from_y, left, right, *outs):
+def assemble_body(widths, half, at_left, at_right, own, stack, from_x, from_y, in_y, in_x, *outs):
     part = own.shape[1]
-    half = left.shape[1]
     start = 0
     for out, width in zip(outs, widths):
         stop = start + width
@@ -380,35 +392,43 @@
                 continue
             middle = min(max(half, start), stop)
             if middle > start:
-                out[rows, : middle - start] = left[:, start:middle]
+                out[rows, : middle - start] = in_y[:, at_left + start : at_left + middle]
             if stop > middle:
-                out[rows, middle - start :] = right[:, middle - half : stop - half]
+                out[rows, middle - start :] = in_x[:, at_right + middle - half : at_right + stop - half]
         start = stop
 
 
 class Gather:
     def __init__(self, own, first, widths):
         self.own, self.first, self.widths = own, first, widths
+        self.total = sum(widths)
+        self.half = self.total // 256 * 128
         self.state = []
 
     def along(self):
         self.state = [jnp.concatenate([swap(self.first, "col", k) for k in (1, 2, 3)], axis=0)]
 
-    def across(self):
-        stack = self.state[0]
-        self.state = [stack, swap(stack, "dp", 1), swap(stack, "dp", 2)]
-
-    def diagonal(self):
-        stack, from_x, from_y = self.state
-        half = stack.shape[1] // 256 * 128
-        left = swap(from_x[:, :half], "dp", 2)
-        right = swap(from_y[:, half:], "dp", 1)
-        self.state = [stack, from_x, from_y, left, right]
+    @staticmethod
+    def across(new, old):
+        out_x, out_y = [], []
+        if new is not None:
+            out_x.append(new.state[0])
+            out_y.append(new.state[0])
+        if old is not None:
+            out_y.append(old.state[1][:, : old.half])
+            out_x.append(old.state[2][:, old.half : old.total])
+        got_x = swap(jnp.concatenate(out_x, axis=1) if len(out_x) > 1 else out_x[0], "dp", 1)
+        got_y = swap(jnp.concatenate(out_y, axis=1) if len(out_y) > 1 else out_y[0], "dp", 2)
+        if new is not None:
+            new.state += [got_x, got_y]
+        if old is not None:
+            old.at = 0 if new is None else new.total
+            old.state += [got_y, got_x]
 
     def weights(self):
         height = 16 * self.own.shape[1]
         mine = whole_call(
-            lambda *refs: assemble_body(self.widths, *refs),
+            lambda *refs: assemble_body(self.widths, self.half, self.at, self.at, *refs),
             [((height, w), bf16) for w in self.widths],
             "assemble",
             10**8,
@@ -416,14 +436,15 @@
         return [(w, swap(w, "row", 1)) for w in mine]
 
 
-DIMS = ("y", "x", "c1", "c0")
-WHERE = {"c1": ("col", 2), "c0": ("col", 1), "y": ("dp", 2), "x": ("dp", 1)}
-
-
 def row_runs(name, part):
-    block = part << (3 - DIMS.index(name))
-    count = 16 * part // block
-    return [(i * block, block) for i in range(0, count, 2)], [(i * block, block) for i in range(1, count, 2)]
+    runs = []
+    for bit in range(2):
+        rows = []
+        for other in range(2):
+            sub = 2 * other + bit if name == "x" else 2 * bit + other
+            rows += [((4 * sub + 2 * high + low) * part, part) for low in range(2) for high in range(2)]
+        runs.append(rows)
+    return runs
 
 
 def product_body(runs, left, left_got, right, right_got, keep, send, power, total):
@@ -441,18 +462,20 @@
     send[at:, :] = jnp.broadcast_to(exponent, (16, exponent.shape[1]))
 
 
-def product_sum(name, left, left_got, right, right_got, block, blocks):
+def product_sum(name, left, left_got, left_at, right, right_got, right_at, block, blocks):
     rows, height = left.shape
     width = block * len(blocks)
     first = blocks[0]
     runs = row_runs(name, height // 16)
     whole = pl.BlockSpec((rows, height), lambda i: (0, 0))
+    whole_got = pl.BlockSpec((rows, height), lambda i: (0, left_at // height))
     part = pl.BlockSpec((rows, block), lambda i: (0, i + first))
+    part_got = pl.BlockSpec((rows, block), lambda i: (0, i + first + right_at // block))
     half = pl.BlockSpec((height // 2, block), lambda i: (0, i))
     return pl.pallas_call(
         lambda *refs: product_body(runs, *refs),
         grid=(len(blocks),),
-        in_specs=[whole, whole, part, part],
+        in_specs=[whole, whole_got, part, part_got],
         out_specs=[
             half,
             pl.BlockSpec((height // 2 + 16, block), lambda i: (0, i)),
@@ -485,11 +508,6 @@
     return rows.astype(f32) * jnp.exp2(exponent - 14.0)
 
 
-def halves(rows, block):
-    shaped = rows.reshape(-1, 2, block, rows.shape[1])
-    return shaped[:, 0].reshape(-1, rows.shape[1]), shaped[:, 1].reshape(-1, rows.shape[1])
-
-
 class Reduce:
     def __init__(self, first_x, first_y):
         self.parts = []
@@ -503,24 +521,16 @@
         self.got = [swap(part[1], axis, mask) for part, (axis, mask) in zip(self.parts, ways)]
 
     def absorb(self):
-        part = self.parts[0][0].shape[0] * 2 // (16 >> self.stage)
-        if self.stage == 0:
-            blocks = (8 * part // 2, 4 * part)
-        elif self.stage == 1:
-            blocks = (part, part)
-        elif self.stage == 2:
-            blocks = (part,)
         made = []
-        for i, ((keep, _, exponent), got) in enumerate(zip(self.parts, self.got)):
+        for (keep, _, exponent), got in zip(self.parts, self.got):
             theirs = tail_of(got)
             after = jnp.maximum(exponent, theirs) + 1.0
             if self.stage == 3:
                 made.append([keep + decoded(got[:-16], theirs), None, after])
                 continue
-            stay, leave = halves(keep, blocks[i])
-            got_stay, got_leave = halves(got[:-16], blocks[i])
-            stay = stay + decoded(got_stay, theirs)
-            leave = leave + decoded(got_leave, theirs)
+            half = keep.shape[0] // 2
+            stay = keep[:half] + decoded(got[:half], theirs)
+            leave = keep[half:] + decoded(got[half : 2 * half], theirs)
             made.append([stay, leave, after])
         if self.stage == 1:
             made = [[jnp.concatenate(list(p), axis=1) for p in zip(*made)]]
@@ -536,6 +546,16 @@
         self.keep, self.exponent = keep, after
 
 
+def split(value):
+    high = value.astype(bf16)
+    return high, (value - high.astype(f32)).astype(bf16)
+
+
+def close(lhs, rhs, lhs_dim, rhs_dim):
+    small = dot(lhs[0], rhs[1], lhs_dim, rhs_dim) + dot(lhs[1], rhs[0], lhs_dim, rhs_dim)
+    return dot(lhs[0], rhs[0], lhs_dim, rhs_dim) + small
+
+
 def shampoo_body(
     group, layout, info, weight, *rest
 ):
@@ -562,9 +582,11 @@
         g = block_of(grads, slot)
         grad_out[j] = g
         weight_out[j] = block_of(weight, slot)
-        left[j] = exact(g, g, 1, 1)
-        right[j] = exact(g, g, 0, 0)
-        precond[j] = exact(rl[j], exact(g, rr[j], 1, 0), 1, 0)
+        both = split(g)
+        left[j] = close(both, both, 1, 1)
+        right[j] = close(both, both, 0, 0)
+        inner = close(both, split(rr[j]), 1, 0)
+        precond[j] = close(split(rl[j]), split(inner), 1, 0)
 
 
 def shampoo(info, weight, pieces, layout, root_left, root_right):
@@ -655,10 +677,13 @@
         plan.append((name, i, at, sizes[name]))
         at += sizes[name]
     start_of = {entry[:2]: entry[2] for entry in plan}
-    cuts = [0]
+    stage_cuts = [0]
     for i in range(layer_count):
-        cuts += [2 + 4 * i, 4 + 4 * i]
-    cuts.append(len(plan))
+        stage_cuts += [2 + 4 * i, 4 + 4 * i]
+    stage_cuts.append(len(plan))
+    last = len(stage_cuts) - 1
+    stages_of = [[0, 1]] + [[k] for k in range(2, last - 2)] + [[last - 2, last - 1]]
+    cuts = [stage_cuts[stages[0]] for stages in stages_of] + [len(plan)]
     tiles_own, owns, firsts = prepare_tiles(
         plan, cuts, places, weight_qkv, weight_out, weight_up, weight_down, weight_ends
     )
@@ -703,11 +728,36 @@
     flags = jnp.stack([c.astype(f32).reshape(-1) for c in columns] + [jnp.zeros((images * LP,), f32)] * 3, axis=1)
     tokens = images * LP
 
+    per_owner = owner_map.shape[1] // data_count
+    slots = lax.dynamic_slice_in_dim(owner_map[0], data_index * per_owner, per_owner)
+    edge = part * 4 // BLK
+    firsts_of, kinds = [], []
+    at = 0
+    for i in range(layer_count):
+        for name in ("qkv", "out", "up", "down"):
+            firsts_of.append(at)
+            kinds.append((start_of[name, i], sizes[name] // BLK, name in ("out", "down")))
+            at += edge * sizes[name] // BLK
+    top = jnp.zeros_like(slots)
+    left_at = jnp.zeros_like(slots)
+    turned = jnp.zeros_like(slots)
+    for begin, (start, across, is_turned) in zip(firsts_of, kinds):
+        inside = slots >= begin
+        local = slots - begin
+        top = jnp.where(inside, local % edge if is_turned else local // across, top)
+        left_at = jnp.where(inside, start + BLK * (local // edge if is_turned else local % across), left_at)
+        turned = jnp.where(inside, int(is_turned), turned)
+    upper = (2 * top) ^ sub_index
+    shift = left_at % 128
+    info = jnp.stack([upper, (2 * top + 1) ^ sub_index, left_at // 128, (256 - shift) % 256, turned]).astype(jnp.int32)
+
     def activations(*widths):
         return [((tokens, w), bf16) for w in widths]
 
     weights, values = {}, {}
-    qkv_outs = [((tokens, width), f32)] + activations(width, *[sizes["qkv"]] * 2, *[sizes["out"]] * 2)
+    qkv_outs = [((tokens, width), f32)] + activations(
+        width, *[sizes["qkv"]] * 2, *[sizes["out"]] * 2, width + sizes["out"]
+    )
     full = 2 * tokens * width
     loss_scale = 1.0 / (PATCH * count_all)
 
@@ -717,12 +767,10 @@
     def keep_qkv(i, got):
         values["residual", i], values["low_one", i] = got[0], got[1]
         values["qkv", i], values["context", i] = got[2:4], got[4:6]
-        values["got_one", i], values["got_context", i] = across_core(got[1]), across_core(got[5])
-
-    def forward_stage(index, pairs):
+        values["got_qkv", i] = across_core(got[6])
+
+    def forward_stage(index):
         layer, odd = divmod(index, 2)
-        for entry, pair in zip(plan[cuts[index] : cuts[index + 1]], pairs):
-            weights[entry[:2]] = pair
         base = L + 6 + 12 * layer
         if index == 0:
             got = whole_call_smem(
@@ -731,7 +779,7 @@
             keep_qkv(0, got)
         elif odd:
             outs = [((tokens, width), f32)] + activations(width, *[sizes["up"]] * 2)
-            outs += [((tokens, sizes["up"]), f32)] * 2
+            outs += [((tokens, sizes["up"]), f32)] * 2 + activations(width + sizes["up"])
             got = whole_call_smem(
                 lambda *refs: up_body(base, *refs), 1, 9, outs, "out_up", full * 5 * width
             )(
@@ -740,7 +788,7 @@
             )
             values["mid", layer], values["low_two", layer] = got[0], got[1]
             values["active", layer], values["slope", layer] = got[2:4], got[4:6]
-            values["got_two", layer], values["got_active", layer] = across_core(got[1]), across_core(got[3])
+            values["got_up", layer] = across_core(got[6])
         elif layer < layer_count:
             got = whole_call_smem(
                 lambda *refs: down_qkv_body(base, *refs), 1, 9, qkv_outs, "down_qkv", full * 7 * width
@@ -752,6 +800,7 @@
         else:
             outs = activations(width, *[sizes["ends"]] * 2) + [((tokens, width), f32)] + activations(width)
             outs += [((8, width), f32), ((8, width), f32), ((8, 128), f32)]
+            outs += activations(2 * width + sizes["ends"])
             got = whole_call_smem(
                 lambda *refs: down_head_body(base - 12, refs[0], refs[2], refs[3], refs[1], *refs[4:]),
                 2, 12, outs, "down_head", full * 6 * width,
@@ -762,25 +811,32 @@
             )
             values["low_fin"], values["pred"] = got[0], got[1:3]
             values["grad_res"], values["grad_low"] = got[3], got[4]
-            values["wide", "head"], values["flat", "head"], values["loss"] = got[5:]
-            values["got_fin"], values["got_pred"] = across_core(got[0]), across_core(got[2])
-            values["got_low"] = across_core(got[4])
+            values["wide", "head"], values["flat", "head"], values["loss"] = got[5:8]
+            values["got_head"] = across_core(got[8])
 
     count = len(chunks)
     for step in range(count + 3):
         begun = list(values)
         if step < count:
             chunks[step].along()
-        if 0 <= step - 1 < count:
-            chunks[step - 1].across()
-        if 0 <= step - 2 < count:
-            chunks[step - 2].diagonal()
+        new = chunks[step - 1] if 0 <= step - 1 < count else None
+        old = chunks[step - 2] if 0 <= step - 2 < count else None
+        if new is not None or old is not None:
+            Gather.across(new, old)
         if 0 <= step - 3 < count:
-            forward_stage(step - 3, chunks[step - 3].weights())
+            pairs = chunks[step - 3].weights()
+            for entry, pair in zip(plan[cuts[step - 3] : cuts[step - 2]], pairs):
+                weights[entry[:2]] = pair
+            for stage in stages_of[step - 3]:
+                forward_stage(stage)
         if step == count + 2:
             break
         moving = chunks[max(0, step - 2) : step + 1]
         later = chunks[step + 1 :]
+        if step == 0:
+            setup = (vec, flags, pix_half, pix_other, loss_scale, info, turn)
+            chunks[0].state, setup = tie(chunks[0].state, setup)
+            vec, flags, pix_half, pix_other, loss_scale, info, turn = setup
         keys = [k for k in values if k in begun or not (isinstance(k, tuple) and k[0][:3] == "got")]
         states, waiting, kept = tie(
             [c.state for c in moving], [c.first for c in later], [values[k] for k in keys]
@@ -793,89 +849,114 @@
 
     flying, done = [], []
 
+    spreads, groups = [], []
+    ready = 0
+
+    def spread(members):
+        value = jnp.concatenate([g.keep for g in members], axis=1)
+        exponent = jnp.concatenate([g.exponent for g in members], axis=1)
+        payload = lowered(value, exponent)
+        return [payload] + [swap(payload, "dp", k) for k in (1, 2, 3)]
+
     def step_on(value, fresh):
-        value, landed, ready = tie(value, [r.got for r in flying], [r.parts for r in fresh])
+        nonlocal ready
+        value, landed, parts_in = tie(value, [r.got for r in flying], [r.parts for r in fresh])
         for r, got in zip(flying, landed):
             r.got = got
             r.absorb()
-        for r, parts in zip(fresh, ready):
+        for r, parts in zip(fresh, parts_in):
             r.parts = parts
         done.extend(r for r in flying if r.stage == 4)
         flying[:] = [r for r in flying if r.stage < 4] + list(fresh)
         for r in flying:
             r.send()
+        stop = sum(1 for g, _ in groups if g.stage == 4)
+        if stop > ready and len(groups) == 2 * layer_count:
+            spreads.append([spread([g for g, _ in groups[ready:stop]]), groups[ready:stop]])
+            ready = stop
         return value
 
     wides = {"head": values["wide", "head"]}
     flats = {"head": values["flat", "head"]}
-    grad_res, grad_low, got_low = values["grad_res"], values["grad_low"], values["got_low"]
+    grad_res, grad_low = values["grad_res"], values["grad_low"]
+    got_low, low_at = values["got_head"], width
     small = sizes["out"]
     blocks_of = {name: range(sizes[name] // small) for name in sizes}
     big = 2 * small
-    groups = []
-
-    def product(way, left, left_got, right, right_got, name, part=None):
+
+    def product(way, left, left_got, left_at, right, right_got, right_at, name, part=None):
         blocks = list(part if part is not None else blocks_of[name])
         block = small
-        if len(blocks) % 2 == 0 and blocks[0] % 2 == 0:
+        if len(blocks) % 2 == 0 and blocks[0] % 2 == 0 and right_at % big == 0:
             block, blocks = big, list(range(blocks[0] // 2, blocks[0] // 2 + len(blocks) // 2))
-        return product_sum(way, left, left_got, right, right_got, block, blocks)
+        return product_sum(way, left, left_got, left_at, right, right_got, right_at, block, blocks)
 
     for i in reversed(range(layer_count)):
         base = L + 6 + 12 * i
         outs = [((tokens, width), f32)] + activations(width, *[sizes["up"]] * 2) + [((8, width), f32)] * 2
-        grad_mid, mid_low, hid_a, hid_b, wides["mlp", i], flats["mlp", i] = whole_call(
-            lambda *refs: back_mlp_body(base, *refs), outs, "back_mlp", full * 8 * width
-        )(
+        outs += activations(width + sizes["up"])
+        got = whole_call(lambda *refs: back_mlp_body(base, *refs), outs, "back_mlp", full * 8 * width)(
             vec, grad_res, grad_low, *weights["down", i], *values["slope", i], *weights["up", i],
             values["mid", i],
         )
-        got_mid, got_hid = across_core(mid_low), across_core(hid_b)
+        got, got_low = step_on((got, got_low), [])
+        grad_mid, mid_low, hid_a, hid_b, wides["mlp", i], flats["mlp", i], gift = got
+        got_mid = across_core(gift)
         active = values["active", i]
-        first_x = [product("x", grad_low, got_low, active[0], values["got_active", i], "down")]
+        first_x = [product("x", grad_low, got_low, low_at, active[0], values["got_up", i], width, "down")]
         names_x = [("down", i)]
         if i == layer_count - 1:
+            head = values["got_head"]
             first_x.append(
-                product("x", values["low_fin"], values["got_fin"], values["pred"][0], values["got_pred"], "ends")
+                product("x", values["low_fin"], head, 0, values["pred"][0], head, 2 * width, "ends")
             )
             names_x.append(("ends", 1))
-        first_y = [product("y", values["low_two", i], values["got_two", i], hid_a, got_hid, "up")]
+        first_y = [product("y", values["low_two", i], values["got_up", i], 0, hid_a, got_mid, width, "up")]
         group = Reduce(first_x, first_y)
         groups.append((group, names_x + [("up", i)]))
         grad_mid, mid_low, got_mid = step_on((grad_mid, mid_low, got_mid), [group])
         outs = [((tokens, width), f32)] + activations(width, *[sizes["qkv"]] * 2) + [((8, width), f32)] * 2
-        grad_res, grad_low, mix_a, mix_b, wides["mix", i], flats["mix", i] = whole_call(
+        outs += activations(width + sizes["qkv"])
+        got = whole_call(
             lambda *refs: back_attend_body(base, *refs), outs, "back_attend", full * 8 * width,
             [pltpu.VMEM((tokens, sizes["out"]), f32)],
         )(
             vec, grad_mid, mid_low, *weights["out", i], *values["qkv", i], *weights["qkv", i],
             values["residual", i],
         )
-        got_mix = across_core(mix_b)
+        got = step_on(got, [])
+        grad_res, grad_low, mix_a, mix_b, wides["mix", i], flats["mix", i], gift = got
+        got_low, low_at = across_core(gift), 0
+        low_one, got_qkv = values["low_one", i], values["got_qkv", i]
+        out_args = (mid_low, got_mid, 0, values["context", i][0], got_qkv, width, "out")
+        mix_args = (low_one, got_qkv, 0, mix_a, got_low, width, "qkv")
         if i > 0:
-            got_low = across_core(grad_low)
+            first_x = [product("x", *mix_args, range(0, 2))]
+            first_y = [product("y", *mix_args, range(2, 3)), product("y", *out_args)]
+            group_names = [("qkv", i), ("out", i)]
         else:
             outs = activations(width) + [((LP, width), f32), ((8, width), f32)]
             embed_low, place_sum, wides["embed"] = whole_call(back_embed_body, outs, "back_embed", full)(
                 grad_res, flags
             )
             got_embed = across_core(embed_low)
-        low_one, got_one = values["low_one", i], values["got_one", i]
-        out_args = (mid_low, got_mid, values["context", i][0], values["got_context", i], "out")
-        if i > 0:
-            first_x = [product("x", low_one, got_one, mix_a, got_mix, "qkv", range(0, 2))]
-            first_y = [product("y", low_one, got_one, mix_a, got_mix, "qkv", range(2, 3)), product("y", *out_args)]
-            group_names = [("qkv", i), ("out", i)]
-        else:
-            first_x = [product("x", low_one, got_one, mix_a, got_mix, "qkv")]
+            first_x = [product("x", *mix_args)]
             first_y = [
                 product("y", *out_args),
-                product("y", embed_low, got_embed, pix_half[0], pix_other, "ends"),
+                product("y", embed_low, got_embed, 0, pix_half[0], pix_other, 0, "ends"),
             ]
             group_names = [("qkv", i), ("out", i), ("ends", 0)]
         group = Reduce(first_x, first_y)
         groups.append((group, group_names))
-        grad_res, grad_low, got_low = step_on((grad_res, grad_low, got_low), [group])
+        if i > 0:
+            grad_res, grad_low, got_low = step_on((grad_res, grad_low, got_low), [group])
+        else:
+            wide_keys, flat_keys = list(wides), list(flats)
+            place_sum, wide_rows, flat_rows = step_on(
+                (place_sum, [wides[k] for k in wide_keys], [flats[k] for k in flat_keys]), [group]
+            )
+            wides.update(zip(wide_keys, wide_rows))
+            flats.update(zip(flat_keys, flat_rows))
 
     raw_wide = [place_sum, wides["embed"], wides["head"]]
     raw_flat = [flats["head"]]
@@ -906,55 +987,36 @@
     def rows_at(value, index, size):
         return lax.dynamic_slice_in_dim(value, index * size, size)
 
-    half_rows, sub_rows, end_rows = rows_all // 2, rows_all // 8, rows_all // 32
+    half_rows, sub_rows = rows_all // 2, rows_all // 8
     value = rows_at(grad_vec, row_index, half_rows) + across_core(rows_at(grad_vec, 1 - row_index, half_rows))
+    value = step_on(value, [])
     value = rows_at(value, sub_index, sub_rows) + sum(
         swap(rows_at(value, sub_index ^ k, sub_rows), "dp", k) for k in (1, 2, 3)
     )
-    value = rows_at(value, col_index, end_rows) + sum(
-        swap(rows_at(value, col_index ^ k, end_rows), "col", k) for k in (1, 2, 3)
-    )
+    value = step_on(value, [])
+    value = butterfly(value, ("col",))
     for mask in bits_of("dp")[2:]:
         value = value + swap(value, "dp", mask)
-    vec_square = jnp.sum(value * value)
-    value = jnp.concatenate([value] + [swap(value, "col", k) for k in (1, 2, 3)], axis=0)
+    while flying:
+        value = step_on(value, [])
+    copies = max(1, data_count // 4)
+    square = sum(jnp.sum(g.keep * g.keep) for g, _ in groups)
+    square = (square + jnp.sum(value * value) / lax.axis_size("col")) / copies
+    pair = butterfly(jnp.stack([square, values["loss"][0, 0]]), ("row", "dp"))
     value = jnp.concatenate([value] + [swap(value, "dp", k) for k in (1, 2, 3)], axis=0)
     value = jnp.concatenate([value, across_core(value)], axis=0)
+    pair, value, payloads = tie(pair, value, [payloads for payloads, _ in spreads])
+    for entry, got in zip(spreads, payloads):
+        entry[0] = got
     spot = jnp.arange(rows_all)
     native = (
         ((spot // half_rows) ^ row_index) * half_rows
         + (((spot // sub_rows) & 3) ^ sub_index) * sub_rows
-        + (((spot // end_rows) & 3) ^ col_index) * end_rows
-        + spot % end_rows
+        + spot % sub_rows
     )
     pick = (jnp.arange(vectors.shape[0])[:, None] == native[None, :]).astype(f32)
     vec_sum = exact(pick, value, 1, 0)
-
-    def spread(members):
-        value = jnp.concatenate([g.keep for g in members], axis=1)
-        exponent = jnp.concatenate([g.exponent for g in members], axis=1)
-        payload = lowered(value, exponent)
-        return [payload] + [swap(payload, "dp", k) for k in (1, 2, 3)]
-
-    spreads = []
-    ready = 0
-
-    def spread_ready(size):
-        nonlocal ready
-        spreads.append((spread([g for g, _ in groups[ready : ready + size]]), groups[ready : ready + size]))
-        ready += size
-
-    marker = grad_res
-    while flying:
-        marker = step_on(marker, [])
-        finished = sum(1 for g, _ in groups if g.stage == 4)
-        if ready == 0 and finished >= 2:
-            spread_ready(2)
-    spread_ready(len(groups) - ready)
-    axes = ("row", "dp", "col")
-    copies = max(1, data_count // 4)
-    square = sum(jnp.sum(g.keep * g.keep) for g, _ in groups) + vec_square
-    pair = butterfly(jnp.stack([square / copies, values["loss"][0, 0]]), axes)
+    pair = butterfly(pair, ("col",))
     loss_total = pair[1]
     grad_norm = jnp.sqrt(pair[0])
     factor = jnp.minimum(1.0, clip_scale / math.sqrt(total_tokens) / grad_norm)
@@ -972,28 +1034,6 @@
         for k, payload in enumerate(payloads):
             pieces.append(decoded(payload[:-16], tail_of(payload)))
             layout.append((k, spans))
-    per_owner = owner_map.shape[1] // data_count
-    slots = lax.dynamic_slice_in_dim(owner_map[0], data_index * per_owner, per_owner)
-    edge = part * 4 // BLK
-    firsts_of, kinds = [], []
-    at = 0
-    for i in range(layer_count):
-        for name in ("qkv", "out", "up", "down"):
-            firsts_of.append(at)
-            kinds.append((start_of[name, i], sizes[name] // BLK, name in ("out", "down")))
-            at += edge * sizes[name] // BLK
-    top = jnp.zeros_like(slots)
-    left_at = jnp.zeros_like(slots)
-    turned = jnp.zeros_like(slots)
-    for begin, (start, across, is_turned) in zip(firsts_of, kinds):
-        inside = slots >= begin
-        local = slots - begin
-        top = jnp.where(inside, local % edge if is_turned else local // across, top)
-        left_at = jnp.where(inside, start + BLK * (local // edge if is_turned else local % across), left_at)
-        turned = jnp.where(inside, int(is_turned), turned)
-    upper = (2 * top) ^ sub_index
-    shift = left_at % 128
-    info = jnp.stack([upper, (2 * top + 1) ^ sub_index, left_at // 128, (256 - shift) % 256, turned]).astype(jnp.int32)
     raw_grad, raw_left, raw_right, raw_precond, own_weight = shampoo(
         info, tiles_own, pieces, layout, root_left[0], root_right[0]
     )

time: 720 us -> 636 us (0.88)
  waiting for transfers between devices: 228 us -> 171 us
  local copies, waits for them, and re-layouts: 74.1 us -> 43.1 us
  other arithmetic: 74.4 us -> 97.4 us
  starting transfers between devices: 103 us -> 88.1 us
    ppermute x116 -> x88, waiting for transfers between devices: 228 us -> 171 us  [swap(): return lax.ppermute(value, axis, [(i, i ^ mask) for i in range(size)])]
    slice x70 -> x8, local copies, waits for them, and re-layouts: 24.1 us -> 2.8 us  [the longest x3 1.16 us: across(): out_x.append(old.state[2][:, old.half:old.total])]
    add x24 -> x16, other arithmetic: 3.14 us -> 20.4 us  [absorb(): stay = keep[:half] + decoded(got[:half], theirs)]
    ppermute x116 -> x88, starting transfers between devices: 103 us -> 88.1 us  [swap(): return lax.ppermute(value, axis, [(i, i ^ mask) for i in range(size)])]
    unnamed x332 -> x292, local copies, waits for them, and re-layouts: 34.1 us -> 31.7 us
    reduce_max x32 -> x36, other arithmetic: 12.8 us -> 14.5 us  [tail_of(): return jnp.max(payload[-16:].astype(f32), axis=0, keepdims=True)]
    pallas_call x5 -> x3, Pallas kernels: 17 us -> 15.3 us  [weights(): whole_call(lambda *refs: assemble_body(self.widths, self.half, self.at, s...]
  transfers between devices with their start and end apart: 116 -> 88, of which waited for: 51 -> 30; matrix products, arithmetic and copies ran while one was open for 13% -> 14% of each run, Pallas kernels for 21% -> 27%
where the time goes in v2:
time: 636 us; the launch traced here: 625 us
  Pallas kernels  206 us (32%)
  waiting for transfers between devices  171 us (27%)
  other arithmetic  97.4 us (15%)
  starting transfers between devices  88.1 us (14%)
  local copies, waits for them, and re-layouts  43.1 us (7%)
  between operations  11.4 us (2%)
  matrix products  7.64 us (1%)
    ppermute x88, waiting for transfers between devices, swap(): return lax.ppermute(value, axis, [(i, i ^ mask) for i in range(size)])  171 us
    ppermute x88, starting transfers between devices, swap(): return lax.ppermute(value, axis, [(i, i ^ mask) for i in range(size)])  88.1 us
    pallas_call x2, Pallas kernels, shards(): whole_call(lambda *refs: back_attend_body(base, *refs), outs, 'back_atten...  44.1 us
    unnamed x292, local copies, waits for them, and re-layouts  31.7 us
    pallas_call x11, Pallas kernels, product_sum(): pl.pallas_call(lambda *refs: product_body(runs, *refs), grid=(len(blocks)...  29 us
    pallas_call x2, Pallas kernels, shards(): whole_call(lambda *refs: back_mlp_body(base, *refs), outs, 'back_mlp', fu...  26.5 us
    pallas_call x2, Pallas kernels, forward_stage(): whole_call_smem(lambda *refs: up_body(base, *refs), 1, 9, outs, 'out_up',...  23.1 us
    add x16, other arithmetic, absorb(): stay = keep[:half] + decoded(got[:half], theirs)  20.4 us
  transfers between devices with their start and end apart: 88, of which 30 were waited for; matrix products, arithmetic and copies ran while one was open for 14% of the time, Pallas kernels for 27%

profile of v2, /device:TPU:0, one launch (start us, length us, event | category | flops | bytes accessed | tf_op | source)
XLA Modules:
  0.0 624.8 jit_solution(16388200910082939801)
XLA Ops:
  1.8 2.6 copy.55.refs_4_
  4.6 6.2 prepare_tiles.1
  10.8 5.0 collective-permute-start.2
  16.5 3.2 constant_dynamic-slice_fusion.5
  30.0 2.9 collective-permute-start.5
  35.5 8.8 %collective-permute-done.1 = bf16[48,3456]{1,0:T(8,128)(2,1)} collective-permute-done((bf16[48,3456]{1,0:T(8,128)(2,1)S(1)}, bf16[48,3456]{1,0:T(8,128)(2,1)}, u32[]{:S(2)}, u32[]{:S(2)}) %collective-permute-start.1) | collective-permute-done | bytes 331808 | tf_op jit(solution)/shard_map/ppermute | solution.py:66
  53.0 6.7 %collective-permute-done.10 = bf16[48,2688]{1,0:T(8,128)(2,1)S(1)} collective-permute-done((bf16[48,2688]{1,0:T(8,128)(2,1)S(1)}, bf16[48,2688]{1,0:T(8,128)(2,1)S(1)}, u32[]{:S(2)}, u32[]{:S(2)}) %collective-permute-start.10) | collective-permute-done | bytes 258080 | tf_op jit(solution)/shard_map/ppermute | solution.py:66
  59.7 11.1 %collective-permute-done.9 = bf16[48,2688]{1,0:T(8,128)(2,1)S(1)} collective-permute-done((bf16[48,2688]{1,0:T(8,128)(2,1)S(1)}, bf16[48,2688]{1,0:T(8,128)(2,1)S(1)}, u32[]{:S(2)}, u32[]{:S(2)}) %collective-permute-start.9) | collective-permute-done | bytes 258080 | tf_op jit(solution)/shard_map/ppermute | solution.py:66
  77.7 9.0 %collective-permute-done.15 = bf16[48,3840]{1,0:T(8,128)(2,1)S(1)} collective-permute-done((bf16[48,3840]{1,0:T(8,128)(2,1)S(1)}, bf16[48,3840]{1,0:T(8,128)(2,1)S(1)}, u32[]{:S(2)}, u32[]{:S(2)}) %collective-permute-start.15) | collective-permute-done | bytes 368672 | tf_op jit(solution)/shard_map/ppermute | solution.py:66
  86.7 16.9 %collective-permute-done.14 = bf16[48,3840]{1,0:T(8,128)(2,1)S(1)} collective-permute-done((bf16[48,3840]{1,0:T(8,128)(2,1)S(1)}, bf16[48,3840]{1,0:T(8,128)(2,1)S(1)}, u32[]{:S(2)}, u32[]{:S(2)}) %collective-permute-start.14) | collective-permute-done | bytes 368672 | tf_op jit(solution)/shard_map/ppermute | solution.py:66
  105.6 5.1 assemble.3
  119.8 13.3 %embed_qkv.1 = (f32[416,768]{1,0:T(8,128)}, bf16[416,768]{1,0:T(8,128)(2,1)}, bf16[416,1152]{1,0:T(8,128)(2,1)}, bf16[416,1152]{1,0:T(8,128)(2,1)}, bf16[416,384...) custom-call(s32[2]{0:T(128)S(1)} %pad_add_fusion.refs_0_.places, ...), custom_call_target="tpu_custom_call" | custom-call | flops 122683392 | bytes 65536 | tf_op jit(solution)/shard_map/embed_qkv/pallas_call | solution.py:776
  133.2 11.8 %out_up.2 = (f32[416,768]{1,0:T(8,128)}, bf16[416,768]{1,0:T(8,128)(2,1)}, bf16[416,1536]{1,0:T(8,128)(2,1)}, bf16[416,1536]{1,0:T(8,128)(2,1)}, f32[416,1536]{1...) custom-call(s32[2]{0:T(128)S(1)} %pad_add_fusion.refs_0_.places, ...), custom_call_target="tpu_custom_call" | custom-call | flops 153354240 | bytes 65536 | tf_op jit(solution)/shard_map/out_up/pallas_call | solution.py:783
  144.9 4.8 collective-permute-done.16.refs_4_.refs_3_
  149.8 4.8 assemble.4
  164.5 14.8 %down_qkv.1 = (f32[416,768]{1,0:T(8,128)}, bf16[416,768]{1,0:T(8,128)(2,1)S(1)}, bf16[416,1152]{1,0:T(8,128)(2,1)}, bf16[416,1152]{1,0:T(8,128)(2,1)}, bf16[416,...) custom-call(s32[2]{0:T(128)S(1)} %pad_add_fusion.refs_0_.places, ...), custom_call_target="tpu_custom_call" | custom-call | flops 214695936 | bytes 65536 | tf_op jit(solution)/shard_map/down_qkv/pallas_call | solution.py:793
  179.3 5.5 assemble.5
  185.8 7.8 %collective-permute-done.28.refs_7_.refs_4_ = bf16[768,384]{1,0:T(8,128)(2,1)S(1)} collective-permute-done((bf16[768,384]{1,0:T(8,128)(2,1)S(1)}, bf16[768,384]{1,0:T(8,128)(2,1)S(1)}, u32[]{:S(2)}, u32[]{:S(2)}) %collective-permute-start.28) | collective-permute-done | bytes 589856 | tf_op jit(solution)/shard_map/ppermute | solution.py:66
  195.1 11.3 %out_up.3 = (f32[416,768]{1,0:T(8,128)}, bf16[416,768]{1,0:T(8,128)(2,1)}, bf16[416,1536]{1,0:T(8,128)(2,1)}, bf16[416,1536]{1,0:T(8,128)(2,1)}, f32[416,1536]{1...) custom-call(s32[2]{0:T(128)S(1)} %pad_add_fusion.refs_0_.places, ...), custom_call_target="tpu_custom_call" | custom-call | flops 153354240 | bytes 65536 | tf_op jit(solution)/shard_map/out_up/pallas_call | solution.py:783
  207.3 12.0 %down_head.1 = (bf16[416,768]{1,0:T(8,128)(2,1)}, bf16[416,384]{1,0:T(8,128)(2,1)S(1)}, bf16[416,384]{1,0:T(8,128)(2,1)}, f32[416,768]{1,0:T(8,128)}, bf16[416,7...) custom-call(s32[2]{0:T(128)S(1)} %pad_add_fusion.refs_0_.places, ...), custom_call_target="tpu_custom_call" | custom-call | flops 184025088 | bytes 65536 | tf_op jit(solution)/shard_map/down_head/pallas_call | solution.py:804
  222.2 13.2 %back_mlp.2 = (f32[416,768]{1,0:T(8,128)}, bf16[416,768]{1,0:T(8,128)(2,1)S(1)}, bf16[416,1536]{1,0:T(8,128)(2,1)}, bf16[416,1536]{1,0:T(8,128)(2,1)}, f32[8,768...) custom-call(f32[227,768]{1,0:T(8,128)} %fusion.5.vec.refs_1_.refs_2_.refs_0_, ...), custom_call_target="tpu_custom_call" | custom-call | flops 245366784 | bytes 65536 | tf_op jit(solution)/shard_map/back_mlp/pallas_call | solution.py:898
  236.9 3.7 product_sum.11
  244.7 3.9 product_sum.13
  253.1 21.6 %back_attend.2 = (f32[416,768]{1,0:T(8,128)}, bf16[416,768]{1,0:T(8,128)(2,1)S(1)}, bf16[416,1152]{1,0:T(8,128)(2,1)}, bf16[416,1152]{1,0:T(8,128)(2,1)}, f32[8,...) custom-call(f32[227,768]{1,0:T(8,128)} %fusion.5.vec.refs_1_.refs_2_.refs_0_, ...), custom_call_target="tpu_custom_call" | custom-call | flops 245366784 | bytes 65536 | tf_op jit(solution)/shard_map/back_attend/pallas_call | solution.py:920
  274.6 6.0 collective-permute-done.36
  280.6 5.5 collective-permute-done.35
  287.2 2.8 multiply_add_fusion
  304.3 6.0 collective-permute-done.39
  317.3 13.3 %back_mlp.3 = (f32[416,768]{1,0:T(8,128)}, bf16[416,768]{1,0:T(8,128)(2,1)S(1)}, bf16[416,1536]{1,0:T(8,128)(2,1)}, bf16[416,1536]{1,0:T(8,128)(2,1)}, f32[8,768...) custom-call(f32[227,768]{1,0:T(8,128)} %fusion.5.vec.refs_1_.refs_2_.refs_0_, ...), custom_call_target="tpu_custom_call" | custom-call | flops 245366784 | bytes 65536 | tf_op jit(solution)/shard_map/back_mlp/pallas_call | solution.py:898
  353.0 3.7 product_sum.17
  358.6 4.8 product_sum.18
  374.8 22.5 %back_attend.3 = (f32[416,768]{1,0:T(8,128)}, bf16[416,768]{1,0:T(8,128)(2,1)}, bf16[416,1152]{1,0:T(8,128)(2,1)}, bf16[416,1152]{1,0:T(8,128)(2,1)}, f32[8,768]...) custom-call(f32[227,768]{1,0:T(8,128)} %fusion.5.vec.refs_1_.refs_2_.refs_0_, ...), custom_call_target="tpu_custom_call" | custom-call | flops 245366784 | bytes 65536 | tf_op jit(solution)/shard_map/back_attend/pallas_call | solution.py:920
  397.4 2.8 multiply_reduce_fusion
  415.6 4.2 product_sum.19
  420.0 3.1 collective-permute-done.51
  423.0 3.0 collective-permute-done.53
  436.1 14.6 %collective-permute-done.59 = f16[400,768]{1,0:T(8,128)(2,1)S(1)} collective-permute-done((f16[400,768]{1,0:T(8,128)(2,1)S(1)}, f16[400,768]{1,0:T(8,128)(2,1)S(1)}, u32[]{:S(2)}, u32[]{:S(2)}) %collective-permute-start.59) | collective-permute-done | bytes 614432 | tf_op jit(solution)/shard_map/ppermute | solution.py:66
  450.7 6.1 collective-permute-done.58
  473.1 4.9 collective-permute-done.65
  492.1 7.7 %collective-permute-done.67 = f32[32,768]{1,0:T(8,128)S(1)} collective-permute-done((f32[32,768]{1,0:T(8,128)S(1)}, f32[32,768]{1,0:T(8,128)S(1)}, u32[]{:S(2)}, u32[]{:S(2)}) %collective-permute-start.67) | collective-permute-done | bytes 98336 | tf_op jit(solution)/shard_map/ppermute | solution.py:66
  502.6 2.6 collective-permute-start.69
  505.3 10.4 %collective-permute-done.69 = f16[64,1920]{1,0:T(8,128)(2,1)S(1)} collective-permute-done((f16[64,1920]{1,0:T(8,128)(2,1)S(1)}, f16[64,1920]{1,0:T(8,128)(2,1)S(1)}, u32[]{:S(2)}, u32[]{:S(2)}) %collective-permute-start.69) | collective-permute-done | bytes 245792 | tf_op jit(solution)/shard_map/ppermute | solution.py:66
  547.7 16.4 %collective-permute-done.81 = f16[64,3072]{1,0:T(8,128)(2,1)S(1)} collective-permute-done((f16[64,3072]{1,0:T(8,128)(2,1)S(1)}, f16[64,3072]{1,0:T(8,128)(2,1)S(1)}, u32[]{:S(2)}, u32[]{:S(2)}) %collective-permute-start.81) | collective-permute-done | bytes 393248 | tf_op jit(solution)/shard_map/ppermute | solution.py:66
  564.1 4.9 collective-permute-done.84
  581.3 19.3 %shampoo.1 = (f32[48,96,96]{2,1,0:T(8,128)}, f32[48,96,96]{2,1,0:T(8,128)}, f32[48,96,96]{2,1,0:T(8,128)}, f32[48,96,96]{2,1,0:T(8,128)}, f32[48,96,96]{2,1,0:T(8,128)}) custom-call(s32[5,48]{1,0:T(8,128)S(1)} %stack.34.refs_0_, bf16[4,48,9984]{2,1,0:T(8,128)(2,1)} %get-tuple-element.596.refs_1_, f32[48,4992]{1,0:T(8,128)} %copy-done.72, ...), custom_call_target="tpu_custom_call" | custom-call | flops 127401984 | bytes 65536 | tf_op jit(solution)/shard_map/shampoo/pallas_call | solution.py:596
  600.6 3.0 collective-permute-start.87
  606.4 3.4 multiply_bitcast_fusion
  609.8 3.7 fusion.1
  (749 shorter events, 233.0 us)
Async XLA Ops:
  10.8 24.6 %collective-permute-start.2 = (bf16[48,3456]{1,0:T(8,128)(2,1)S(1)}, bf16[48,3456]{1,0:T(8,128)(2,1)}, u32[]{:S(2)}, u32[]{:S(2)}) collective-permute-start(bf16[48,3456]{1,0:T(8,128)(2,1)S(1)} %get-tuple-element.309), channel_id=1, source_target_pairs={{0,3},{1,2},{2,1},{3,0},{4,7},{5,6},{6,5},{7,4},{8,11},{9,10},{10,... | collective-permute-start | bytes 995336 | tf_op jit(solution)/shard_map/ppermute | solution.py:66
  15.9 28.4 %collective-permute-start.1 = (bf16[48,3456]{1,0:T(8,128)(2,1)S(1)}, bf16[48,3456]{1,0:T(8,128)(2,1)}, u32[]{:S(2)}, u32[]{:S(2)}) collective-permute-start(bf16[48,3456]{1,0:T(8,128)(2,1)S(1)} %get-tuple-element.309), channel_id=1, source_target_pairs={{0,2},{1,3},{2,0},{3,1},{4,6},{5,7},{6,4},{7,5},{8,10},{9,11},{10,... | collective-permute-start | bytes 995336 | tf_op jit(solution)/shard_map/ppermute | solution.py:66
  15.9 28.4 %collective-permute-start = (bf16[48,3456]{1,0:T(8,128)(2,1)S(1)}, bf16[48,3456]{1,0:T(8,128)(2,1)}, u32[]{:S(2)}, u32[]{:S(2)}) collective-permute-start(bf16[48,3456]{1,0:T(8,128)(2,1)S(1)} %get-tuple-element.309), channel_id=1, source_target_pairs={{0,1},{1,0},{2,3},{3,2},{4,5},{5,4},{6,7},{7,6},{8,9},{9,8},{10,11... | collective-permute-start | bytes 995336 | tf_op jit(solution)/shard_map/ppermute | solution.py:66
  45.5 25.3 %collective-permute-start.6 = (bf16[144,3456]{1,0:T(8,128)(2,1)S(1)}, bf16[144,3456]{1,0:T(8,128)(2,1)S(1)}, u32[]{:S(2)}, u32[]{:S(2)}) collective-permute-start(bf16[144,3456]{1,0:T(8,128)(2,1)S(1)} %pad_maximum_fusion.9.refs_1_), channel_id=1, source_target_pairs={{0,8},{8,0},{16,24},{24,16},{1,9},{9,1},{17,25},{25,17},{2,10},{10... | collective-permute-start | bytes 2985992 | tf_op jit(solution)/shard_map/ppermute | solution.py:66
  47.1 23.8 %collective-permute-start.7 = (bf16[144,3456]{1,0:T(8,128)(2,1)S(1)}, bf16[144,3456]{1,0:T(8,128)(2,1)S(1)}, u32[]{:S(2)}, u32[]{:S(2)}) collective-permute-start(bf16[144,3456]{1,0:T(8,128)(2,1)S(1)} %pad_maximum_fusion.9.refs_1_), channel_id=1, source_target_pairs={{0,16},{8,24},{16,0},{24,8},{1,17},{9,25},{17,1},{25,9},{2,18},{10... | collective-permute-start | bytes 2985992 | tf_op jit(solution)/shard_map/ppermute | solution.py:66
  51.1 19.7 %collective-permute-start.9 = (bf16[48,2688]{1,0:T(8,128)(2,1)S(1)}, bf16[48,2688]{1,0:T(8,128)(2,1)S(1)}, u32[]{:S(2)}, u32[]{:S(2)}) collective-permute-start(bf16[48,2688]{1,0:T(8,128)(2,1)S(1)} %get-tuple-element.316), channel_id=1, source_target_pairs={{0,2},{1,3},{2,0},{3,1},{4,6},{5,7},{6,4},{7,5},{8,10},{9,11},{10,... | collective-permute-start | bytes 774152 | tf_op jit(solution)/shard_map/ppermute | solution.py:66
  51.1 19.7 %collective-permute-start.8 = (bf16[48,2688]{1,0:T(8,128)(2,1)S(1)}, bf16[48,2688]{1,0:T(8,128)(2,1)S(1)}, u32[]{:S(2)}, u32[]{:S(2)}) collective-permute-start(bf16[48,2688]{1,0:T(8,128)(2,1)S(1)} %get-tuple-element.316), channel_id=1, source_target_pairs={{0,1},{1,0},{2,3},{3,2},{4,5},{5,4},{6,7},{7,6},{8,9},{9,8},{10,11... | collective-permute-start | bytes 774152 | tf_op jit(solution)/shard_map/ppermute | solution.py:66
  72.1 31.6 %collective-permute-start.12 = (bf16[144,4480]{1,0:T(8,128)(2,1)S(1)}, bf16[144,4480]{1,0:T(8,128)(2,1)S(1)}, u32[]{:S(2)}, u32[]{:S(2)}) collective-permute-start(bf16[144,4480]{1,0:T(8,128)(2,1)S(1)} %pad_maximum_fusion.4), channel_id=1, source_target_pairs={{0,8},{8,0},{16,24},{24,16},{1,9},{9,1},{17,25},{25,17},{2,10},{10... | collective-permute-start | bytes 3870728 | tf_op jit(solution)/shard_map/ppermute | solution.py:66
  72.8 30.9 %collective-permute-start.11 = (bf16[144,4352]{1,0:T(8,128)(2,1)S(1)}, bf16[144,4352]{1,0:T(8,128)(2,1)S(1)}, u32[]{:S(2)}, u32[]{:S(2)}) collective-permute-start(bf16[144,4352]{1,0:T(8,128)(2,1)S(1)} %pad_maximum_fusion.5), channel_id=1, source_target_pairs={{0,16},{8,24},{16,0},{24,8},{1,17},{9,25},{17,1},{25,9},{2,18},{10... | collective-permute-start | bytes 3760136 | tf_op jit(solution)/shard_map/ppermute | solution.py:66
  75.4 28.2 %collective-permute-start.14 = (bf16[48,3840]{1,0:T(8,128)(2,1)S(1)}, bf16[48,3840]{1,0:T(8,128)(2,1)S(1)}, u32[]{:S(2)}, u32[]{:S(2)}) collective-permute-start(bf16[48,3840]{1,0:T(8,128)(2,1)S(1)} %get-tuple-element.322), channel_id=1, source_target_pairs={{0,2},{1,3},{2,0},{3,1},{4,6},{5,7},{6,4},{7,5},{8,10},{9,11},{10,... | collective-permute-start | bytes 1105928 | tf_op jit(solution)/shard_map/ppermute | solution.py:66
  75.4 28.2 %collective-permute-start.13 = (bf16[48,3840]{1,0:T(8,128)(2,1)S(1)}, bf16[48,3840]{1,0:T(8,128)(2,1)S(1)}, u32[]{:S(2)}, u32[]{:S(2)}) collective-permute-start(bf16[48,3840]{1,0:T(8,128)(2,1)S(1)} %get-tuple-element.322), channel_id=1, source_target_pairs={{0,1},{1,0},{2,3},{3,2},{4,5},{5,4},{6,7},{7,6},{8,9},{9,8},{10,11... | collective-permute-start | bytes 1105928 | tf_op jit(solution)/shard_map/ppermute | solution.py:66
  110.7 22.4 %collective-permute-start.21 = (bf16[768,1536]{1,0:T(8,128)(2,1)}, bf16[768,1536]{1,0:T(8,128)(2,1)}, u32[]{:S(2)}, u32[]{:S(2)}) collective-permute-start(bf16[768,1536]{1,0:T(8,128)(2,1)} %get-tuple-element.345.refs_8_.refs_7_), channel_id=1, source_target_pairs={{0,4},{4,0},{1,5},{5,1},{2,6},{6,2},{3,7},{7,3},{8,12},{12,8},{9,1... | collective-permute-start | bytes 7077896 | tf_op jit(solution)/shard_map/ppermute | solution.py:66
  112.0 37.8 %collective-permute-start.17 = (bf16[144,5248]{1,0:T(8,128)(2,1)}, bf16[144,5248]{1,0:T(8,128)(2,1)}, u32[]{:S(2)}, u32[]{:S(2)}) collective-permute-start(bf16[144,5248]{1,0:T(8,128)(2,1)} %pad_maximum_fusion.2), channel_id=1, source_target_pairs={{0,8},{8,0},{16,24},{24,16},{1,9},{9,1},{17,25},{25,17},{2,10},{10... | collective-permute-start | bytes 4534280 | tf_op jit(solution)/shard_map/ppermute | solution.py:66
  115.0 34.8 %collective-permute-start.16 = (bf16[144,5120]{1,0:T(8,128)(2,1)}, bf16[144,5120]{1,0:T(8,128)(2,1)}, u32[]{:S(2)}, u32[]{:S(2)}) collective-permute-start(bf16[144,5120]{1,0:T(8,128)(2,1)} %pad_maximum_fusion.3), channel_id=1, source_target_pairs={{0,16},{8,24},{16,0},{24,8},{1,17},{9,25},{17,1},{25,9},{2,18},{10... | collective-permute-start | bytes 4423688 | tf_op jit(solution)/shard_map/ppermute | solution.py:66
  155.1 24.3 %collective-permute-start.25 = (bf16[416,2304]{1,0:T(8,128)(2,1)}, bf16[416,2304]{1,0:T(8,128)(2,1)S(1)}, u32[]{:S(2)}, u32[]{:S(2)}) collective-permute-start(bf16[416,2304]{1,0:T(8,128)(2,1)} %get-tuple-element.367), channel_id=1, source_target_pairs={{0,4},{4,0},{1,5},{5,1},{2,6},{6,2},{3,7},{7,3},{8,12},{12,8},{9,1... | collective-permute-start | bytes 5750792 | tf_op jit(solution)/shard_map/ppermute | solution.py:66
  155.1 24.2 %collective-permute-start.24 = (bf16[416,1152]{1,0:T(8,128)(2,1)}, bf16[416,1152]{1,0:T(8,128)(2,1)S(1)}, u32[]{:S(2)}, u32[]{:S(2)}) collective-permute-start(bf16[416,1152]{1,0:T(8,128)(2,1)} %get-tuple-element.360), channel_id=1, source_target_pairs={{0,4},{4,0},{1,5},{5,1},{2,6},{6,2},{3,7},{7,3},{8,12},{12,8},{9,1... | collective-permute-start | bytes 2875400 | tf_op jit(solution)/shard_map/ppermute | solution.py:66
  156.7 22.6 %collective-permute-start.22 = (bf16[144,1920]{1,0:T(8,128)(2,1)S(1)}, bf16[144,1920]{1,0:T(8,128)(2,1)S(1)}, u32[]{:S(2)}, u32[]{:S(2)}) collective-permute-start(bf16[144,1920]{1,0:T(8,128)(2,1)S(1)} %slice.457), channel_id=1, source_target_pairs={{0,16},{8,24},{16,0},{24,8},{1,17},{9,25},{17,1},{25,9},{2,18},{10... | collective-permute-start | bytes 1658888 | tf_op jit(solution)/shard_map/ppermute | solution.py:66
  161.8 17.5 %collective-permute-start.23 = (bf16[144,1920]{1,0:T(8,128)(2,1)S(1)}, bf16[144,1920]{1,0:T(8,128)(2,1)S(1)}, u32[]{:S(2)}, u32[]{:S(2)}) collective-permute-start(bf16[144,1920]{1,0:T(8,128)(2,1)S(1)} %slice.458), channel_id=1, source_target_pairs={{0,8},{8,0},{16,24},{24,16},{1,9},{9,1},{17,25},{25,17},{2,10},{10... | collective-permute-start | bytes 1658888 | tf_op jit(solution)/shard_map/ppermute | solution.py:66
  185.0 21.5 %collective-permute-start.30 = (bf16[768,1536]{1,0:T(8,128)(2,1)}, bf16[768,1536]{1,0:T(8,128)(2,1)}, u32[]{:S(2)}, u32[]{:S(2)}) collective-permute-start(bf16[768,1536]{1,0:T(8,128)(2,1)} %get-tuple-element.396.refs_7_.refs_3_), channel_id=1, source_target_pairs={{0,4},{4,0},{1,5},{5,1},{2,6},{6,2},{3,7},{7,3},{8,12},{12,8},{9,1... | collective-permute-start | bytes 7077896 | tf_op jit(solution)/shard_map/ppermute | solution.py:66
  185.5 21.0 %collective-permute-start.31 = (bf16[768,384]{1,0:T(8,128)(2,1)}, bf16[768,384]{1,0:T(8,128)(2,1)S(1)}, u32[]{:S(2)}, u32[]{:S(2)}) collective-permute-start(bf16[768,384]{1,0:T(8,128)(2,1)} %get-tuple-element.397.refs_9_), channel_id=1, source_target_pairs={{0,4},{4,0},{1,5},{5,1},{2,6},{6,2},{3,7},{7,3},{8,12},{12,8},{9,1... | collective-permute-start | bytes 1769480 | tf_op jit(solution)/shard_map/ppermute | solution.py:66
  250.0 36.1 %collective-permute-start.35 = (f16[400,1920]{1,0:T(8,128)(2,1)}, f16[400,1920]{1,0:T(8,128)(2,1)S(1)}, u32[]{:S(2)}, u32[]{:S(2)}) collective-permute-start(f16[400,1920]{1,0:T(8,128)(2,1)} %pad_maximum_fusion.1), channel_id=1, source_target_pairs={{0,8},{8,0},{16,24},{24,16},{1,9},{9,1},{17,25},{25,17},{2,10},{10... | collective-permute-start | bytes 4608008 | tf_op jit(solution)/shard_map/ppermute | solution.py:66
  251.5 29.1 %collective-permute-start.36 = (f16[400,1536]{1,0:T(8,128)(2,1)S(1)}, f16[400,1536]{1,0:T(8,128)(2,1)}, u32[]{:S(2)}, u32[]{:S(2)}) collective-permute-start(f16[400,1536]{1,0:T(8,128)(2,1)S(1)} %convert_element_type.354), channel_id=1, source_target_pairs={{0,16},{8,24},{16,0},{24,8},{1,17},{9,25},{17,1},{25,9},{2,18},{10... | collective-permute-start | bytes 3686408 | tf_op jit(solution)/shard_map/ppermute | solution.py:66
  253.1 43.1 %collective-permute-start.40 = (bf16[416,1152]{1,0:T(8,128)(2,1)S(1)}, bf16[416,1152]{1,0:T(8,128)(2,1)S(1)}, u32[]{:S(2)}, u32[]{:S(2)}) collective-permute-start(bf16[416,1152]{1,0:T(8,128)(2,1)S(1)} %copy-done.133), channel_id=1, source_target_pairs={{0,4},{4,0},{1,5},{5,1},{2,6},{6,2},{3,7},{7,3},{8,12},{12,8},{9,1... | collective-permute-start | bytes 2875400 | tf_op jit(solution)/shard_map/ppermute | solution.py:66
  290.2 20.0 %collective-permute-start.38 = (f16[208,1920]{1,0:T(8,128)(2,1)S(1)}, f16[208,1920]{1,0:T(8,128)(2,1)S(1)}, u32[]{:S(2)}, u32[]{:S(2)}) collective-permute-start(f16[208,1920]{1,0:T(8,128)(2,1)S(1)} %pad_maximum_fusion.10), channel_id=1, source_target_pairs={{0,16},{8,24},{16,0},{24,8},{1,17},{9,25},{17,1},{25,9},{2,18},{10... | collective-permute-start | bytes 2396168 | tf_op jit(solution)/shard_map/ppermute | solution.py:66
  313.9 17.9 %collective-permute-start.41 = (f16[112,3456]{1,0:T(8,128)(2,1)}, f16[112,3456]{1,0:T(8,128)(2,1)}, u32[]{:S(2)}, u32[]{:S(2)}) collective-permute-start(f16[112,3456]{1,0:T(8,128)(2,1)} %pad_maximum_fusion.12), channel_id=1, source_target_pairs={{0,1},{1,0},{2,3},{3,2},{4,5},{5,4},{6,7},{7,6},{8,9},{9,8},{10,11... | collective-permute-start | bytes 2322440 | tf_op jit(solution)/shard_map/ppermute | solution.py:66
  313.9 17.9 %collective-permute-start.42 = (f16[400,768]{1,0:T(8,128)(2,1)}, f16[400,768]{1,0:T(8,128)(2,1)}, u32[]{:S(2)}, u32[]{:S(2)}) collective-permute-start(f16[400,768]{1,0:T(8,128)(2,1)} %convert_element_type.360), channel_id=1, source_target_pairs={{0,8},{8,0},{16,24},{24,16},{1,9},{9,1},{17,25},{25,17},{2,10},{10... | collective-permute-start | bytes 1843208 | tf_op jit(solution)/shard_map/ppermute | solution.py:66
  315.3 16.4 %collective-permute-start.43 = (f16[400,768]{1,0:T(8,128)(2,1)}, f16[400,768]{1,0:T(8,128)(2,1)}, u32[]{:S(2)}, u32[]{:S(2)}) collective-permute-start(f16[400,768]{1,0:T(8,128)(2,1)} %pad_maximum_fusion.19), channel_id=1, source_target_pairs={{0,16},{8,24},{16,0},{24,8},{1,17},{9,25},{17,1},{25,9},{2,18},{10... | collective-permute-start | bytes 1843208 | tf_op jit(solution)/shard_map/ppermute | solution.py:66
  331.8 26.2 %collective-permute-start.44 = (bf16[416,2304]{1,0:T(8,128)(2,1)}, bf16[416,2304]{1,0:T(8,128)(2,1)}, u32[]{:S(2)}, u32[]{:S(2)}) collective-permute-start(bf16[416,2304]{1,0:T(8,128)(2,1)} %get-tuple-element.480), channel_id=1, source_target_pairs={{0,4},{4,0},{1,5},{5,1},{2,6},{6,2},{3,7},{7,3},{8,12},{12,8},{9,1... | collective-permute-start | bytes 5750792 | tf_op jit(solution)/shard_map/ppermute | solution.py:66
  335.7 28.0 %collective-permute-start.45 = (f16[64,3456]{1,0:T(8,128)(2,1)}, f16[64,3456]{1,0:T(8,128)(2,1)}, u32[]{:S(2)}, u32[]{:S(2)}) collective-permute-start(f16[64,3456]{1,0:T(8,128)(2,1)} %pad_maximum_fusion.23), channel_id=1, source_target_pairs={{0,2},{1,3},{2,0},{3,1},{4,6},{5,7},{6,4},{7,5},{8,10},{9,11},{10,... | collective-permute-start | bytes 1327112 | tf_op jit(solution)/shard_map/ppermute | solution.py:66
  342.1 21.6 %collective-permute-start.46 = (f16[208,768]{1,0:T(8,128)(2,1)}, f16[208,768]{1,0:T(8,128)(2,1)}, u32[]{:S(2)}, u32[]{:S(2)}) collective-permute-start(f16[208,768]{1,0:T(8,128)(2,1)} %pad_maximum_fusion.30), channel_id=1, source_target_pairs={{0,16},{8,24},{16,0},{24,8},{1,17},{9,25},{17,1},{25,9},{2,18},{10... | collective-permute-start | bytes 958472 | tf_op jit(solution)/shard_map/ppermute | solution.py:66
  365.3 34.9 %collective-permute-start.49 = (f16[400,1536]{1,0:T(8,128)(2,1)}, f16[400,1536]{1,0:T(8,128)(2,1)}, u32[]{:S(2)}, u32[]{:S(2)}) collective-permute-start(f16[400,1536]{1,0:T(8,128)(2,1)} %convert_element_type.375), channel_id=1, source_target_pairs={{0,8},{8,0},{16,24},{24,16},{1,9},{9,1},{17,25},{25,17},{2,10},{10... | collective-permute-start | bytes 3686408 | tf_op jit(solution)/shard_map/ppermute | solution.py:66
  366.7 33.5 %collective-permute-start.50 = (f16[400,1536]{1,0:T(8,128)(2,1)S(1)}, f16[400,1536]{1,0:T(8,128)(2,1)}, u32[]{:S(2)}, u32[]{:S(2)}) collective-permute-start(f16[400,1536]{1,0:T(8,128)(2,1)S(1)} %convert_element_type.376), channel_id=1, source_target_pairs={{0,16},{8,24},{16,0},{24,8},{1,17},{9,25},{17,1},{25,9},{2,18},{10... | collective-permute-start | bytes 3686408 | tf_op jit(solution)/shard_map/ppermute | solution.py:66
  370.1 30.0 %collective-permute-start.48 = (f16[112,1536]{1,0:T(8,128)(2,1)S(1)}, f16[112,1536]{1,0:T(8,128)(2,1)S(1)}, u32[]{:S(2)}, u32[]{:S(2)}) collective-permute-start(f16[112,1536]{1,0:T(8,128)(2,1)S(1)} %pad_maximum_fusion.29), channel_id=1, source_target_pairs={{0,1},{1,0},{2,3},{3,2},{4,5},{5,4},{6,7},{7,6},{8,9},{9,8},{10,11... | collective-permute-start | bytes 1032200 | tf_op jit(solution)/shard_map/ppermute | solution.py:66
  405.0 18.0 %collective-permute-start.52 = (f16[208,1536]{1,0:T(8,128)(2,1)S(1)}, f16[208,1536]{1,0:T(8,128)(2,1)S(1)}, u32[]{:S(2)}, u32[]{:S(2)}) collective-permute-start(f16[208,1536]{1,0:T(8,128)(2,1)S(1)} %pad_maximum_fusion.16), channel_id=1, source_target_pairs={{0,16},{8,24},{16,0},{24,8},{1,17},{9,25},{17,1},{25,9},{2,18},{10... | collective-permute-start | bytes 1916936 | tf_op jit(solution)/shard_map/ppermute | solution.py:66
  409.1 16.8 %collective-permute-start.53 = (f16[208,1536]{1,0:T(8,128)(2,1)S(1)}, f16[208,1536]{1,0:T(8,128)(2,1)S(1)}, u32[]{:S(2)}, u32[]{:S(2)}) collective-permute-start(f16[208,1536]{1,0:T(8,128)(2,1)S(1)} %pad_maximum_fusion.17), channel_id=1, source_target_pairs={{0,8},{8,0},{16,24},{24,16},{1,9},{9,1},{17,25},{25,17},{2,10},{10... | collective-permute-start | bytes 1916936 | tf_op jit(solution)/shard_map/ppermute | solution.py:66
  432.2 18.5 %collective-permute-start.57 = (f16[112,3072]{1,0:T(8,128)(2,1)S(1)}, f16[112,3072]{1,0:T(8,128)(2,1)S(1)}, u32[]{:S(2)}, u32[]{:S(2)}) collective-permute-start(f16[112,3072]{1,0:T(8,128)(2,1)S(1)} %pad_maximum_fusion.13), channel_id=1, source_target_pairs={{0,1},{1,0},{2,3},{3,2},{4,5},{5,4},{6,7},{7,6},{8,9},{9,8},{10,11... | collective-permute-start | bytes 2064392 | tf_op jit(solution)/shard_map/ppermute | solution.py:66
  434.2 22.6 %collective-permute-start.58 = (f16[400,1152]{1,0:T(8,128)(2,1)S(1)}, f16[400,1152]{1,0:T(8,128)(2,1)S(1)}, u32[]{:S(2)}, u32[]{:S(2)}) collective-permute-start(f16[400,1152]{1,0:T(8,128)(2,1)S(1)} %convert_element_type.394), channel_id=1, source_target_pairs={{0,8},{8,0},{16,24},{24,16},{1,9},{9,1},{17,25},{25,17},{2,10},{10... | collective-permute-start | bytes 2764808 | tf_op jit(solution)/shard_map/ppermute | solution.py:66
  462.1 19.2 %collective-permute-start.63 = (f16[64,3072]{1,0:T(8,128)(2,1)}, f16[64,3072]{1,0:T(8,128)(2,1)}, u32[]{:S(2)}, u32[]{:S(2)}) collective-permute-start(f16[64,3072]{1,0:T(8,128)(2,1)} %pad_maximum_fusion.25), channel_id=1, source_target_pairs={{0,2},{1,3},{2,0},{3,1},{4,6},{5,7},{6,4},{7,5},{8,10},{9,11},{10,... | collective-permute-start | bytes 1179656 | tf_op jit(solution)/shard_map/ppermute | solution.py:66
  464.6 16.7 %collective-permute-start.64 = (f16[208,1152]{1,0:T(8,128)(2,1)}, f16[208,1152]{1,0:T(8,128)(2,1)}, u32[]{:S(2)}, u32[]{:S(2)}) collective-permute-start(f16[208,1152]{1,0:T(8,128)(2,1)} %pad_maximum_fusion.22), channel_id=1, source_target_pairs={{0,16},{8,24},{16,0},{24,8},{1,17},{9,25},{17,1},{25,9},{2,18},{10... | collective-permute-start | bytes 1437704 | tf_op jit(solution)/shard_map/ppermute | solution.py:66
  469.7 68.8 %collective-permute-start.77 = (f16[64,4992]{1,0:T(8,128)(2,1)S(1)}, f16[64,4992]{1,0:T(8,128)(2,1)}, u32[]{:S(2)}, u32[]{:S(2)}) collective-permute-start(f16[64,4992]{1,0:T(8,128)(2,1)S(1)} %pad_maximum_fusion.18), channel_id=1, source_target_pairs={{0,8},{8,0},{16,24},{24,16},{1,9},{9,1},{17,25},{25,17},{2,10},{10... | collective-permute-start | bytes 1916936 | tf_op jit(solution)/shard_map/ppermute | solution.py:66
  470.9 68.7 %collective-permute-start.78 = (f16[64,4992]{1,0:T(8,128)(2,1)S(1)}, f16[64,4992]{1,0:T(8,128)(2,1)}, u32[]{:S(2)}, u32[]{:S(2)}) collective-permute-start(f16[64,4992]{1,0:T(8,128)(2,1)S(1)} %pad_maximum_fusion.18), channel_id=1, source_target_pairs={{0,16},{8,24},{16,0},{24,8},{1,17},{9,25},{17,1},{25,9},{2,18},{10... | collective-permute-start | bytes 1916936 | tf_op jit(solution)/shard_map/ppermute | solution.py:66
  478.0 64.0 %collective-permute-start.79 = (f16[64,4992]{1,0:T(8,128)(2,1)S(1)}, f16[64,4992]{1,0:T(8,128)(2,1)}, u32[]{:S(2)}, u32[]{:S(2)}) collective-permute-start(f16[64,4992]{1,0:T(8,128)(2,1)S(1)} %pad_maximum_fusion.18), channel_id=1, source_target_pairs={{0,24},{8,16},{16,8},{24,0},{1,25},{9,17},{17,9},{25,1},{2,26},{10... | collective-permute-start | bytes 1916936 | tf_op jit(solution)/shard_map/ppermute | solution.py:66
  538.4 25.7 %collective-permute-start.81 = (f16[64,3072]{1,0:T(8,128)(2,1)S(1)}, f16[64,3072]{1,0:T(8,128)(2,1)S(1)}, u32[]{:S(2)}, u32[]{:S(2)}) collective-permute-start(f16[64,3072]{1,0:T(8,128)(2,1)S(1)} %pad_maximum_fusion.27), channel_id=1, source_target_pairs={{0,16},{8,24},{16,0},{24,8},{1,17},{9,25},{17,1},{25,9},{2,18},{10... | collective-permute-start | bytes 1179656 | tf_op jit(solution)/shard_map/ppermute | solution.py:66
  539.6 24.5 %collective-permute-start.82 = (f16[64,3072]{1,0:T(8,128)(2,1)S(1)}, f16[64,3072]{1,0:T(8,128)(2,1)S(1)}, u32[]{:S(2)}, u32[]{:S(2)}) collective-permute-start(f16[64,3072]{1,0:T(8,128)(2,1)S(1)} %pad_maximum_fusion.27), channel_id=1, source_target_pairs={{0,24},{8,16},{16,8},{24,0},{1,25},{9,17},{17,9},{25,1},{2,26},{10... | collective-permute-start | bytes 1179656 | tf_op jit(solution)/shard_map/ppermute | solution.py:66
  542.1 22.0 %collective-permute-start.83 = (f16[64,1920]{1,0:T(8,128)(2,1)S(1)}, f16[64,1920]{1,0:T(8,128)(2,1)S(1)}, u32[]{:S(2)}, u32[]{:S(2)}) collective-permute-start(f16[64,1920]{1,0:T(8,128)(2,1)S(1)} %pad_maximum_fusion.35), channel_id=1, source_target_pairs={{0,8},{8,0},{16,24},{24,16},{1,9},{9,1},{17,25},{25,17},{2,10},{10... | collective-permute-start | bytes 737288 | tf_op jit(solution)/shard_map/ppermute | solution.py:66
  542.6 26.3 %collective-permute-start.84 = (f16[64,1920]{1,0:T(8,128)(2,1)S(1)}, f16[64,1920]{1,0:T(8,128)(2,1)S(1)}, u32[]{:S(2)}, u32[]{:S(2)}) collective-permute-start(f16[64,1920]{1,0:T(8,128)(2,1)S(1)} %pad_maximum_fusion.35), channel_id=1, source_target_pairs={{0,16},{8,24},{16,0},{24,8},{1,17},{9,25},{17,1},{25,9},{2,18},{10... | collective-permute-start | bytes 737288 | tf_op jit(solution)/shard_map/ppermute | solution.py:66
  543.8 25.2 %collective-permute-start.85 = (f16[64,1920]{1,0:T(8,128)(2,1)S(1)}, f16[64,1920]{1,0:T(8,128)(2,1)S(1)}, u32[]{:S(2)}, u32[]{:S(2)}) collective-permute-start(f16[64,1920]{1,0:T(8,128)(2,1)S(1)} %pad_maximum_fusion.35), channel_id=1, source_target_pairs={{0,24},{8,16},{16,8},{24,0},{1,25},{9,17},{17,9},{25,1},{2,26},{10... | collective-permute-start | bytes 737288 | tf_op jit(solution)/shard_map/ppermute | solution.py:66
  569.0 31.6 %collective-permute-start.86 = (f32[2]{0:T(128)S(1)}, f32[2]{0:T(128)S(1)}, u32[]{:S(2)}, u32[]{:S(2)}) collective-permute-start(f32[2]{0:T(128)S(1)} %add.1082), channel_id=1, source_target_pairs={{0,1},{1,0},{2,3},{3,2},{4,5},{5,4},{6,7},{7,6},{8,9},{9,8},{10,11... | collective-permute-start | bytes 32 | tf_op jit(solution)/shard_map/ppermute | solution.py:66
  (178 other events, 1460.4 us)

commit v3 on v2

--- a/solution.py
+++ b/solution.py
@@ -324,14 +324,18 @@
     put_rows(wide, [class_sum, mask_sum, rows_sum(low)])
 
 
+def four(value, axis):
+    got = [swap(value, axis, k) for k in (1, 2, 3)]
+    return (value + got[0]) + (got[1] + got[2])
+
+
 def tie(*trees):
     leaves, shape = jax.tree.flatten(trees)
     return jax.tree.unflatten(shape, lax.optimization_barrier(leaves))
 
 
 def prepare_body(plan, cuts, places, qkv, out, up, down, ends, *rest):
-    outs, turned = rest[:-1], rest[-1]
-    whole, owns, firsts = outs[0], outs[1::2], outs[2::2]
+    whole, owns, firsts = rest[0], rest[1::2], rest[2::2]
     sub_at = places[0]
     part = whole.shape[1]
     refs = {"qkv": qkv, "out": out, "up": up, "down": down, "ends": ends}
@@ -339,12 +343,9 @@
         begin = plan[cuts[chunk]][2]
         for name, layer, start, width in plan[cuts[chunk] : cuts[chunk + 1]]:
             ref = refs[name]
-            plain = name in ("qkv", "up")
-            if not plain:
-                turned[:, :width] = ref[layer].T.astype(f32)
             for k in range(4):
                 rows = pl.ds(pl.multiple_of(jnp.bitwise_xor(sub_at, k) * part, 16), part)
-                piece = ref[layer, rows, :] if plain else turned[rows, :width].astype(bf16)
+                piece = ref[layer, rows, :]
                 whole[k, :, start : start + width] = piece
                 owns[chunk][k, :, start - begin : start - begin + width] = piece
                 if k == 0:
@@ -358,11 +359,9 @@
     for j, k in zip(cuts[:-1], cuts[1:]):
         width = plan[k - 1][2] + plan[k - 1][3] - plan[j][2]
         outs += [((4, part, width), bf16), ((part, width), bf16)]
-    widest = max(entry[3] for entry in plan)
     got = whole_call_smem(
         lambda *refs: prepare_body(plan, cuts, *refs), 1, 5, outs, "prepare_tiles", 10**8,
-        [pltpu.VMEM((height, widest), f32)],
-    )(places, qkv, out, up, down, ends)
+    )(places, qkv, out.swapaxes(1, 2), up, down.swapaxes(1, 2), ends.swapaxes(1, 2))
     return got[0], got[1::2], got[2::2]
 
 
@@ -565,8 +564,9 @@
     @pl.when(step == 0)
     def _():
         for ref, (sub, spans) in zip(pieces, layout):
+            part = grads.shape[1]
             for source, target, size in spans:
-                grads[sub, :, target : target + size] = ref[:, source : source + size]
+                grads[sub, :, target : target + size] = scaled(ref[:, source : source + size], part)
 
     window = 2 * 128
 
@@ -608,13 +608,17 @@
     )(info, weight, *pieces, root_left, root_right)
 
 
+def scaled(rows, part):
+    return rows[:part] * jnp.exp2(rows[part : part + 1] - 14.0)
+
+
 def ends_body(places, *refs):
     out = refs[-1]
-    part = refs[0].shape[0]
+    part = out.shape[1] // 4
     for end in range(2):
         for k in range(4):
             sub = jnp.bitwise_xor(places[0], k)
-            out[end, pl.ds(pl.multiple_of(sub * part, 8), part), :] = refs[4 * end + k][...]
+            out[end, pl.ds(pl.multiple_of(sub * part, 8), part), :] = scaled(refs[4 * end + k][...], part)
 
 
 def adam_update(weight, gradient, moment, second, rate, decay, factor, step_value):
@@ -849,7 +853,7 @@
 
     flying, done = [], []
 
-    spreads, groups = [], []
+    groups = []
     ready = 0
 
     def spread(members):
@@ -870,11 +874,16 @@
         flying[:] = [r for r in flying if r.stage < 4] + list(fresh)
         for r in flying:
             r.send()
-        stop = sum(1 for g, _ in groups if g.stage == 4)
-        if stop > ready and len(groups) == 2 * layer_count:
-            spreads.append([spread([g for g, _ in groups[ready:stop]]), groups[ready:stop]])
-            ready = stop
         return value
+
+    def spread_done(stop):
+        nonlocal ready
+        members = groups[ready:stop]
+        ready = stop
+        return [spread([g for g, _ in members]), members]
+
+    def decode_all(entry):
+        entry[0] = [payload.astype(f32) for payload in entry[0]]
 
     wides = {"head": values["wide", "head"]}
     flats = {"head": values["flat", "head"]}
@@ -994,20 +1003,29 @@
         swap(rows_at(value, sub_index ^ k, sub_rows), "dp", k) for k in (1, 2, 3)
     )
     value = step_on(value, [])
+    early = spread_done(len(groups) - 2)
     value = butterfly(value, ("col",))
     for mask in bits_of("dp")[2:]:
         value = value + swap(value, "dp", mask)
-    while flying:
-        value = step_on(value, [])
+    value, early[0] = step_on((value, early[0]), [])
+    decode_all(early)
+    middle = spread_done(len(groups) - 1)
+    square = jnp.sum(value * value) / lax.axis_size("col")
+    value = jnp.concatenate([value] + [swap(value, "dp", k) for k in (1, 2, 3)], axis=0)
+    value, middle[0], early[0] = step_on((value, middle[0], early[0]), [])
+    decode_all(middle)
+    late = spread_done(len(groups))
+    spreads = [early, middle, late]
     copies = max(1, data_count // 4)
-    square = sum(jnp.sum(g.keep * g.keep) for g, _ in groups)
-    square = (square + jnp.sum(value * value) / lax.axis_size("col")) / copies
-    pair = butterfly(jnp.stack([square, values["loss"][0, 0]]), ("row", "dp"))
-    value = jnp.concatenate([value] + [swap(value, "dp", k) for k in (1, 2, 3)], axis=0)
+    square = (square + sum(jnp.sum(g.keep * g.keep) for g, _ in groups)) / copies
+    pair = butterfly(jnp.stack([square, values["loss"][0, 0]]), ("row",))
+    pair = four(pair, "dp")
+    for mask in bits_of("dp")[2:]:
+        pair = pair + swap(pair, "dp", mask)
+    pair, late[0], middle[0] = tie(pair, late[0], middle[0])
+    decode_all(late)
+    pair = four(pair, "col")
     value = jnp.concatenate([value, across_core(value)], axis=0)
-    pair, value, payloads = tie(pair, value, [payloads for payloads, _ in spreads])
-    for entry, got in zip(spreads, payloads):
-        entry[0] = got
     spot = jnp.arange(rows_all)
     native = (
         ((spot // half_rows) ^ row_index) * half_rows
@@ -1016,7 +1034,6 @@
     )
     pick = (jnp.arange(vectors.shape[0])[:, None] == native[None, :]).astype(f32)
     vec_sum = exact(pick, value, 1, 0)
-    pair = butterfly(pair, ("col",))
     loss_total = pair[1]
     grad_norm = jnp.sqrt(pair[0])
     factor = jnp.minimum(1.0, clip_scale / math.sqrt(total_tokens) / grad_norm)
@@ -1032,7 +1049,7 @@
                 ends_parts[name[1]] = (len(pieces), at)
             at += size
         for k, payload in enumerate(payloads):
-            pieces.append(decoded(payload[:-16], tail_of(payload)))
+            pieces.append(payload)
             layout.append((k, spans))
     raw_grad, raw_left, raw_right, raw_precond, own_weight = shampoo(
         info, tiles_own, pieces, layout, root_left[0], root_right[0]

time: 636 us -> 608 us (0.956)
  waiting for transfers between devices: 171 us -> 154 us
  local copies, waits for them, and re-layouts: 43.1 us -> 34.7 us
    ppermute x88 -> x90, waiting for transfers between devices: 171 us -> 154 us  [swap(): return lax.ppermute(value, axis, [(i, i ^ mask) for i in range(size)])]
    convert_element_type x0 -> x12, other arithmetic: none -> 11.3 us  [decode_all(): entry[0] = [payload.astype(f32) for payload in entry[0]]]
    unnamed x292 -> x298, local copies, waits for them, and re-layouts: 31.7 us -> 23 us
    mul x12 -> x0, other arithmetic: 7.07 us -> none  [decoded(): return rows.astype(f32) * jnp.exp2(exponent - 14.0)]
    reduce_max x36 -> x24, other arithmetic: 14.5 us -> 8.75 us  [tail_of(): return jnp.max(payload[-16:].astype(f32), axis=0, keepdims=True)]
    ppermute x88 -> x90, starting transfers between devices: 88.1 us -> 91.2 us  [swap(): return lax.ppermute(value, axis, [(i, i ^ mask) for i in range(size)])]
  transfers between devices with their start and end apart: 88 -> 90, of which waited for: 30 -> 28; matrix products, arithmetic and copies ran while one was open for 14% -> 16% of each run, Pallas kernels for 27% -> 28%
where the time goes in v3:
time: 608 us; the launch traced here: 597 us
  Pallas kernels  204 us (34%)
  waiting for transfers between devices  154 us (25%)
  other arithmetic  93 us (15%)
  starting transfers between devices  91.2 us (15%)
  local copies, waits for them, and re-layouts  34.7 us (6%)
  between operations  11.5 us (2%)
  matrix products  8.78 us (1%)
    ppermute x90, waiting for transfers between devices, swap(): return lax.ppermute(value, axis, [(i, i ^ mask) for i in range(size)])  154 us
    ppermute x90, starting transfers between devices, swap(): return lax.ppermute(value, axis, [(i, i ^ mask) for i in range(size)])  91.2 us
    pallas_call x2, Pallas kernels, shards(): whole_call(lambda *refs: back_attend_body(base, *refs), outs, 'back_atten...  44.1 us
    pallas_call x11, Pallas kernels, product_sum(): pl.pallas_call(lambda *refs: product_body(runs, *refs), grid=(len(blocks)...  27 us
    pallas_call x2, Pallas kernels, shards(): whole_call(lambda *refs: back_mlp_body(base, *refs), outs, 'back_mlp', fu...  26.6 us
    pallas_call x2, Pallas kernels, forward_stage(): whole_call_smem(lambda *refs: up_body(base, *refs), 1, 9, outs, 'out_up',...  23 us
    unnamed x298, local copies, waits for them, and re-layouts  23 us
    pallas_call x1, Pallas kernels, shampoo(): pl.pallas_call(lambda *refs: shampoo_body(group, layout, *refs), grid=(co...  20.1 us
  transfers between devices with their start and end apart: 90, of which 28 were waited for; matrix products, arithmetic and copies ran while one was open for 16% of the time, Pallas kernels for 28%

profile of v3, /device:TPU:0, one launch (start us, length us, event | category | flops | bytes accessed | tf_op | source)
XLA Modules:
  0.0 597.1 jit_solution(11340643740426147232)
XLA Ops:
  2.7 5.7 prepare_tiles.1
  8.4 5.0 collective-permute-start.2
  14.0 2.5 constant_dynamic-slice_fusion.5
  27.0 2.9 collective-permute-start.5
  32.4 9.4 %collective-permute-done.1 = bf16[48,3456]{1,0:T(8,128)(2,1)} collective-permute-done((bf16[48,3456]{1,0:T(8,128)(2,1)S(1)}, bf16[48,3456]{1,0:T(8,128)(2,1)}, u32[]{:S(2)}, u32[]{:S(2)}) %collective-permute-start.1) | collective-permute-done | bytes 331808 | tf_op jit(solution)/shard_map/ppermute | solution.py:66
  46.1 2.5 collective-permute-start.10
  50.5 6.7 %collective-permute-done.10 = bf16[48,2688]{1,0:T(8,128)(2,1)S(1)} collective-permute-done((bf16[48,2688]{1,0:T(8,128)(2,1)S(1)}, bf16[48,2688]{1,0:T(8,128)(2,1)S(1)}, u32[]{:S(2)}, u32[]{:S(2)}) %collective-permute-start.10) | collective-permute-done | bytes 258080 | tf_op jit(solution)/shard_map/ppermute | solution.py:66
  57.2 11.1 %collective-permute-done.9 = bf16[48,2688]{1,0:T(8,128)(2,1)S(1)} collective-permute-done((bf16[48,2688]{1,0:T(8,128)(2,1)S(1)}, bf16[48,2688]{1,0:T(8,128)(2,1)S(1)}, u32[]{:S(2)}, u32[]{:S(2)}) %collective-permute-start.9) | collective-permute-done | bytes 258080 | tf_op jit(solution)/shard_map/ppermute | solution.py:66
  75.3 9.0 %collective-permute-done.15 = bf16[48,3840]{1,0:T(8,128)(2,1)S(1)} collective-permute-done((bf16[48,3840]{1,0:T(8,128)(2,1)S(1)}, bf16[48,3840]{1,0:T(8,128)(2,1)S(1)}, u32[]{:S(2)}, u32[]{:S(2)}) %collective-permute-start.15) | collective-permute-done | bytes 368672 | tf_op jit(solution)/shard_map/ppermute | solution.py:66
  84.3 16.9 %collective-permute-done.14 = bf16[48,3840]{1,0:T(8,128)(2,1)S(1)} collective-permute-done((bf16[48,3840]{1,0:T(8,128)(2,1)S(1)}, bf16[48,3840]{1,0:T(8,128)(2,1)S(1)}, u32[]{:S(2)}, u32[]{:S(2)}) %collective-permute-start.14) | collective-permute-done | bytes 368672 | tf_op jit(solution)/shard_map/ppermute | solution.py:66
  103.1 5.1 assemble.3
  117.3 13.3 %embed_qkv.1 = (f32[416,768]{1,0:T(8,128)}, bf16[416,768]{1,0:T(8,128)(2,1)}, bf16[416,1152]{1,0:T(8,128)(2,1)}, bf16[416,1152]{1,0:T(8,128)(2,1)}, bf16[416,384...) custom-call(s32[2]{0:T(128)S(1)} %pad_add_fusion.refs_0_.places, ...), custom_call_target="tpu_custom_call" | custom-call | flops 122683392 | bytes 65536 | tf_op jit(solution)/shard_map/embed_qkv/pallas_call | solution.py:780
  130.6 11.8 %out_up.2 = (f32[416,768]{1,0:T(8,128)}, bf16[416,768]{1,0:T(8,128)(2,1)}, bf16[416,1536]{1,0:T(8,128)(2,1)}, bf16[416,1536]{1,0:T(8,128)(2,1)}, f32[416,1536]{1...) custom-call(s32[2]{0:T(128)S(1)} %pad_add_fusion.refs_0_.places, ...), custom_call_target="tpu_custom_call" | custom-call | flops 153354240 | bytes 65536 | tf_op jit(solution)/shard_map/out_up/pallas_call | solution.py:787
  142.4 4.8 collective-permute-done.16.refs_4_.refs_3_
  147.3 4.8 assemble.4
  156.9 2.5 collective-permute-done.27.refs_9_.refs_8_
  162.0 14.8 %down_qkv.1 = (f32[416,768]{1,0:T(8,128)}, bf16[416,768]{1,0:T(8,128)(2,1)S(1)}, bf16[416,1152]{1,0:T(8,128)(2,1)}, bf16[416,1152]{1,0:T(8,128)(2,1)}, bf16[416,...) custom-call(s32[2]{0:T(128)S(1)} %pad_add_fusion.refs_0_.places, ...), custom_call_target="tpu_custom_call" | custom-call | flops 214695936 | bytes 65536 | tf_op jit(solution)/shard_map/down_qkv/pallas_call | solution.py:797
  176.8 5.5 assemble.5
  183.3 8.2 %collective-permute-done.28.refs_7_.refs_4_ = bf16[768,384]{1,0:T(8,128)(2,1)S(1)} collective-permute-done((bf16[768,384]{1,0:T(8,128)(2,1)S(1)}, bf16[768,384]{1,0:T(8,128)(2,1)S(1)}, u32[]{:S(2)}, u32[]{:S(2)}) %collective-permute-start.28) | collective-permute-done | bytes 589856 | tf_op jit(solution)/shard_map/ppermute | solution.py:66
  192.9 11.3 %out_up.3 = (f32[416,768]{1,0:T(8,128)}, bf16[416,768]{1,0:T(8,128)(2,1)}, bf16[416,1536]{1,0:T(8,128)(2,1)}, bf16[416,1536]{1,0:T(8,128)(2,1)}, f32[416,1536]{1...) custom-call(s32[2]{0:T(128)S(1)} %pad_add_fusion.refs_0_.places, ...), custom_call_target="tpu_custom_call" | custom-call | flops 153354240 | bytes 65536 | tf_op jit(solution)/shard_map/out_up/pallas_call | solution.py:787
  205.0 11.5 %down_head.1 = (bf16[416,768]{1,0:T(8,128)(2,1)}, bf16[416,384]{1,0:T(8,128)(2,1)S(1)}, bf16[416,384]{1,0:T(8,128)(2,1)}, f32[416,768]{1,0:T(8,128)}, bf16[416,7...) custom-call(s32[2]{0:T(128)S(1)} %pad_add_fusion.refs_0_.places, ...), custom_call_target="tpu_custom_call" | custom-call | flops 184025088 | bytes 65536 | tf_op jit(solution)/shard_map/down_head/pallas_call | solution.py:808
  219.9 13.2 %back_mlp.2 = (f32[416,768]{1,0:T(8,128)}, bf16[416,768]{1,0:T(8,128)(2,1)S(1)}, bf16[416,1536]{1,0:T(8,128)(2,1)}, bf16[416,1536]{1,0:T(8,128)(2,1)}, f32[8,768...) custom-call(f32[227,768]{1,0:T(8,128)} %fusion.5.vec.refs_1_.refs_2_.refs_0_, ...), custom_call_target="tpu_custom_call" | custom-call | flops 245366784 | bytes 65536 | tf_op jit(solution)/shard_map/back_mlp/pallas_call | solution.py:907
  234.6 3.7 product_sum.11
  242.4 3.9 product_sum.13
  250.5 21.6 %back_attend.2 = (f32[416,768]{1,0:T(8,128)}, bf16[416,768]{1,0:T(8,128)(2,1)S(1)}, bf16[416,1152]{1,0:T(8,128)(2,1)}, bf16[416,1152]{1,0:T(8,128)(2,1)}, f32[8,...) custom-call(f32[227,768]{1,0:T(8,128)} %fusion.5.vec.refs_1_.refs_2_.refs_0_, ...), custom_call_target="tpu_custom_call" | custom-call | flops 245366784 | bytes 65536 | tf_op jit(solution)/shard_map/back_attend/pallas_call | solution.py:929
  272.0 6.0 %collective-permute-done.36 = f16[400,1536]{1,0:T(8,128)(2,1)} collective-permute-done((f16[400,1536]{1,0:T(8,128)(2,1)S(1)}, f16[400,1536]{1,0:T(8,128)(2,1)}, u32[]{:S(2)}, u32[]{:S(2)}) %collective-permute-start.36) | collective-permute-done | bytes 1228832 | tf_op jit(solution)/shard_map/ppermute | solution.py:66
  278.0 5.8 collective-permute-done.35
  283.9 2.5 multiply_add_fusion
  300.4 7.0 %collective-permute-done.39 = f16[208,1536]{1,0:T(8,128)(2,1)S(1)} collective-permute-done((f16[208,1536]{1,0:T(8,128)(2,1)S(1)}, f16[208,1536]{1,0:T(8,128)(2,1)S(1)}, u32[]{:S(2)}, u32[]{:S(2)}) %collective-permute-start.39) | collective-permute-done | bytes 639008 | tf_op jit(solution)/shard_map/ppermute | solution.py:66
  316.4 13.4 %back_mlp.3 = (f32[416,768]{1,0:T(8,128)}, bf16[416,768]{1,0:T(8,128)(2,1)S(1)}, bf16[416,1536]{1,0:T(8,128)(2,1)}, bf16[416,1536]{1,0:T(8,128)(2,1)}, f32[8,768...) custom-call(f32[227,768]{1,0:T(8,128)} %fusion.5.vec.refs_1_.refs_2_.refs_0_, ...), custom_call_target="tpu_custom_call" | custom-call | flops 245366784 | bytes 65536 | tf_op jit(solution)/shard_map/back_mlp/pallas_call | solution.py:907
  344.1 3.7 product_sum.17
  349.7 3.9 product_sum.18
  353.8 2.7 collective-permute-done.45
  362.3 22.6 %back_attend.3 = (f32[416,768]{1,0:T(8,128)}, bf16[416,768]{1,0:T(8,128)(2,1)}, bf16[416,1152]{1,0:T(8,128)(2,1)}, bf16[416,1152]{1,0:T(8,128)(2,1)}, f32[8,768]...) custom-call(f32[227,768]{1,0:T(8,128)} %fusion.5.vec.refs_1_.refs_2_.refs_0_, ...), custom_call_target="tpu_custom_call" | custom-call | flops 245366784 | bytes 65536 | tf_op jit(solution)/shard_map/back_attend/pallas_call | solution.py:929
  384.9 2.7 multiply_reduce_fusion
  404.6 4.2 product_sum.19
  409.0 2.8 collective-permute-done.51
  425.0 12.5 %collective-permute-done.59 = f16[400,768]{1,0:T(8,128)(2,1)S(1)} collective-permute-done((f16[400,768]{1,0:T(8,128)(2,1)S(1)}, f16[400,768]{1,0:T(8,128)(2,1)S(1)}, u32[]{:S(2)}, u32[]{:S(2)}) %collective-permute-start.59) | collective-permute-done | bytes 614432 | tf_op jit(solution)/shard_map/ppermute | solution.py:66
  437.5 5.5 collective-permute-done.58
  458.8 5.3 collective-permute-done.65
  476.7 7.5 %collective-permute-done.67 = f32[32,768]{1,0:T(8,128)S(1)} collective-permute-done((f32[32,768]{1,0:T(8,128)S(1)}, f32[32,768]{1,0:T(8,128)S(1)}, u32[]{:S(2)}, u32[]{:S(2)}) %collective-permute-start.67) | collective-permute-done | bytes 98336 | tf_op jit(solution)/shard_map/ppermute | solution.py:66
  489.1 2.6 collective-permute-done.70
  495.6 12.5 %collective-permute-done.74 = f32[32,768]{1,0:T(8,128)S(1)} collective-permute-done((f32[32,768]{1,0:T(8,128)S(1)}, f32[32,768]{1,0:T(8,128)S(1)}, u32[]{:S(2)}, u32[]{:S(2)}) %collective-permute-start.74) | collective-permute-done | bytes 98336 | tf_op jit(solution)/shard_map/ppermute | solution.py:66
  545.9 2.5 collective-permute-done.82
  557.3 20.1 %shampoo.1 = (f32[48,96,96]{2,1,0:T(8,128)}, f32[48,96,96]{2,1,0:T(8,128)}, f32[48,96,96]{2,1,0:T(8,128)}, f32[48,96,96]{2,1,0:T(8,128)}, f32[48,96,96]{2,1,0:T(8,128)}) custom-call(s32[5,48]{1,0:T(8,128)S(1)} %stack.34.refs_0_, bf16[4,48,9984]{2,1,0:T(8,128)(2,1)} %get-tuple-element.610.refs_1_, f32[64,4992]{1,0:T(8,128)} %copy-done.70, ...), custom_call_target="tpu_custom_call" | custom-call | flops 127401984 | bytes 65536 | tf_op jit(solution)/shard_map/shampoo/pallas_call | solution.py:596
  578.7 3.4 multiply_bitcast_fusion
  582.1 3.7 fusion.1
  592.3 3.5 multiply_subtract_fusion
  (733 shorter events, 221.8 us)
Async XLA Ops:
  8.4 24.1 %collective-permute-start.2 = (bf16[48,3456]{1,0:T(8,128)(2,1)S(1)}, bf16[48,3456]{1,0:T(8,128)(2,1)}, u32[]{:S(2)}, u32[]{:S(2)}) collective-permute-start(bf16[48,3456]{1,0:T(8,128)(2,1)S(1)} %get-tuple-element.316), channel_id=1, source_target_pairs={{0,3},{1,2},{2,1},{3,0},{4,7},{5,6},{6,5},{7,4},{8,11},{9,10},{10,... | collective-permute-start | bytes 995336 | tf_op jit(solution)/shard_map/ppermute | solution.py:66
  13.4 28.4 %collective-permute-start.1 = (bf16[48,3456]{1,0:T(8,128)(2,1)S(1)}, bf16[48,3456]{1,0:T(8,128)(2,1)}, u32[]{:S(2)}, u32[]{:S(2)}) collective-permute-start(bf16[48,3456]{1,0:T(8,128)(2,1)S(1)} %get-tuple-element.316), channel_id=1, source_target_pairs={{0,2},{1,3},{2,0},{3,1},{4,6},{5,7},{6,4},{7,5},{8,10},{9,11},{10,... | collective-permute-start | bytes 995336 | tf_op jit(solution)/shard_map/ppermute | solution.py:66
  13.4 28.4 %collective-permute-start = (bf16[48,3456]{1,0:T(8,128)(2,1)S(1)}, bf16[48,3456]{1,0:T(8,128)(2,1)}, u32[]{:S(2)}, u32[]{:S(2)}) collective-permute-start(bf16[48,3456]{1,0:T(8,128)(2,1)S(1)} %get-tuple-element.316), channel_id=1, source_target_pairs={{0,1},{1,0},{2,3},{3,2},{4,5},{5,4},{6,7},{7,6},{8,9},{9,8},{10,11... | collective-permute-start | bytes 995336 | tf_op jit(solution)/shard_map/ppermute | solution.py:66
  43.1 25.3 %collective-permute-start.6 = (bf16[144,3456]{1,0:T(8,128)(2,1)S(1)}, bf16[144,3456]{1,0:T(8,128)(2,1)S(1)}, u32[]{:S(2)}, u32[]{:S(2)}) collective-permute-start(bf16[144,3456]{1,0:T(8,128)(2,1)S(1)} %pad_maximum_fusion.9.refs_1_), channel_id=1, source_target_pairs={{0,8},{8,0},{16,24},{24,16},{1,9},{9,1},{17,25},{25,17},{2,10},{10... | collective-permute-start | bytes 2985992 | tf_op jit(solution)/shard_map/ppermute | solution.py:66
  44.6 23.8 %collective-permute-start.7 = (bf16[144,3456]{1,0:T(8,128)(2,1)S(1)}, bf16[144,3456]{1,0:T(8,128)(2,1)S(1)}, u32[]{:S(2)}, u32[]{:S(2)}) collective-permute-start(bf16[144,3456]{1,0:T(8,128)(2,1)S(1)} %pad_maximum_fusion.9.refs_1_), channel_id=1, source_target_pairs={{0,16},{8,24},{16,0},{24,8},{1,17},{9,25},{17,1},{25,9},{2,18},{10... | collective-permute-start | bytes 2985992 | tf_op jit(solution)/shard_map/ppermute | solution.py:66
  48.6 19.7 %collective-permute-start.9 = (bf16[48,2688]{1,0:T(8,128)(2,1)S(1)}, bf16[48,2688]{1,0:T(8,128)(2,1)S(1)}, u32[]{:S(2)}, u32[]{:S(2)}) collective-permute-start(bf16[48,2688]{1,0:T(8,128)(2,1)S(1)} %get-tuple-element.323), channel_id=1, source_target_pairs={{0,2},{1,3},{2,0},{3,1},{4,6},{5,7},{6,4},{7,5},{8,10},{9,11},{10,... | collective-permute-start | bytes 774152 | tf_op jit(solution)/shard_map/ppermute | solution.py:66
  48.6 19.7 %collective-permute-start.8 = (bf16[48,2688]{1,0:T(8,128)(2,1)S(1)}, bf16[48,2688]{1,0:T(8,128)(2,1)S(1)}, u32[]{:S(2)}, u32[]{:S(2)}) collective-permute-start(bf16[48,2688]{1,0:T(8,128)(2,1)S(1)} %get-tuple-element.323), channel_id=1, source_target_pairs={{0,1},{1,0},{2,3},{3,2},{4,5},{5,4},{6,7},{7,6},{8,9},{9,8},{10,11... | collective-permute-start | bytes 774152 | tf_op jit(solution)/shard_map/ppermute | solution.py:66
  69.7 31.6 %collective-permute-start.12 = (bf16[144,4480]{1,0:T(8,128)(2,1)S(1)}, bf16[144,4480]{1,0:T(8,128)(2,1)S(1)}, u32[]{:S(2)}, u32[]{:S(2)}) collective-permute-start(bf16[144,4480]{1,0:T(8,128)(2,1)S(1)} %pad_maximum_fusion.4), channel_id=1, source_target_pairs={{0,8},{8,0},{16,24},{24,16},{1,9},{9,1},{17,25},{25,17},{2,10},{10... | collective-permute-start | bytes 3870728 | tf_op jit(solution)/shard_map/ppermute | solution.py:66
  70.3 30.9 %collective-permute-start.11 = (bf16[144,4352]{1,0:T(8,128)(2,1)S(1)}, bf16[144,4352]{1,0:T(8,128)(2,1)S(1)}, u32[]{:S(2)}, u32[]{:S(2)}) collective-permute-start(bf16[144,4352]{1,0:T(8,128)(2,1)S(1)} %pad_maximum_fusion.5), channel_id=1, source_target_pairs={{0,16},{8,24},{16,0},{24,8},{1,17},{9,25},{17,1},{25,9},{2,18},{10... | collective-permute-start | bytes 3760136 | tf_op jit(solution)/shard_map/ppermute | solution.py:66
  73.0 28.2 %collective-permute-start.14 = (bf16[48,3840]{1,0:T(8,128)(2,1)S(1)}, bf16[48,3840]{1,0:T(8,128)(2,1)S(1)}, u32[]{:S(2)}, u32[]{:S(2)}) collective-permute-start(bf16[48,3840]{1,0:T(8,128)(2,1)S(1)} %get-tuple-element.329), channel_id=1, source_target_pairs={{0,2},{1,3},{2,0},{3,1},{4,6},{5,7},{6,4},{7,5},{8,10},{9,11},{10,... | collective-permute-start | bytes 1105928 | tf_op jit(solution)/shard_map/ppermute | solution.py:66
  73.0 28.2 %collective-permute-start.13 = (bf16[48,3840]{1,0:T(8,128)(2,1)S(1)}, bf16[48,3840]{1,0:T(8,128)(2,1)S(1)}, u32[]{:S(2)}, u32[]{:S(2)}) collective-permute-start(bf16[48,3840]{1,0:T(8,128)(2,1)S(1)} %get-tuple-element.329), channel_id=1, source_target_pairs={{0,1},{1,0},{2,3},{3,2},{4,5},{5,4},{6,7},{7,6},{8,9},{9,8},{10,11... | collective-permute-start | bytes 1105928 | tf_op jit(solution)/shard_map/ppermute | solution.py:66
  108.2 22.4 %collective-permute-start.21 = (bf16[768,1536]{1,0:T(8,128)(2,1)}, bf16[768,1536]{1,0:T(8,128)(2,1)}, u32[]{:S(2)}, u32[]{:S(2)}) collective-permute-start(bf16[768,1536]{1,0:T(8,128)(2,1)} %get-tuple-element.352.refs_8_.refs_7_), channel_id=1, source_target_pairs={{0,4},{4,0},{1,5},{5,1},{2,6},{6,2},{3,7},{7,3},{8,12},{12,8},{9,1... | collective-permute-start | bytes 7077896 | tf_op jit(solution)/shard_map/ppermute | solution.py:66
  109.5 37.7 %collective-permute-start.17 = (bf16[144,5248]{1,0:T(8,128)(2,1)}, bf16[144,5248]{1,0:T(8,128)(2,1)}, u32[]{:S(2)}, u32[]{:S(2)}) collective-permute-start(bf16[144,5248]{1,0:T(8,128)(2,1)} %pad_maximum_fusion.2), channel_id=1, source_target_pairs={{0,8},{8,0},{16,24},{24,16},{1,9},{9,1},{17,25},{25,17},{2,10},{10... | collective-permute-start | bytes 4534280 | tf_op jit(solution)/shard_map/ppermute | solution.py:66
  112.4 34.8 %collective-permute-start.16 = (bf16[144,5120]{1,0:T(8,128)(2,1)}, bf16[144,5120]{1,0:T(8,128)(2,1)}, u32[]{:S(2)}, u32[]{:S(2)}) collective-permute-start(bf16[144,5120]{1,0:T(8,128)(2,1)} %pad_maximum_fusion.3), channel_id=1, source_target_pairs={{0,16},{8,24},{16,0},{24,8},{1,17},{9,25},{17,1},{25,9},{2,18},{10... | collective-permute-start | bytes 4423688 | tf_op jit(solution)/shard_map/ppermute | solution.py:66
  152.6 24.3 %collective-permute-start.25 = (bf16[416,2304]{1,0:T(8,128)(2,1)}, bf16[416,2304]{1,0:T(8,128)(2,1)S(1)}, u32[]{:S(2)}, u32[]{:S(2)}) collective-permute-start(bf16[416,2304]{1,0:T(8,128)(2,1)} %get-tuple-element.374), channel_id=1, source_target_pairs={{0,4},{4,0},{1,5},{5,1},{2,6},{6,2},{3,7},{7,3},{8,12},{12,8},{9,1... | collective-permute-start | bytes 5750792 | tf_op jit(solution)/shard_map/ppermute | solution.py:66
  152.6 24.2 %collective-permute-start.24 = (bf16[416,1152]{1,0:T(8,128)(2,1)}, bf16[416,1152]{1,0:T(8,128)(2,1)S(1)}, u32[]{:S(2)}, u32[]{:S(2)}) collective-permute-start(bf16[416,1152]{1,0:T(8,128)(2,1)} %get-tuple-element.367), channel_id=1, source_target_pairs={{0,4},{4,0},{1,5},{5,1},{2,6},{6,2},{3,7},{7,3},{8,12},{12,8},{9,1... | collective-permute-start | bytes 2875400 | tf_op jit(solution)/shard_map/ppermute | solution.py:66
  154.2 22.6 %collective-permute-start.22 = (bf16[144,1920]{1,0:T(8,128)(2,1)S(1)}, bf16[144,1920]{1,0:T(8,128)(2,1)S(1)}, u32[]{:S(2)}, u32[]{:S(2)}) collective-permute-start(bf16[144,1920]{1,0:T(8,128)(2,1)S(1)} %slice.385), channel_id=1, source_target_pairs={{0,16},{8,24},{16,0},{24,8},{1,17},{9,25},{17,1},{25,9},{2,18},{10... | collective-permute-start | bytes 1658888 | tf_op jit(solution)/shard_map/ppermute | solution.py:66
  182.4 21.8 %collective-permute-start.30 = (bf16[768,1536]{1,0:T(8,128)(2,1)}, bf16[768,1536]{1,0:T(8,128)(2,1)}, u32[]{:S(2)}, u32[]{:S(2)}) collective-permute-start(bf16[768,1536]{1,0:T(8,128)(2,1)} %get-tuple-element.403.refs_7_.refs_3_), channel_id=1, source_target_pairs={{0,4},{4,0},{1,5},{5,1},{2,6},{6,2},{3,7},{7,3},{8,12},{12,8},{9,1... | collective-permute-start | bytes 7077896 | tf_op jit(solution)/shard_map/ppermute | solution.py:66
  182.9 21.3 %collective-permute-start.31 = (bf16[768,384]{1,0:T(8,128)(2,1)}, bf16[768,384]{1,0:T(8,128)(2,1)S(1)}, u32[]{:S(2)}, u32[]{:S(2)}) collective-permute-start(bf16[768,384]{1,0:T(8,128)(2,1)} %get-tuple-element.404.refs_9_), channel_id=1, source_target_pairs={{0,4},{4,0},{1,5},{5,1},{2,6},{6,2},{3,7},{7,3},{8,12},{12,8},{9,1... | collective-permute-start | bytes 1769480 | tf_op jit(solution)/shard_map/ppermute | solution.py:66
  247.7 36.1 %collective-permute-start.35 = (f16[400,1920]{1,0:T(8,128)(2,1)}, f16[400,1920]{1,0:T(8,128)(2,1)S(1)}, u32[]{:S(2)}, u32[]{:S(2)}) collective-permute-start(f16[400,1920]{1,0:T(8,128)(2,1)} %pad_maximum_fusion.1), channel_id=1, source_target_pairs={{0,8},{8,0},{16,24},{24,16},{1,9},{9,1},{17,25},{25,17},{2,10},{10... | collective-permute-start | bytes 4608008 | tf_op jit(solution)/shard_map/ppermute | solution.py:66
  248.9 29.1 %collective-permute-start.36 = (f16[400,1536]{1,0:T(8,128)(2,1)S(1)}, f16[400,1536]{1,0:T(8,128)(2,1)}, u32[]{:S(2)}, u32[]{:S(2)}) collective-permute-start(f16[400,1536]{1,0:T(8,128)(2,1)S(1)} %convert_element_type.318), channel_id=1, source_target_pairs={{0,16},{8,24},{16,0},{24,8},{1,17},{9,25},{17,1},{25,9},{2,18},{10... | collective-permute-start | bytes 3686408 | tf_op jit(solution)/shard_map/ppermute | solution.py:66
  250.4 41.9 %collective-permute-start.40 = (bf16[416,1152]{1,0:T(8,128)(2,1)S(1)}, bf16[416,1152]{1,0:T(8,128)(2,1)S(1)}, u32[]{:S(2)}, u32[]{:S(2)}) collective-permute-start(bf16[416,1152]{1,0:T(8,128)(2,1)S(1)} %copy-done.140), channel_id=1, source_target_pairs={{0,4},{4,0},{1,5},{5,1},{2,6},{6,2},{3,7},{7,3},{8,12},{12,8},{9,1... | collective-permute-start | bytes 2875400 | tf_op jit(solution)/shard_map/ppermute | solution.py:66
  286.7 20.8 %collective-permute-start.38 = (f16[208,1920]{1,0:T(8,128)(2,1)S(1)}, f16[208,1920]{1,0:T(8,128)(2,1)S(1)}, u32[]{:S(2)}, u32[]{:S(2)}) collective-permute-start(f16[208,1920]{1,0:T(8,128)(2,1)S(1)} %pad_maximum_fusion.10), channel_id=1, source_target_pairs={{0,16},{8,24},{16,0},{24,8},{1,17},{9,25},{17,1},{25,9},{2,18},{10... | collective-permute-start | bytes 2396168 | tf_op jit(solution)/shard_map/ppermute | solution.py:66
  311.1 19.9 %collective-permute-start.41 = (f16[112,3456]{1,0:T(8,128)(2,1)}, f16[112,3456]{1,0:T(8,128)(2,1)}, u32[]{:S(2)}, u32[]{:S(2)}) collective-permute-start(f16[112,3456]{1,0:T(8,128)(2,1)} %pad_maximum_fusion.12), channel_id=1, source_target_pairs={{0,1},{1,0},{2,3},{3,2},{4,5},{5,4},{6,7},{7,6},{8,9},{9,8},{10,11... | collective-permute-start | bytes 2322440 | tf_op jit(solution)/shard_map/ppermute | solution.py:66
  311.1 19.9 %collective-permute-start.42 = (f16[400,768]{1,0:T(8,128)(2,1)}, f16[400,768]{1,0:T(8,128)(2,1)}, u32[]{:S(2)}, u32[]{:S(2)}) collective-permute-start(f16[400,768]{1,0:T(8,128)(2,1)} %convert_element_type.323), channel_id=1, source_target_pairs={{0,8},{8,0},{16,24},{24,16},{1,9},{9,1},{17,25},{25,17},{2,10},{10... | collective-permute-start | bytes 1843208 | tf_op jit(solution)/shard_map/ppermute | solution.py:66
  333.5 22.9 %collective-permute-start.45 = (f16[64,3456]{1,0:T(8,128)(2,1)S(1)}, f16[64,3456]{1,0:T(8,128)(2,1)S(1)}, u32[]{:S(2)}, u32[]{:S(2)}) collective-permute-start(f16[64,3456]{1,0:T(8,128)(2,1)S(1)} %pad_maximum_fusion.23), channel_id=1, source_target_pairs={{0,2},{1,3},{2,0},{3,1},{4,6},{5,7},{6,4},{7,5},{8,10},{9,11},{10,... | collective-permute-start | bytes 1327112 | tf_op jit(solution)/shard_map/ppermute | solution.py:66
  356.6 31.0 %collective-permute-start.49 = (f16[400,1536]{1,0:T(8,128)(2,1)}, f16[400,1536]{1,0:T(8,128)(2,1)}, u32[]{:S(2)}, u32[]{:S(2)}) collective-permute-start(f16[400,1536]{1,0:T(8,128)(2,1)} %convert_element_type.338), channel_id=1, source_target_pairs={{0,8},{8,0},{16,24},{24,16},{1,9},{9,1},{17,25},{25,17},{2,10},{10... | collective-permute-start | bytes 3686408 | tf_op jit(solution)/shard_map/ppermute | solution.py:66
  357.3 30.3 %collective-permute-start.50 = (f16[400,1536]{1,0:T(8,128)(2,1)S(1)}, f16[400,1536]{1,0:T(8,128)(2,1)}, u32[]{:S(2)}, u32[]{:S(2)}) collective-permute-start(f16[400,1536]{1,0:T(8,128)(2,1)S(1)} %convert_element_type.339), channel_id=1, source_target_pairs={{0,16},{8,24},{16,0},{24,8},{1,17},{9,25},{17,1},{25,9},{2,18},{10... | collective-permute-start | bytes 3686408 | tf_op jit(solution)/shard_map/ppermute | solution.py:66
  359.7 27.9 %collective-permute-start.48 = (f16[112,1536]{1,0:T(8,128)(2,1)}, f16[112,1536]{1,0:T(8,128)(2,1)}, u32[]{:S(2)}, u32[]{:S(2)}) collective-permute-start(f16[112,1536]{1,0:T(8,128)(2,1)} %pad_maximum_fusion.29), channel_id=1, source_target_pairs={{0,1},{1,0},{2,3},{3,2},{4,5},{5,4},{6,7},{7,6},{8,9},{9,8},{10,11... | collective-permute-start | bytes 1032200 | tf_op jit(solution)/shard_map/ppermute | solution.py:66
  392.3 19.6 %collective-permute-start.52 = (f16[208,1536]{1,0:T(8,128)(2,1)S(1)}, f16[208,1536]{1,0:T(8,128)(2,1)S(1)}, u32[]{:S(2)}, u32[]{:S(2)}) collective-permute-start(f16[208,1536]{1,0:T(8,128)(2,1)S(1)} %pad_maximum_fusion.16), channel_id=1, source_target_pairs={{0,16},{8,24},{16,0},{24,8},{1,17},{9,25},{17,1},{25,9},{2,18},{10... | collective-permute-start | bytes 1916936 | tf_op jit(solution)/shard_map/ppermute | solution.py:66
  418.4 19.1 %collective-permute-start.57 = (f16[112,3072]{1,0:T(8,128)(2,1)S(1)}, f16[112,3072]{1,0:T(8,128)(2,1)S(1)}, u32[]{:S(2)}, u32[]{:S(2)}) collective-permute-start(f16[112,3072]{1,0:T(8,128)(2,1)S(1)} %pad_maximum_fusion.13), channel_id=1, source_target_pairs={{0,1},{1,0},{2,3},{3,2},{4,5},{5,4},{6,7},{7,6},{8,9},{9,8},{10,11... | collective-permute-start | bytes 2064392 | tf_op jit(solution)/shard_map/ppermute | solution.py:66
  420.5 22.6 %collective-permute-start.58 = (f16[400,1152]{1,0:T(8,128)(2,1)S(1)}, f16[400,1152]{1,0:T(8,128)(2,1)S(1)}, u32[]{:S(2)}, u32[]{:S(2)}) collective-permute-start(f16[400,1152]{1,0:T(8,128)(2,1)S(1)} %convert_element_type.354), channel_id=1, source_target_pairs={{0,8},{8,0},{16,24},{24,16},{1,9},{9,1},{17,25},{25,17},{2,10},{10... | collective-permute-start | bytes 2764808 | tf_op jit(solution)/shard_map/ppermute | solution.py:66
  448.3 19.2 %collective-permute-start.63 = (f16[64,3072]{1,0:T(8,128)(2,1)}, f16[64,3072]{1,0:T(8,128)(2,1)}, u32[]{:S(2)}, u32[]{:S(2)}) collective-permute-start(f16[64,3072]{1,0:T(8,128)(2,1)} %pad_maximum_fusion.25), channel_id=1, source_target_pairs={{0,2},{1,3},{2,0},{3,1},{4,6},{5,7},{6,4},{7,5},{8,10},{9,11},{10,... | collective-permute-start | bytes 1179656 | tf_op jit(solution)/shard_map/ppermute | solution.py:66
  456.2 29.3 %collective-permute-start.68 = (f16[64,4992]{1,0:T(8,128)(2,1)S(1)}, f16[64,4992]{1,0:T(8,128)(2,1)S(1)}, u32[]{:S(2)}, u32[]{:S(2)}) collective-permute-start(f16[64,4992]{1,0:T(8,128)(2,1)S(1)} %pad_maximum_fusion.18), channel_id=1, source_target_pairs={{0,8},{8,0},{16,24},{24,16},{1,9},{9,1},{17,25},{25,17},{2,10},{10... | collective-permute-start | bytes 1916936 | tf_op jit(solution)/shard_map/ppermute | solution.py:66
  456.9 29.9 %collective-permute-start.69 = (f16[64,4992]{1,0:T(8,128)(2,1)S(1)}, f16[64,4992]{1,0:T(8,128)(2,1)S(1)}, u32[]{:S(2)}, u32[]{:S(2)}) collective-permute-start(f16[64,4992]{1,0:T(8,128)(2,1)S(1)} %pad_maximum_fusion.18), channel_id=1, source_target_pairs={{0,16},{8,24},{16,0},{24,8},{1,17},{9,25},{17,1},{25,9},{2,18},{10... | collective-permute-start | bytes 1916936 | tf_op jit(solution)/shard_map/ppermute | solution.py:66
  464.0 27.7 %collective-permute-start.70 = (f16[64,4992]{1,0:T(8,128)(2,1)S(1)}, f16[64,4992]{1,0:T(8,128)(2,1)S(1)}, u32[]{:S(2)}, u32[]{:S(2)}) collective-permute-start(f16[64,4992]{1,0:T(8,128)(2,1)S(1)} %pad_maximum_fusion.18), channel_id=1, source_target_pairs={{0,24},{8,16},{16,8},{24,0},{1,25},{9,17},{17,9},{25,1},{2,26},{10... | collective-permute-start | bytes 1916936 | tf_op jit(solution)/shard_map/ppermute | solution.py:66
  471.0 20.8 %collective-permute-start.71 = (f16[112,1920]{1,0:T(8,128)(2,1)S(1)}, f16[112,1920]{1,0:T(8,128)(2,1)S(1)}, u32[]{:S(2)}, u32[]{:S(2)}) collective-permute-start(f16[112,1920]{1,0:T(8,128)(2,1)S(1)} %pad_maximum_fusion.24), channel_id=1, source_target_pairs={{0,1},{1,0},{2,3},{3,2},{4,5},{5,4},{6,7},{7,6},{8,9},{9,8},{10,11... | collective-permute-start | bytes 1290248 | tf_op jit(solution)/shard_map/ppermute | solution.py:66
  484.1 37.6 %collective-permute-start.75 = (f16[64,3072]{1,0:T(8,128)(2,1)}, f16[64,3072]{1,0:T(8,128)(2,1)}, u32[]{:S(2)}, u32[]{:S(2)}) collective-permute-start(f16[64,3072]{1,0:T(8,128)(2,1)} %pad_maximum_fusion.27), channel_id=1, source_target_pairs={{0,8},{8,0},{16,24},{24,16},{1,9},{9,1},{17,25},{25,17},{2,10},{10... | collective-permute-start | bytes 1179656 | tf_op jit(solution)/shard_map/ppermute | solution.py:66
  485.5 36.3 %collective-permute-start.76 = (f16[64,3072]{1,0:T(8,128)(2,1)}, f16[64,3072]{1,0:T(8,128)(2,1)}, u32[]{:S(2)}, u32[]{:S(2)}) collective-permute-start(f16[64,3072]{1,0:T(8,128)(2,1)} %pad_maximum_fusion.27), channel_id=1, source_target_pairs={{0,16},{8,24},{16,0},{24,8},{1,17},{9,25},{17,1},{25,9},{2,18},{10... | collective-permute-start | bytes 1179656 | tf_op jit(solution)/shard_map/ppermute | solution.py:66
  486.8 34.9 %collective-permute-start.77 = (f16[64,3072]{1,0:T(8,128)(2,1)}, f16[64,3072]{1,0:T(8,128)(2,1)}, u32[]{:S(2)}, u32[]{:S(2)}) collective-permute-start(f16[64,3072]{1,0:T(8,128)(2,1)} %pad_maximum_fusion.27), channel_id=1, source_target_pairs={{0,24},{8,16},{16,8},{24,0},{1,25},{9,17},{17,9},{25,1},{2,26},{10... | collective-permute-start | bytes 1179656 | tf_op jit(solution)/shard_map/ppermute | solution.py:66
  493.8 21.5 %collective-permute-start.73 = (f32[32,768]{1,0:T(8,128)S(1)}, f32[32,768]{1,0:T(8,128)}, u32[]{:S(2)}, u32[]{:S(2)}) collective-permute-start(f32[32,768]{1,0:T(8,128)S(1)} %add.991), channel_id=1, source_target_pairs={{0,16},{8,24},{16,0},{24,8},{1,17},{9,25},{17,1},{25,9},{2,18},{10... | collective-permute-start | bytes 294920 | tf_op jit(solution)/shard_map/ppermute | solution.py:66
  523.9 28.0 %collective-permute-start.83 = (f16[64,1920]{1,0:T(8,128)(2,1)S(1)}, f16[64,1920]{1,0:T(8,128)(2,1)S(1)}, u32[]{:S(2)}, u32[]{:S(2)}) collective-permute-start(f16[64,1920]{1,0:T(8,128)(2,1)S(1)} %pad_maximum_fusion.35), channel_id=1, source_target_pairs={{0,8},{8,0},{16,24},{24,16},{1,9},{9,1},{17,25},{25,17},{2,10},{10... | collective-permute-start | bytes 737288 | tf_op jit(solution)/shard_map/ppermute | solution.py:66
  525.3 26.6 %collective-permute-start.84 = (f16[64,1920]{1,0:T(8,128)(2,1)S(1)}, f16[64,1920]{1,0:T(8,128)(2,1)S(1)}, u32[]{:S(2)}, u32[]{:S(2)}) collective-permute-start(f16[64,1920]{1,0:T(8,128)(2,1)S(1)} %pad_maximum_fusion.35), channel_id=1, source_target_pairs={{0,16},{8,24},{16,0},{24,8},{1,17},{9,25},{17,1},{25,9},{2,18},{10... | collective-permute-start | bytes 737288 | tf_op jit(solution)/shard_map/ppermute | solution.py:66
  526.5 25.4 %collective-permute-start.85 = (f16[64,1920]{1,0:T(8,128)(2,1)S(1)}, f16[64,1920]{1,0:T(8,128)(2,1)}, u32[]{:S(2)}, u32[]{:S(2)}) collective-permute-start(f16[64,1920]{1,0:T(8,128)(2,1)S(1)} %pad_maximum_fusion.35), channel_id=1, source_target_pairs={{0,24},{8,16},{16,8},{24,0},{1,25},{9,17},{17,9},{25,1},{2,26},{10... | collective-permute-start | bytes 737288 | tf_op jit(solution)/shard_map/ppermute | solution.py:66
  537.3 54.9 %collective-permute-start.89 = (f32[128,768]{1,0:T(8,128)}, f32[128,768]{1,0:T(8,128)}, u32[]{:S(2)}, u32[]{:S(2)}) collective-permute-start(f32[128,768]{1,0:T(8,128)} %pad_maximum_fusion.26), channel_id=1, source_target_pairs={{0,4},{4,0},{1,5},{5,1},{2,6},{6,2},{3,7},{7,3},{8,12},{12,8},{9,1... | collective-permute-start | bytes 1179656 | tf_op jit(solution)/shard_map/ppermute | solution.py:66
  551.9 25.4 %collective-permute-start.87 = (f32[2]{0:T(128)S(1)}, f32[2]{0:T(128)S(1)}, u32[]{:S(2)}, u32[]{:S(2)}) collective-permute-start(f32[2]{0:T(128)S(1)} %add_add_fusion.2), channel_id=1, source_target_pairs={{0,2},{1,3},{2,0},{3,1},{4,6},{5,7},{6,4},{7,5},{8,10},{9,11},{10,... | collective-permute-start | bytes 32 | tf_op jit(solution)/shard_map/ppermute | solution.py:66
  553.0 24.4 %collective-permute-start.88 = (f32[2]{0:T(128)S(1)}, f32[2]{0:T(128)S(1)}, u32[]{:S(2)}, u32[]{:S(2)}) collective-permute-start(f32[2]{0:T(128)S(1)} %add_add_fusion.2), channel_id=1, source_target_pairs={{0,3},{1,2},{2,1},{3,0},{4,7},{5,6},{6,5},{7,4},{8,11},{9,10},{10,... | collective-permute-start | bytes 32 | tf_op jit(solution)/shard_map/ppermute | solution.py:66
  555.0 22.3 %collective-permute-start.86 = (f32[2]{0:T(128)S(1)}, f32[2]{0:T(128)S(1)}, u32[]{:S(2)}, u32[]{:S(2)}) collective-permute-start(f32[2]{0:T(128)S(1)} %add_add_fusion.2), channel_id=1, source_target_pairs={{0,1},{1,0},{2,3},{3,2},{4,5},{5,4},{6,7},{7,6},{8,9},{9,8},{10,11... | collective-permute-start | bytes 32 | tf_op jit(solution)/shard_map/ppermute | solution.py:66
  (186 other events, 1830.2 us)

commit v4 on v3

--- a/solution.py
+++ b/solution.py
@@ -322,11 +322,6 @@
     class_sum = rows_sum(jnp.where(flags[:, 0:1] > 0, grad, 0.0))
     mask_sum = rows_sum(jnp.where(flags[:, 1:2] > 0, grad, 0.0))
     put_rows(wide, [class_sum, mask_sum, rows_sum(low)])
-
-
-def four(value, axis):
-    got = [swap(value, axis, k) for k in (1, 2, 3)]
-    return (value + got[0]) + (got[1] + got[2])
 
 
 def tie(*trees):
@@ -1013,18 +1008,16 @@
     square = jnp.sum(value * value) / lax.axis_size("col")
     value = jnp.concatenate([value] + [swap(value, "dp", k) for k in (1, 2, 3)], axis=0)
     value, middle[0], early[0] = step_on((value, middle[0], early[0]), [])
-    decode_all(middle)
     late = spread_done(len(groups))
     spreads = [early, middle, late]
     copies = max(1, data_count // 4)
     square = (square + sum(jnp.sum(g.keep * g.keep) for g, _ in groups)) / copies
-    pair = butterfly(jnp.stack([square, values["loss"][0, 0]]), ("row",))
-    pair = four(pair, "dp")
-    for mask in bits_of("dp")[2:]:
-        pair = pair + swap(pair, "dp", mask)
-    pair, late[0], middle[0] = tie(pair, late[0], middle[0])
+    pair = butterfly(jnp.stack([square, values["loss"][0, 0]]), ("row", "dp"))
+    pair, middle[0] = tie(pair, middle[0])
+    decode_all(middle)
+    late[0], middle[0] = tie(late[0], middle[0])
     decode_all(late)
-    pair = four(pair, "col")
+    pair = butterfly(pair, ("col",))
     value = jnp.concatenate([value, across_core(value)], axis=0)
     spot = jnp.arange(rows_all)
     native = (

time: 608 us -> 605 us (level)
    ppermute x90 -> x88, starting transfers between devices: 91.2 us -> 88.3 us  [swap(): return lax.ppermute(value, axis, [(i, i ^ mask) for i in range(size)])]
    ppermute x90 -> x88, waiting for transfers between devices: 154 us -> 153 us  [swap(): return lax.ppermute(value, axis, [(i, i ^ mask) for i in range(size)])]
    unnamed x298 -> x306, local copies, waits for them, and re-layouts: 23 us -> 23.7 us
  transfers between devices with their start and end apart: 90 -> 88, of which waited for: 28 -> 27; matrix products, arithmetic and copies ran while one was open for 16% -> 16% of each run, Pallas kernels for 28% -> 28%
where the time goes in v4:
time: 605 us; the launch traced here: 594 us
  Pallas kernels  204 us (34%)
  waiting for transfers between devices  153 us (25%)
  other arithmetic  93.9 us (16%)
  starting transfers between devices  88.3 us (15%)
  local copies, waits for them, and re-layouts  35.4 us (6%)
  between operations  11.5 us (2%)
  matrix products  8.66 us (1%)
    ppermute x88, waiting for transfers between devices, swap(): return lax.ppermute(value, axis, [(i, i ^ mask) for i in range(size)])  153 us
    ppermute x88, starting transfers between devices, swap(): return lax.ppermute(value, axis, [(i, i ^ mask) for i in range(size)])  88.3 us
    pallas_call x2, Pallas kernels, shards(): whole_call(lambda *refs: back_attend_body(base, *refs), outs, 'back_atten...  44.1 us
    pallas_call x11, Pallas kernels, product_sum(): pl.pallas_call(lambda *refs: product_body(runs, *refs), grid=(len(blocks)...  26.9 us
    pallas_call x2, Pallas kernels, shards(): whole_call(lambda *refs: back_mlp_body(base, *refs), outs, 'back_mlp', fu...  26.6 us
    unnamed x306, local copies, waits for them, and re-layouts  23.7 us
    pallas_call x2, Pallas kernels, forward_stage(): whole_call_smem(lambda *refs: up_body(base, *refs), 1, 9, outs, 'out_up',...  23 us
    pallas_call x1, Pallas kernels, shampoo(): pl.pallas_call(lambda *refs: shampoo_body(group, layout, *refs), grid=(co...  20.1 us
  transfers between devices with their start and end apart: 88, of which 27 were waited for; matrix products, arithmetic and copies ran while one was open for 16% of the time, Pallas kernels for 28%

profile of v4, /device:TPU:0, one launch (start us, length us, event | category | flops | bytes accessed | tf_op | source)
XLA Modules:
  0.0 594.3 jit_solution(930006682271523700)
XLA Ops:
  2.7 5.7 prepare_tiles.1
  8.4 5.0 collective-permute-start.2
  14.0 2.5 constant_dynamic-slice_fusion.5
  26.9 2.9 collective-permute-start.5
  32.3 9.5 %collective-permute-done.1 = bf16[48,3456]{1,0:T(8,128)(2,1)} collective-permute-done((bf16[48,3456]{1,0:T(8,128)(2,1)S(1)}, bf16[48,3456]{1,0:T(8,128)(2,1)}, u32[]{:S(2)}, u32[]{:S(2)}) %collective-permute-start.1) | collective-permute-done | bytes 331808 | tf_op jit(solution)/shard_map/ppermute | solution.py:66
  46.1 2.5 collective-permute-start.10
  50.5 6.7 %collective-permute-done.10 = bf16[48,2688]{1,0:T(8,128)(2,1)S(1)} collective-permute-done((bf16[48,2688]{1,0:T(8,128)(2,1)S(1)}, bf16[48,2688]{1,0:T(8,128)(2,1)S(1)}, u32[]{:S(2)}, u32[]{:S(2)}) %collective-permute-start.10) | collective-permute-done | bytes 258080 | tf_op jit(solution)/shard_map/ppermute | solution.py:66
  57.2 11.1 %collective-permute-done.9 = bf16[48,2688]{1,0:T(8,128)(2,1)S(1)} collective-permute-done((bf16[48,2688]{1,0:T(8,128)(2,1)S(1)}, bf16[48,2688]{1,0:T(8,128)(2,1)S(1)}, u32[]{:S(2)}, u32[]{:S(2)}) %collective-permute-start.9) | collective-permute-done | bytes 258080 | tf_op jit(solution)/shard_map/ppermute | solution.py:66
  75.2 9.0 %collective-permute-done.15 = bf16[48,3840]{1,0:T(8,128)(2,1)S(1)} collective-permute-done((bf16[48,3840]{1,0:T(8,128)(2,1)S(1)}, bf16[48,3840]{1,0:T(8,128)(2,1)S(1)}, u32[]{:S(2)}, u32[]{:S(2)}) %collective-permute-start.15) | collective-permute-done | bytes 368672 | tf_op jit(solution)/shard_map/ppermute | solution.py:66
  84.2 16.9 %collective-permute-done.14 = bf16[48,3840]{1,0:T(8,128)(2,1)S(1)} collective-permute-done((bf16[48,3840]{1,0:T(8,128)(2,1)S(1)}, bf16[48,3840]{1,0:T(8,128)(2,1)S(1)}, u32[]{:S(2)}, u32[]{:S(2)}) %collective-permute-start.14) | collective-permute-done | bytes 368672 | tf_op jit(solution)/shard_map/ppermute | solution.py:66
  103.0 5.1 assemble.3
  117.2 13.3 %embed_qkv.1 = (f32[416,768]{1,0:T(8,128)}, bf16[416,768]{1,0:T(8,128)(2,1)}, bf16[416,1152]{1,0:T(8,128)(2,1)}, bf16[416,1152]{1,0:T(8,128)(2,1)}, bf16[416,384...) custom-call(s32[2]{0:T(128)S(1)} %pad_add_fusion.refs_0_.places, ...), custom_call_target="tpu_custom_call" | custom-call | flops 122683392 | bytes 65536 | tf_op jit(solution)/shard_map/embed_qkv/pallas_call | solution.py:775
  130.6 11.8 %out_up.2 = (f32[416,768]{1,0:T(8,128)}, bf16[416,768]{1,0:T(8,128)(2,1)}, bf16[416,1536]{1,0:T(8,128)(2,1)}, bf16[416,1536]{1,0:T(8,128)(2,1)}, f32[416,1536]{1...) custom-call(s32[2]{0:T(128)S(1)} %pad_add_fusion.refs_0_.places, ...), custom_call_target="tpu_custom_call" | custom-call | flops 153354240 | bytes 65536 | tf_op jit(solution)/shard_map/out_up/pallas_call | solution.py:782
  142.3 4.8 collective-permute-done.16.refs_4_.refs_3_
  147.2 4.8 assemble.4
  156.8 2.5 collective-permute-done.27.refs_9_.refs_8_
  161.9 14.8 %down_qkv.1 = (f32[416,768]{1,0:T(8,128)}, bf16[416,768]{1,0:T(8,128)(2,1)S(1)}, bf16[416,1152]{1,0:T(8,128)(2,1)}, bf16[416,1152]{1,0:T(8,128)(2,1)}, bf16[416,...) custom-call(s32[2]{0:T(128)S(1)} %pad_add_fusion.refs_0_.places, ...), custom_call_target="tpu_custom_call" | custom-call | flops 214695936 | bytes 65536 | tf_op jit(solution)/shard_map/down_qkv/pallas_call | solution.py:792
  176.7 5.5 assemble.5
  183.2 8.0 %collective-permute-done.28.refs_7_.refs_4_ = bf16[768,384]{1,0:T(8,128)(2,1)S(1)} collective-permute-done((bf16[768,384]{1,0:T(8,128)(2,1)S(1)}, bf16[768,384]{1,0:T(8,128)(2,1)S(1)}, u32[]{:S(2)}, u32[]{:S(2)}) %collective-permute-start.28) | collective-permute-done | bytes 589856 | tf_op jit(solution)/shard_map/ppermute | solution.py:66
  192.6 11.3 %out_up.3 = (f32[416,768]{1,0:T(8,128)}, bf16[416,768]{1,0:T(8,128)(2,1)}, bf16[416,1536]{1,0:T(8,128)(2,1)}, bf16[416,1536]{1,0:T(8,128)(2,1)}, f32[416,1536]{1...) custom-call(s32[2]{0:T(128)S(1)} %pad_add_fusion.refs_0_.places, ...), custom_call_target="tpu_custom_call" | custom-call | flops 153354240 | bytes 65536 | tf_op jit(solution)/shard_map/out_up/pallas_call | solution.py:782
  204.7 11.5 %down_head.1 = (bf16[416,768]{1,0:T(8,128)(2,1)}, bf16[416,384]{1,0:T(8,128)(2,1)S(1)}, bf16[416,384]{1,0:T(8,128)(2,1)}, f32[416,768]{1,0:T(8,128)}, bf16[416,7...) custom-call(s32[2]{0:T(128)S(1)} %pad_add_fusion.refs_0_.places, ...), custom_call_target="tpu_custom_call" | custom-call | flops 184025088 | bytes 65536 | tf_op jit(solution)/shard_map/down_head/pallas_call | solution.py:803
  219.6 13.2 %back_mlp.2 = (f32[416,768]{1,0:T(8,128)}, bf16[416,768]{1,0:T(8,128)(2,1)S(1)}, bf16[416,1536]{1,0:T(8,128)(2,1)}, bf16[416,1536]{1,0:T(8,128)(2,1)}, f32[8,768...) custom-call(f32[227,768]{1,0:T(8,128)} %fusion.5.vec.refs_1_.refs_2_.refs_0_, ...), custom_call_target="tpu_custom_call" | custom-call | flops 245366784 | bytes 65536 | tf_op jit(solution)/shard_map/back_mlp/pallas_call | solution.py:902
  234.3 3.7 product_sum.11
  242.1 3.9 product_sum.13
  250.3 21.6 %back_attend.2 = (f32[416,768]{1,0:T(8,128)}, bf16[416,768]{1,0:T(8,128)(2,1)S(1)}, bf16[416,1152]{1,0:T(8,128)(2,1)}, bf16[416,1152]{1,0:T(8,128)(2,1)}, f32[8,...) custom-call(f32[227,768]{1,0:T(8,128)} %fusion.5.vec.refs_1_.refs_2_.refs_0_, ...), custom_call_target="tpu_custom_call" | custom-call | flops 245366784 | bytes 65536 | tf_op jit(solution)/shard_map/back_attend/pallas_call | solution.py:924
  271.9 6.0 %collective-permute-done.36 = f16[400,1536]{1,0:T(8,128)(2,1)} collective-permute-done((f16[400,1536]{1,0:T(8,128)(2,1)S(1)}, f16[400,1536]{1,0:T(8,128)(2,1)}, u32[]{:S(2)}, u32[]{:S(2)}) %collective-permute-start.36) | collective-permute-done | bytes 1228832 | tf_op jit(solution)/shard_map/ppermute | solution.py:66
  277.9 5.6 collective-permute-done.35
  283.6 2.5 multiply_add_fusion
  300.3 6.9 %collective-permute-done.39 = f16[208,1536]{1,0:T(8,128)(2,1)S(1)} collective-permute-done((f16[208,1536]{1,0:T(8,128)(2,1)S(1)}, f16[208,1536]{1,0:T(8,128)(2,1)S(1)}, u32[]{:S(2)}, u32[]{:S(2)}) %collective-permute-start.39) | collective-permute-done | bytes 639008 | tf_op jit(solution)/shard_map/ppermute | solution.py:66
  316.2 13.4 %back_mlp.3 = (f32[416,768]{1,0:T(8,128)}, bf16[416,768]{1,0:T(8,128)(2,1)S(1)}, bf16[416,1536]{1,0:T(8,128)(2,1)}, bf16[416,1536]{1,0:T(8,128)(2,1)}, f32[8,768...) custom-call(f32[227,768]{1,0:T(8,128)} %fusion.5.vec.refs_1_.refs_2_.refs_0_, ...), custom_call_target="tpu_custom_call" | custom-call | flops 245366784 | bytes 65536 | tf_op jit(solution)/shard_map/back_mlp/pallas_call | solution.py:902
  343.9 3.7 product_sum.17
  349.5 3.9 product_sum.18
  353.6 2.7 collective-permute-done.45
  362.0 22.6 %back_attend.3 = (f32[416,768]{1,0:T(8,128)}, bf16[416,768]{1,0:T(8,128)(2,1)}, bf16[416,1152]{1,0:T(8,128)(2,1)}, bf16[416,1152]{1,0:T(8,128)(2,1)}, f32[8,768]...) custom-call(f32[227,768]{1,0:T(8,128)} %fusion.5.vec.refs_1_.refs_2_.refs_0_, ...), custom_call_target="tpu_custom_call" | custom-call | flops 245366784 | bytes 65536 | tf_op jit(solution)/shard_map/back_attend/pallas_call | solution.py:924
  384.6 2.7 multiply_reduce_fusion
  404.5 4.2 product_sum.19
  408.9 2.8 collective-permute-done.51
  424.9 12.5 %collective-permute-done.59 = f16[400,768]{1,0:T(8,128)(2,1)S(1)} collective-permute-done((f16[400,768]{1,0:T(8,128)(2,1)S(1)}, f16[400,768]{1,0:T(8,128)(2,1)S(1)}, u32[]{:S(2)}, u32[]{:S(2)}) %collective-permute-start.59) | collective-permute-done | bytes 614432 | tf_op jit(solution)/shard_map/ppermute | solution.py:66
  437.4 5.4 collective-permute-done.58
  457.9 4.5 collective-permute-done.65
  464.1 3.1 collective-permute-done.63
  477.0 7.6 %collective-permute-done.67 = f32[32,768]{1,0:T(8,128)S(1)} collective-permute-done((f32[32,768]{1,0:T(8,128)S(1)}, f32[32,768]{1,0:T(8,128)S(1)}, u32[]{:S(2)}, u32[]{:S(2)}) %collective-permute-start.67) | collective-permute-done | bytes 98336 | tf_op jit(solution)/shard_map/ppermute | solution.py:66
  494.3 12.0 %collective-permute-done.74 = f32[32,768]{1,0:T(8,128)S(1)} collective-permute-done((f32[32,768]{1,0:T(8,128)S(1)}, f32[32,768]{1,0:T(8,128)S(1)}, u32[]{:S(2)}, u32[]{:S(2)}) %collective-permute-start.74) | collective-permute-done | bytes 98336 | tf_op jit(solution)/shard_map/ppermute | solution.py:66
  506.3 2.9 collective-permute-start.78
  537.1 2.7 collective-permute-done.81
  555.5 20.1 %shampoo.1 = (f32[48,96,96]{2,1,0:T(8,128)}, f32[48,96,96]{2,1,0:T(8,128)}, f32[48,96,96]{2,1,0:T(8,128)}, f32[48,96,96]{2,1,0:T(8,128)}, f32[48,96,96]{2,1,0:T(8,128)}) custom-call(s32[5,48]{1,0:T(8,128)S(1)} %stack.34.refs_0_, bf16[4,48,9984]{2,1,0:T(8,128)(2,1)} %get-tuple-element.618.refs_1_, f32[64,4992]{1,0:T(8,128)} %copy-done.70, ...), custom_call_target="tpu_custom_call" | custom-call | flops 127401984 | bytes 65536 | tf_op jit(solution)/shard_map/shampoo/pallas_call | solution.py:591
  575.6 3.4 multiply_bitcast_fusion
  589.6 3.3 multiply_subtract_fusion
  (739 shorter events, 220.9 us)
Async XLA Ops:
  8.4 24.0 %collective-permute-start.2 = (bf16[48,3456]{1,0:T(8,128)(2,1)S(1)}, bf16[48,3456]{1,0:T(8,128)(2,1)}, u32[]{:S(2)}, u32[]{:S(2)}) collective-permute-start(bf16[48,3456]{1,0:T(8,128)(2,1)S(1)} %get-tuple-element.320), channel_id=1, source_target_pairs={{0,3},{1,2},{2,1},{3,0},{4,7},{5,6},{6,5},{7,4},{8,11},{9,10},{10,... | collective-permute-start | bytes 995336 | tf_op jit(solution)/shard_map/ppermute | solution.py:66
  13.4 28.4 %collective-permute-start.1 = (bf16[48,3456]{1,0:T(8,128)(2,1)S(1)}, bf16[48,3456]{1,0:T(8,128)(2,1)}, u32[]{:S(2)}, u32[]{:S(2)}) collective-permute-start(bf16[48,3456]{1,0:T(8,128)(2,1)S(1)} %get-tuple-element.320), channel_id=1, source_target_pairs={{0,2},{1,3},{2,0},{3,1},{4,6},{5,7},{6,4},{7,5},{8,10},{9,11},{10,... | collective-permute-start | bytes 995336 | tf_op jit(solution)/shard_map/ppermute | solution.py:66
  13.4 28.4 %collective-permute-start = (bf16[48,3456]{1,0:T(8,128)(2,1)S(1)}, bf16[48,3456]{1,0:T(8,128)(2,1)}, u32[]{:S(2)}, u32[]{:S(2)}) collective-permute-start(bf16[48,3456]{1,0:T(8,128)(2,1)S(1)} %get-tuple-element.320), channel_id=1, source_target_pairs={{0,1},{1,0},{2,3},{3,2},{4,5},{5,4},{6,7},{7,6},{8,9},{9,8},{10,11... | collective-permute-start | bytes 995336 | tf_op jit(solution)/shard_map/ppermute | solution.py:66
  43.1 25.3 %collective-permute-start.6 = (bf16[144,3456]{1,0:T(8,128)(2,1)S(1)}, bf16[144,3456]{1,0:T(8,128)(2,1)S(1)}, u32[]{:S(2)}, u32[]{:S(2)}) collective-permute-start(bf16[144,3456]{1,0:T(8,128)(2,1)S(1)} %pad_maximum_fusion.9.refs_1_), channel_id=1, source_target_pairs={{0,8},{8,0},{16,24},{24,16},{1,9},{9,1},{17,25},{25,17},{2,10},{10... | collective-permute-start | bytes 2985992 | tf_op jit(solution)/shard_map/ppermute | solution.py:66
  44.6 23.8 %collective-permute-start.7 = (bf16[144,3456]{1,0:T(8,128)(2,1)S(1)}, bf16[144,3456]{1,0:T(8,128)(2,1)S(1)}, u32[]{:S(2)}, u32[]{:S(2)}) collective-permute-start(bf16[144,3456]{1,0:T(8,128)(2,1)S(1)} %pad_maximum_fusion.9.refs_1_), channel_id=1, source_target_pairs={{0,16},{8,24},{16,0},{24,8},{1,17},{9,25},{17,1},{25,9},{2,18},{10... | collective-permute-start | bytes 2985992 | tf_op jit(solution)/shard_map/ppermute | solution.py:66
  48.6 19.7 %collective-permute-start.9 = (bf16[48,2688]{1,0:T(8,128)(2,1)S(1)}, bf16[48,2688]{1,0:T(8,128)(2,1)S(1)}, u32[]{:S(2)}, u32[]{:S(2)}) collective-permute-start(bf16[48,2688]{1,0:T(8,128)(2,1)S(1)} %get-tuple-element.327), channel_id=1, source_target_pairs={{0,2},{1,3},{2,0},{3,1},{4,6},{5,7},{6,4},{7,5},{8,10},{9,11},{10,... | collective-permute-start | bytes 774152 | tf_op jit(solution)/shard_map/ppermute | solution.py:66
  48.6 19.7 %collective-permute-start.8 = (bf16[48,2688]{1,0:T(8,128)(2,1)S(1)}, bf16[48,2688]{1,0:T(8,128)(2,1)S(1)}, u32[]{:S(2)}, u32[]{:S(2)}) collective-permute-start(bf16[48,2688]{1,0:T(8,128)(2,1)S(1)} %get-tuple-element.327), channel_id=1, source_target_pairs={{0,1},{1,0},{2,3},{3,2},{4,5},{5,4},{6,7},{7,6},{8,9},{9,8},{10,11... | collective-permute-start | bytes 774152 | tf_op jit(solution)/shard_map/ppermute | solution.py:66
  69.6 31.6 %collective-permute-start.12 = (bf16[144,4480]{1,0:T(8,128)(2,1)S(1)}, bf16[144,4480]{1,0:T(8,128)(2,1)S(1)}, u32[]{:S(2)}, u32[]{:S(2)}) collective-permute-start(bf16[144,4480]{1,0:T(8,128)(2,1)S(1)} %pad_maximum_fusion.4), channel_id=1, source_target_pairs={{0,8},{8,0},{16,24},{24,16},{1,9},{9,1},{17,25},{25,17},{2,10},{10... | collective-permute-start | bytes 3870728 | tf_op jit(solution)/shard_map/ppermute | solution.py:66
  70.3 30.9 %collective-permute-start.11 = (bf16[144,4352]{1,0:T(8,128)(2,1)S(1)}, bf16[144,4352]{1,0:T(8,128)(2,1)S(1)}, u32[]{:S(2)}, u32[]{:S(2)}) collective-permute-start(bf16[144,4352]{1,0:T(8,128)(2,1)S(1)} %pad_maximum_fusion.5), channel_id=1, source_target_pairs={{0,16},{8,24},{16,0},{24,8},{1,17},{9,25},{17,1},{25,9},{2,18},{10... | collective-permute-start | bytes 3760136 | tf_op jit(solution)/shard_map/ppermute | solution.py:66
  72.9 28.2 %collective-permute-start.14 = (bf16[48,3840]{1,0:T(8,128)(2,1)S(1)}, bf16[48,3840]{1,0:T(8,128)(2,1)S(1)}, u32[]{:S(2)}, u32[]{:S(2)}) collective-permute-start(bf16[48,3840]{1,0:T(8,128)(2,1)S(1)} %get-tuple-element.333), channel_id=1, source_target_pairs={{0,2},{1,3},{2,0},{3,1},{4,6},{5,7},{6,4},{7,5},{8,10},{9,11},{10,... | collective-permute-start | bytes 1105928 | tf_op jit(solution)/shard_map/ppermute | solution.py:66
  72.9 28.2 %collective-permute-start.13 = (bf16[48,3840]{1,0:T(8,128)(2,1)S(1)}, bf16[48,3840]{1,0:T(8,128)(2,1)S(1)}, u32[]{:S(2)}, u32[]{:S(2)}) collective-permute-start(bf16[48,3840]{1,0:T(8,128)(2,1)S(1)} %get-tuple-element.333), channel_id=1, source_target_pairs={{0,1},{1,0},{2,3},{3,2},{4,5},{5,4},{6,7},{7,6},{8,9},{9,8},{10,11... | collective-permute-start | bytes 1105928 | tf_op jit(solution)/shard_map/ppermute | solution.py:66
  108.1 22.4 %collective-permute-start.21 = (bf16[768,1536]{1,0:T(8,128)(2,1)}, bf16[768,1536]{1,0:T(8,128)(2,1)}, u32[]{:S(2)}, u32[]{:S(2)}) collective-permute-start(bf16[768,1536]{1,0:T(8,128)(2,1)} %get-tuple-element.356.refs_8_.refs_7_), channel_id=1, source_target_pairs={{0,4},{4,0},{1,5},{5,1},{2,6},{6,2},{3,7},{7,3},{8,12},{12,8},{9,1... | collective-permute-start | bytes 7077896 | tf_op jit(solution)/shard_map/ppermute | solution.py:66
  109.4 37.7 %collective-permute-start.17 = (bf16[144,5248]{1,0:T(8,128)(2,1)}, bf16[144,5248]{1,0:T(8,128)(2,1)}, u32[]{:S(2)}, u32[]{:S(2)}) collective-permute-start(bf16[144,5248]{1,0:T(8,128)(2,1)} %pad_maximum_fusion.2), channel_id=1, source_target_pairs={{0,8},{8,0},{16,24},{24,16},{1,9},{9,1},{17,25},{25,17},{2,10},{10... | collective-permute-start | bytes 4534280 | tf_op jit(solution)/shard_map/ppermute | solution.py:66
  112.4 34.8 %collective-permute-start.16 = (bf16[144,5120]{1,0:T(8,128)(2,1)}, bf16[144,5120]{1,0:T(8,128)(2,1)}, u32[]{:S(2)}, u32[]{:S(2)}) collective-permute-start(bf16[144,5120]{1,0:T(8,128)(2,1)} %pad_maximum_fusion.3), channel_id=1, source_target_pairs={{0,16},{8,24},{16,0},{24,8},{1,17},{9,25},{17,1},{25,9},{2,18},{10... | collective-permute-start | bytes 4423688 | tf_op jit(solution)/shard_map/ppermute | solution.py:66
  152.5 24.2 %collective-permute-start.25 = (bf16[416,2304]{1,0:T(8,128)(2,1)}, bf16[416,2304]{1,0:T(8,128)(2,1)S(1)}, u32[]{:S(2)}, u32[]{:S(2)}) collective-permute-start(bf16[416,2304]{1,0:T(8,128)(2,1)} %get-tuple-element.378), channel_id=1, source_target_pairs={{0,4},{4,0},{1,5},{5,1},{2,6},{6,2},{3,7},{7,3},{8,12},{12,8},{9,1... | collective-permute-start | bytes 5750792 | tf_op jit(solution)/shard_map/ppermute | solution.py:66
  152.5 24.2 %collective-permute-start.24 = (bf16[416,1152]{1,0:T(8,128)(2,1)}, bf16[416,1152]{1,0:T(8,128)(2,1)S(1)}, u32[]{:S(2)}, u32[]{:S(2)}) collective-permute-start(bf16[416,1152]{1,0:T(8,128)(2,1)} %get-tuple-element.371), channel_id=1, source_target_pairs={{0,4},{4,0},{1,5},{5,1},{2,6},{6,2},{3,7},{7,3},{8,12},{12,8},{9,1... | collective-permute-start | bytes 2875400 | tf_op jit(solution)/shard_map/ppermute | solution.py:66
  154.1 22.6 %collective-permute-start.22 = (bf16[144,1920]{1,0:T(8,128)(2,1)S(1)}, bf16[144,1920]{1,0:T(8,128)(2,1)S(1)}, u32[]{:S(2)}, u32[]{:S(2)}) collective-permute-start(bf16[144,1920]{1,0:T(8,128)(2,1)S(1)} %slice.385), channel_id=1, source_target_pairs={{0,16},{8,24},{16,0},{24,8},{1,17},{9,25},{17,1},{25,9},{2,18},{10... | collective-permute-start | bytes 1658888 | tf_op jit(solution)/shard_map/ppermute | solution.py:66
  182.3 21.6 %collective-permute-start.30 = (bf16[768,1536]{1,0:T(8,128)(2,1)}, bf16[768,1536]{1,0:T(8,128)(2,1)}, u32[]{:S(2)}, u32[]{:S(2)}) collective-permute-start(bf16[768,1536]{1,0:T(8,128)(2,1)} %get-tuple-element.407.refs_7_.refs_3_), channel_id=1, source_target_pairs={{0,4},{4,0},{1,5},{5,1},{2,6},{6,2},{3,7},{7,3},{8,12},{12,8},{9,1... | collective-permute-start | bytes 7077896 | tf_op jit(solution)/shard_map/ppermute | solution.py:66
  182.9 21.1 %collective-permute-start.31 = (bf16[768,384]{1,0:T(8,128)(2,1)}, bf16[768,384]{1,0:T(8,128)(2,1)S(1)}, u32[]{:S(2)}, u32[]{:S(2)}) collective-permute-start(bf16[768,384]{1,0:T(8,128)(2,1)} %get-tuple-element.408.refs_9_), channel_id=1, source_target_pairs={{0,4},{4,0},{1,5},{5,1},{2,6},{6,2},{3,7},{7,3},{8,12},{12,8},{9,1... | collective-permute-start | bytes 1769480 | tf_op jit(solution)/shard_map/ppermute | solution.py:66
  247.4 36.1 %collective-permute-start.35 = (f16[400,1920]{1,0:T(8,128)(2,1)}, f16[400,1920]{1,0:T(8,128)(2,1)S(1)}, u32[]{:S(2)}, u32[]{:S(2)}) collective-permute-start(f16[400,1920]{1,0:T(8,128)(2,1)} %pad_maximum_fusion.1), channel_id=1, source_target_pairs={{0,8},{8,0},{16,24},{24,16},{1,9},{9,1},{17,25},{25,17},{2,10},{10... | collective-permute-start | bytes 4608008 | tf_op jit(solution)/shard_map/ppermute | solution.py:66
  248.8 29.1 %collective-permute-start.36 = (f16[400,1536]{1,0:T(8,128)(2,1)S(1)}, f16[400,1536]{1,0:T(8,128)(2,1)}, u32[]{:S(2)}, u32[]{:S(2)}) collective-permute-start(f16[400,1536]{1,0:T(8,128)(2,1)S(1)} %convert_element_type.318), channel_id=1, source_target_pairs={{0,16},{8,24},{16,0},{24,8},{1,17},{9,25},{17,1},{25,9},{2,18},{10... | collective-permute-start | bytes 3686408 | tf_op jit(solution)/shard_map/ppermute | solution.py:66
  250.3 41.9 %collective-permute-start.40 = (bf16[416,1152]{1,0:T(8,128)(2,1)S(1)}, bf16[416,1152]{1,0:T(8,128)(2,1)S(1)}, u32[]{:S(2)}, u32[]{:S(2)}) collective-permute-start(bf16[416,1152]{1,0:T(8,128)(2,1)S(1)} %copy-done.144), channel_id=1, source_target_pairs={{0,4},{4,0},{1,5},{5,1},{2,6},{6,2},{3,7},{7,3},{8,12},{12,8},{9,1... | collective-permute-start | bytes 2875400 | tf_op jit(solution)/shard_map/ppermute | solution.py:66
  286.4 20.9 %collective-permute-start.38 = (f16[208,1920]{1,0:T(8,128)(2,1)S(1)}, f16[208,1920]{1,0:T(8,128)(2,1)S(1)}, u32[]{:S(2)}, u32[]{:S(2)}) collective-permute-start(f16[208,1920]{1,0:T(8,128)(2,1)S(1)} %pad_maximum_fusion.10), channel_id=1, source_target_pairs={{0,16},{8,24},{16,0},{24,8},{1,17},{9,25},{17,1},{25,9},{2,18},{10... | collective-permute-start | bytes 2396168 | tf_op jit(solution)/shard_map/ppermute | solution.py:66
  310.8 20.0 %collective-permute-start.41 = (f16[112,3456]{1,0:T(8,128)(2,1)}, f16[112,3456]{1,0:T(8,128)(2,1)}, u32[]{:S(2)}, u32[]{:S(2)}) collective-permute-start(f16[112,3456]{1,0:T(8,128)(2,1)} %pad_maximum_fusion.12), channel_id=1, source_target_pairs={{0,1},{1,0},{2,3},{3,2},{4,5},{5,4},{6,7},{7,6},{8,9},{9,8},{10,11... | collective-permute-start | bytes 2322440 | tf_op jit(solution)/shard_map/ppermute | solution.py:66
  310.8 20.0 %collective-permute-start.42 = (f16[400,768]{1,0:T(8,128)(2,1)}, f16[400,768]{1,0:T(8,128)(2,1)}, u32[]{:S(2)}, u32[]{:S(2)}) collective-permute-start(f16[400,768]{1,0:T(8,128)(2,1)} %convert_element_type.323), channel_id=1, source_target_pairs={{0,8},{8,0},{16,24},{24,16},{1,9},{9,1},{17,25},{25,17},{2,10},{10... | collective-permute-start | bytes 1843208 | tf_op jit(solution)/shard_map/ppermute | solution.py:66
  312.3 18.5 %collective-permute-start.43 = (f16[400,768]{1,0:T(8,128)(2,1)}, f16[400,768]{1,0:T(8,128)(2,1)}, u32[]{:S(2)}, u32[]{:S(2)}) collective-permute-start(f16[400,768]{1,0:T(8,128)(2,1)} %pad_maximum_fusion.19), channel_id=1, source_target_pairs={{0,16},{8,24},{16,0},{24,8},{1,17},{9,25},{17,1},{25,9},{2,18},{10... | collective-permute-start | bytes 1843208 | tf_op jit(solution)/shard_map/ppermute | solution.py:66
  330.8 18.0 %collective-permute-start.44 = (bf16[416,2304]{1,0:T(8,128)(2,1)}, bf16[416,2304]{1,0:T(8,128)(2,1)S(1)}, u32[]{:S(2)}, u32[]{:S(2)}) collective-permute-start(bf16[416,2304]{1,0:T(8,128)(2,1)} %get-tuple-element.490), channel_id=1, source_target_pairs={{0,4},{4,0},{1,5},{5,1},{2,6},{6,2},{3,7},{7,3},{8,12},{12,8},{9,1... | collective-permute-start | bytes 5750792 | tf_op jit(solution)/shard_map/ppermute | solution.py:66
  333.4 22.9 %collective-permute-start.45 = (f16[64,3456]{1,0:T(8,128)(2,1)S(1)}, f16[64,3456]{1,0:T(8,128)(2,1)S(1)}, u32[]{:S(2)}, u32[]{:S(2)}) collective-permute-start(f16[64,3456]{1,0:T(8,128)(2,1)S(1)} %pad_maximum_fusion.23), channel_id=1, source_target_pairs={{0,2},{1,3},{2,0},{3,1},{4,6},{5,7},{6,4},{7,5},{8,10},{9,11},{10,... | collective-permute-start | bytes 1327112 | tf_op jit(solution)/shard_map/ppermute | solution.py:66
  356.4 30.9 %collective-permute-start.49 = (f16[400,1536]{1,0:T(8,128)(2,1)}, f16[400,1536]{1,0:T(8,128)(2,1)}, u32[]{:S(2)}, u32[]{:S(2)}) collective-permute-start(f16[400,1536]{1,0:T(8,128)(2,1)} %convert_element_type.338), channel_id=1, source_target_pairs={{0,8},{8,0},{16,24},{24,16},{1,9},{9,1},{17,25},{25,17},{2,10},{10... | collective-permute-start | bytes 3686408 | tf_op jit(solution)/shard_map/ppermute | solution.py:66
  357.1 30.3 %collective-permute-start.50 = (f16[400,1536]{1,0:T(8,128)(2,1)S(1)}, f16[400,1536]{1,0:T(8,128)(2,1)}, u32[]{:S(2)}, u32[]{:S(2)}) collective-permute-start(f16[400,1536]{1,0:T(8,128)(2,1)S(1)} %convert_element_type.339), channel_id=1, source_target_pairs={{0,16},{8,24},{16,0},{24,8},{1,17},{9,25},{17,1},{25,9},{2,18},{10... | collective-permute-start | bytes 3686408 | tf_op jit(solution)/shard_map/ppermute | solution.py:66
  359.4 27.9 %collective-permute-start.48 = (f16[112,1536]{1,0:T(8,128)(2,1)}, f16[112,1536]{1,0:T(8,128)(2,1)}, u32[]{:S(2)}, u32[]{:S(2)}) collective-permute-start(f16[112,1536]{1,0:T(8,128)(2,1)} %pad_maximum_fusion.29), channel_id=1, source_target_pairs={{0,1},{1,0},{2,3},{3,2},{4,5},{5,4},{6,7},{7,6},{8,9},{9,8},{10,11... | collective-permute-start | bytes 1032200 | tf_op jit(solution)/shard_map/ppermute | solution.py:66
  392.0 19.7 %collective-permute-start.52 = (f16[208,1536]{1,0:T(8,128)(2,1)S(1)}, f16[208,1536]{1,0:T(8,128)(2,1)S(1)}, u32[]{:S(2)}, u32[]{:S(2)}) collective-permute-start(f16[208,1536]{1,0:T(8,128)(2,1)S(1)} %pad_maximum_fusion.16), channel_id=1, source_target_pairs={{0,16},{8,24},{16,0},{24,8},{1,17},{9,25},{17,1},{25,9},{2,18},{10... | collective-permute-start | bytes 1916936 | tf_op jit(solution)/shard_map/ppermute | solution.py:66
  418.1 19.3 %collective-permute-start.57 = (f16[112,3072]{1,0:T(8,128)(2,1)S(1)}, f16[112,3072]{1,0:T(8,128)(2,1)S(1)}, u32[]{:S(2)}, u32[]{:S(2)}) collective-permute-start(f16[112,3072]{1,0:T(8,128)(2,1)S(1)} %pad_maximum_fusion.13), channel_id=1, source_target_pairs={{0,1},{1,0},{2,3},{3,2},{4,5},{5,4},{6,7},{7,6},{8,9},{9,8},{10,11... | collective-permute-start | bytes 2064392 | tf_op jit(solution)/shard_map/ppermute | solution.py:66
  420.2 22.6 %collective-permute-start.58 = (f16[400,1152]{1,0:T(8,128)(2,1)S(1)}, f16[400,1152]{1,0:T(8,128)(2,1)S(1)}, u32[]{:S(2)}, u32[]{:S(2)}) collective-permute-start(f16[400,1152]{1,0:T(8,128)(2,1)S(1)} %convert_element_type.354), channel_id=1, source_target_pairs={{0,8},{8,0},{16,24},{24,16},{1,9},{9,1},{17,25},{25,17},{2,10},{10... | collective-permute-start | bytes 2764808 | tf_op jit(solution)/shard_map/ppermute | solution.py:66
  448.0 19.2 %collective-permute-start.63 = (f16[64,3072]{1,0:T(8,128)(2,1)}, f16[64,3072]{1,0:T(8,128)(2,1)}, u32[]{:S(2)}, u32[]{:S(2)}) collective-permute-start(f16[64,3072]{1,0:T(8,128)(2,1)} %pad_maximum_fusion.25), channel_id=1, source_target_pairs={{0,2},{1,3},{2,0},{3,1},{4,6},{5,7},{6,4},{7,5},{8,10},{9,11},{10,... | collective-permute-start | bytes 1179656 | tf_op jit(solution)/shard_map/ppermute | solution.py:66
  449.2 18.0 %collective-permute-start.64 = (f16[208,1152]{1,0:T(8,128)(2,1)S(1)}, f16[208,1152]{1,0:T(8,128)(2,1)}, u32[]{:S(2)}, u32[]{:S(2)}) collective-permute-start(f16[208,1152]{1,0:T(8,128)(2,1)S(1)} %pad_maximum_fusion.22), channel_id=1, source_target_pairs={{0,16},{8,24},{16,0},{24,8},{1,17},{9,25},{17,1},{25,9},{2,18},{10... | collective-permute-start | bytes 1437704 | tf_op jit(solution)/shard_map/ppermute | solution.py:66
  455.4 30.7 %collective-permute-start.68 = (f16[64,4992]{1,0:T(8,128)(2,1)}, f16[64,4992]{1,0:T(8,128)(2,1)S(1)}, u32[]{:S(2)}, u32[]{:S(2)}) collective-permute-start(f16[64,4992]{1,0:T(8,128)(2,1)} %pad_maximum_fusion.18), channel_id=1, source_target_pairs={{0,8},{8,0},{16,24},{24,16},{1,9},{9,1},{17,25},{25,17},{2,10},{10... | collective-permute-start | bytes 1916936 | tf_op jit(solution)/shard_map/ppermute | solution.py:66
  456.0 33.5 %collective-permute-start.69 = (f16[64,4992]{1,0:T(8,128)(2,1)}, f16[64,4992]{1,0:T(8,128)(2,1)S(1)}, u32[]{:S(2)}, u32[]{:S(2)}) collective-permute-start(f16[64,4992]{1,0:T(8,128)(2,1)} %pad_maximum_fusion.18), channel_id=1, source_target_pairs={{0,16},{8,24},{16,0},{24,8},{1,17},{9,25},{17,1},{25,9},{2,18},{10... | collective-permute-start | bytes 1916936 | tf_op jit(solution)/shard_map/ppermute | solution.py:66
  462.4 28.8 %collective-permute-start.70 = (f16[64,4992]{1,0:T(8,128)(2,1)}, f16[64,4992]{1,0:T(8,128)(2,1)S(1)}, u32[]{:S(2)}, u32[]{:S(2)}) collective-permute-start(f16[64,4992]{1,0:T(8,128)(2,1)} %pad_maximum_fusion.18), channel_id=1, source_target_pairs={{0,24},{8,16},{16,8},{24,0},{1,25},{9,17},{17,9},{25,1},{2,26},{10... | collective-permute-start | bytes 1916936 | tf_op jit(solution)/shard_map/ppermute | solution.py:66
  471.5 19.7 %collective-permute-start.71 = (f16[112,1920]{1,0:T(8,128)(2,1)S(1)}, f16[112,1920]{1,0:T(8,128)(2,1)S(1)}, u32[]{:S(2)}, u32[]{:S(2)}) collective-permute-start(f16[112,1920]{1,0:T(8,128)(2,1)S(1)} %pad_maximum_fusion.24), channel_id=1, source_target_pairs={{0,1},{1,0},{2,3},{3,2},{4,5},{5,4},{6,7},{7,6},{8,9},{9,8},{10,11... | collective-permute-start | bytes 1290248 | tf_op jit(solution)/shard_map/ppermute | solution.py:66
  484.6 36.5 %collective-permute-start.75 = (f16[64,3072]{1,0:T(8,128)(2,1)}, f16[64,3072]{1,0:T(8,128)(2,1)}, u32[]{:S(2)}, u32[]{:S(2)}) collective-permute-start(f16[64,3072]{1,0:T(8,128)(2,1)} %pad_maximum_fusion.27), channel_id=1, source_target_pairs={{0,8},{8,0},{16,24},{24,16},{1,9},{9,1},{17,25},{25,17},{2,10},{10... | collective-permute-start | bytes 1179656 | tf_op jit(solution)/shard_map/ppermute | solution.py:66
  486.2 35.0 %collective-permute-start.76 = (f16[64,3072]{1,0:T(8,128)(2,1)}, f16[64,3072]{1,0:T(8,128)(2,1)}, u32[]{:S(2)}, u32[]{:S(2)}) collective-permute-start(f16[64,3072]{1,0:T(8,128)(2,1)} %pad_maximum_fusion.27), channel_id=1, source_target_pairs={{0,16},{8,24},{16,0},{24,8},{1,17},{9,25},{17,1},{25,9},{2,18},{10... | collective-permute-start | bytes 1179656 | tf_op jit(solution)/shard_map/ppermute | solution.py:66
  489.5 31.6 %collective-permute-start.77 = (f16[64,3072]{1,0:T(8,128)(2,1)}, f16[64,3072]{1,0:T(8,128)(2,1)}, u32[]{:S(2)}, u32[]{:S(2)}) collective-permute-start(f16[64,3072]{1,0:T(8,128)(2,1)} %pad_maximum_fusion.27), channel_id=1, source_target_pairs={{0,24},{8,16},{16,8},{24,0},{1,25},{9,17},{17,9},{25,1},{2,26},{10... | collective-permute-start | bytes 1179656 | tf_op jit(solution)/shard_map/ppermute | solution.py:66
  492.5 22.2 %collective-permute-start.73 = (f32[32,768]{1,0:T(8,128)S(1)}, f32[32,768]{1,0:T(8,128)}, u32[]{:S(2)}, u32[]{:S(2)}) collective-permute-start(f32[32,768]{1,0:T(8,128)S(1)} %add.985), channel_id=1, source_target_pairs={{0,16},{8,24},{16,0},{24,8},{1,17},{9,25},{17,1},{25,9},{2,18},{10... | collective-permute-start | bytes 294920 | tf_op jit(solution)/shard_map/ppermute | solution.py:66
  523.3 30.1 %collective-permute-start.85 = (f16[64,1920]{1,0:T(8,128)(2,1)S(1)}, f16[64,1920]{1,0:T(8,128)(2,1)S(1)}, u32[]{:S(2)}, u32[]{:S(2)}) collective-permute-start(f16[64,1920]{1,0:T(8,128)(2,1)S(1)} %pad_maximum_fusion.35), channel_id=1, source_target_pairs={{0,8},{8,0},{16,24},{24,16},{1,9},{9,1},{17,25},{25,17},{2,10},{10... | collective-permute-start | bytes 737288 | tf_op jit(solution)/shard_map/ppermute | solution.py:66
  524.8 28.5 %collective-permute-start.86 = (f16[64,1920]{1,0:T(8,128)(2,1)S(1)}, f16[64,1920]{1,0:T(8,128)(2,1)}, u32[]{:S(2)}, u32[]{:S(2)}) collective-permute-start(f16[64,1920]{1,0:T(8,128)(2,1)S(1)} %pad_maximum_fusion.35), channel_id=1, source_target_pairs={{0,16},{8,24},{16,0},{24,8},{1,17},{9,25},{17,1},{25,9},{2,18},{10... | collective-permute-start | bytes 737288 | tf_op jit(solution)/shard_map/ppermute | solution.py:66
  525.7 27.7 %collective-permute-start.87 = (f16[64,1920]{1,0:T(8,128)(2,1)S(1)}, f16[64,1920]{1,0:T(8,128)(2,1)}, u32[]{:S(2)}, u32[]{:S(2)}) collective-permute-start(f16[64,1920]{1,0:T(8,128)(2,1)S(1)} %pad_maximum_fusion.35), channel_id=1, source_target_pairs={{0,24},{8,16},{16,8},{24,0},{1,25},{9,17},{17,9},{25,1},{2,26},{10... | collective-permute-start | bytes 737288 | tf_op jit(solution)/shard_map/ppermute | solution.py:66
  528.9 60.6 %collective-permute-start.84 = (f32[128,768]{1,0:T(8,128)}, f32[128,768]{1,0:T(8,128)}, u32[]{:S(2)}, u32[]{:S(2)}) collective-permute-start(f32[128,768]{1,0:T(8,128)} %pad_maximum_fusion.26), channel_id=1, source_target_pairs={{0,4},{4,0},{1,5},{5,1},{2,6},{6,2},{3,7},{7,3},{8,12},{12,8},{9,1... | collective-permute-start | bytes 1179656 | tf_op jit(solution)/shard_map/ppermute | solution.py:66
  (188 other events, 1762.8 us)

commit v5 on v4

--- a/solution.py
+++ b/solution.py
@@ -909,12 +909,6 @@
         active = values["active", i]
         first_x = [product("x", grad_low, got_low, low_at, active[0], values["got_up", i], width, "down")]
         names_x = [("down", i)]
-        if i == layer_count - 1:
-            head = values["got_head"]
-            first_x.append(
-                product("x", values["low_fin"], head, 0, values["pred"][0], head, 2 * width, "ends")
-            )
-            names_x.append(("ends", 1))
         first_y = [product("y", values["low_two", i], values["got_up", i], 0, hid_a, got_mid, width, "up")]
         group = Reduce(first_x, first_y)
         groups.append((group, names_x + [("up", i)]))
@@ -938,6 +932,12 @@
             first_x = [product("x", *mix_args, range(0, 2))]
             first_y = [product("y", *mix_args, range(2, 3)), product("y", *out_args)]
             group_names = [("qkv", i), ("out", i)]
+            if i == layer_count - 1:
+                head = values["got_head"]
+                first_y.append(
+                    product("y", values["low_fin"], head, 0, values["pred"][0], head, 2 * width, "ends")
+                )
+                group_names.append(("ends", 1))
         else:
             outs = activations(width) + [((LP, width), f32), ((8, width), f32)]
             embed_low, place_sum, wides["embed"] = whole_call(back_embed_body, outs, "back_embed", full)(

time: 605 us -> 596 us (0.985)
    unnamed x306 -> x334, local copies, waits for them, and re-layouts: 23.7 us -> 25.2 us
  transfers between devices with their start and end apart: 88 -> 88, of which waited for: 27 -> 30; matrix products, arithmetic and copies ran while one was open for 16% -> 17% of each run, Pallas kernels for 28% -> 28%
where the time goes in v5:
time: 596 us; the launch traced here: 586 us
  Pallas kernels  205 us (34%)
  waiting for transfers between devices  148 us (25%)
  other arithmetic  91.9 us (15%)
  starting transfers between devices  83 us (14%)
  local copies, waits for them, and re-layouts  37.5 us (6%)
  between operations  11.9 us (2%)
  matrix products  8.69 us (1%)
    ppermute x88, waiting for transfers between devices, swap(): return lax.ppermute(value, axis, [(i, i ^ mask) for i in range(size)])  148 us
    ppermute x88, starting transfers between devices, swap(): return lax.ppermute(value, axis, [(i, i ^ mask) for i in range(size)])  83 us
    pallas_call x2, Pallas kernels, shards(): whole_call(lambda *refs: back_attend_body(base, *refs), outs, 'back_atten...  44.4 us
    pallas_call x11, Pallas kernels, product_sum(): pl.pallas_call(lambda *refs: product_body(runs, *refs), grid=(len(blocks)...  26.9 us
    pallas_call x2, Pallas kernels, shards(): whole_call(lambda *refs: back_mlp_body(base, *refs), outs, 'back_mlp', fu...  26.6 us
    unnamed x334, local copies, waits for them, and re-layouts  25.2 us
    pallas_call x2, Pallas kernels, forward_stage(): whole_call_smem(lambda *refs: up_body(base, *refs), 1, 9, outs, 'out_up',...  23.3 us
    pallas_call x1, Pallas kernels, shampoo(): pl.pallas_call(lambda *refs: shampoo_body(group, layout, *refs), grid=(co...  20.2 us
  transfers between devices with their start and end apart: 88, of which 30 were waited for; matrix products, arithmetic and copies ran while one was open for 17% of the time, Pallas kernels for 28%

profile of v5, /device:TPU:0, one launch (start us, length us, event | category | flops | bytes accessed | tf_op | source)
XLA Modules:
  0.0 585.8 jit_solution(13891055117371396490)
XLA Ops:
  2.7 5.7 prepare_tiles.1
  8.4 5.0 collective-permute-start.2
  14.0 2.5 constant_dynamic-slice_fusion.5
  26.9 2.9 collective-permute-start.5
  32.3 9.5 %collective-permute-done.1 = bf16[48,3456]{1,0:T(8,128)(2,1)} collective-permute-done((bf16[48,3456]{1,0:T(8,128)(2,1)S(1)}, bf16[48,3456]{1,0:T(8,128)(2,1)}, u32[]{:S(2)}, u32[]{:S(2)}) %collective-permute-start.1) | collective-permute-done | bytes 331808 | tf_op jit(solution)/shard_map/ppermute | solution.py:66
  46.2 2.5 collective-permute-start.10
  50.5 6.7 %collective-permute-done.10 = bf16[48,2688]{1,0:T(8,128)(2,1)S(1)} collective-permute-done((bf16[48,2688]{1,0:T(8,128)(2,1)S(1)}, bf16[48,2688]{1,0:T(8,128)(2,1)S(1)}, u32[]{:S(2)}, u32[]{:S(2)}) %collective-permute-start.10) | collective-permute-done | bytes 258080 | tf_op jit(solution)/shard_map/ppermute | solution.py:66
  57.2 11.1 %collective-permute-done.9 = bf16[48,2688]{1,0:T(8,128)(2,1)S(1)} collective-permute-done((bf16[48,2688]{1,0:T(8,128)(2,1)S(1)}, bf16[48,2688]{1,0:T(8,128)(2,1)S(1)}, u32[]{:S(2)}, u32[]{:S(2)}) %collective-permute-start.9) | collective-permute-done | bytes 258080 | tf_op jit(solution)/shard_map/ppermute | solution.py:66
  73.0 2.3 collective-permute-start.13
  75.3 9.0 %collective-permute-done.15 = bf16[48,3840]{1,0:T(8,128)(2,1)S(1)} collective-permute-done((bf16[48,3840]{1,0:T(8,128)(2,1)S(1)}, bf16[48,3840]{1,0:T(8,128)(2,1)S(1)}, u32[]{:S(2)}, u32[]{:S(2)}) %collective-permute-start.15) | collective-permute-done | bytes 368672 | tf_op jit(solution)/shard_map/ppermute | solution.py:66
  84.3 16.9 %collective-permute-done.14 = bf16[48,3840]{1,0:T(8,128)(2,1)S(1)} collective-permute-done((bf16[48,3840]{1,0:T(8,128)(2,1)S(1)}, bf16[48,3840]{1,0:T(8,128)(2,1)S(1)}, u32[]{:S(2)}, u32[]{:S(2)}) %collective-permute-start.14) | collective-permute-done | bytes 368672 | tf_op jit(solution)/shard_map/ppermute | solution.py:66
  103.1 5.1 assemble.3
  117.3 13.3 %embed_qkv.1 = (f32[416,768]{1,0:T(8,128)}, bf16[416,768]{1,0:T(8,128)(2,1)}, bf16[416,1152]{1,0:T(8,128)(2,1)}, bf16[416,1152]{1,0:T(8,128)(2,1)}, bf16[416,384...) custom-call(s32[2]{0:T(128)S(1)} %pad_add_fusion.refs_0_.places, ...), custom_call_target="tpu_custom_call" | custom-call | flops 122683392 | bytes 65536 | tf_op jit(solution)/shard_map/embed_qkv/pallas_call | solution.py:775
  130.6 11.8 %out_up.2 = (f32[416,768]{1,0:T(8,128)}, bf16[416,768]{1,0:T(8,128)(2,1)}, bf16[416,1536]{1,0:T(8,128)(2,1)}, bf16[416,1536]{1,0:T(8,128)(2,1)}, f32[416,1536]{1...) custom-call(s32[2]{0:T(128)S(1)} %pad_add_fusion.refs_0_.places, ...), custom_call_target="tpu_custom_call" | custom-call | flops 153354240 | bytes 65536 | tf_op jit(solution)/shard_map/out_up/pallas_call | solution.py:782
  142.4 4.9 collective-permute-done.16.refs_4_.refs_3_
  147.3 4.9 assemble.4
  156.9 3.8 collective-permute-done.27.refs_9_.refs_8_
  163.4 14.8 %down_qkv.1 = (f32[416,768]{1,0:T(8,128)}, bf16[416,768]{1,0:T(8,128)(2,1)S(1)}, bf16[416,1152]{1,0:T(8,128)(2,1)}, bf16[416,1152]{1,0:T(8,128)(2,1)}, bf16[416,...) custom-call(s32[2]{0:T(128)S(1)} %pad_add_fusion.refs_0_.places, ...), custom_call_target="tpu_custom_call" | custom-call | flops 214695936 | bytes 65536 | tf_op jit(solution)/shard_map/down_qkv/pallas_call | solution.py:792
  179.1 5.6 assemble.5
  185.7 5.2 collective-permute-done.28.refs_7_.refs_4_
  192.5 11.5 %out_up.3 = (f32[416,768]{1,0:T(8,128)}, bf16[416,768]{1,0:T(8,128)(2,1)}, bf16[416,1536]{1,0:T(8,128)(2,1)}, bf16[416,1536]{1,0:T(8,128)(2,1)}, f32[416,1536]{1...) custom-call(s32[2]{0:T(128)S(1)} %pad_add_fusion.refs_0_.places, ...), custom_call_target="tpu_custom_call" | custom-call | flops 153354240 | bytes 65536 | tf_op jit(solution)/shard_map/out_up/pallas_call | solution.py:782
  205.6 11.5 %down_head.1 = (bf16[416,768]{1,0:T(8,128)(2,1)}, bf16[416,384]{1,0:T(8,128)(2,1)S(1)}, bf16[416,384]{1,0:T(8,128)(2,1)}, f32[416,768]{1,0:T(8,128)}, bf16[416,7...) custom-call(s32[2]{0:T(128)S(1)} %pad_add_fusion.refs_0_.places, ...), custom_call_target="tpu_custom_call" | custom-call | flops 184025088 | bytes 65536 | tf_op jit(solution)/shard_map/down_head/pallas_call | solution.py:803
  219.5 13.3 %back_mlp.2 = (f32[416,768]{1,0:T(8,128)}, bf16[416,768]{1,0:T(8,128)(2,1)S(1)}, bf16[416,1536]{1,0:T(8,128)(2,1)}, bf16[416,1536]{1,0:T(8,128)(2,1)}, f32[8,768...) custom-call(f32[227,768]{1,0:T(8,128)} %fusion.4.vec.refs_1_.refs_2_.refs_0_, ...), custom_call_target="tpu_custom_call" | custom-call | flops 245366784 | bytes 65536 | tf_op jit(solution)/shard_map/back_mlp/pallas_call | solution.py:902
  233.0 3.7 product_sum.11
  239.5 4.2 product_sum.12
  251.6 21.9 %back_attend.2 = (f32[416,768]{1,0:T(8,128)}, bf16[416,768]{1,0:T(8,128)(2,1)S(1)}, bf16[416,1152]{1,0:T(8,128)(2,1)}, bf16[416,1152]{1,0:T(8,128)(2,1)}, f32[8,...) custom-call(f32[227,768]{1,0:T(8,128)} %fusion.4.vec.refs_1_.refs_2_.refs_0_, ...), custom_call_target="tpu_custom_call" | custom-call | flops 245366784 | bytes 65536 | tf_op jit(solution)/shard_map/back_attend/pallas_call | solution.py:918
  291.3 4.2 collective-permute-done.38
  295.5 4.1 collective-permute-done.39
  307.0 13.3 %back_mlp.3 = (f32[416,768]{1,0:T(8,128)}, bf16[416,768]{1,0:T(8,128)(2,1)S(1)}, bf16[416,1536]{1,0:T(8,128)(2,1)}, bf16[416,1536]{1,0:T(8,128)(2,1)}, f32[8,768...) custom-call(f32[227,768]{1,0:T(8,128)} %fusion.4.vec.refs_1_.refs_2_.refs_0_, ...), custom_call_target="tpu_custom_call" | custom-call | flops 245366784 | bytes 65536 | tf_op jit(solution)/shard_map/back_mlp/pallas_call | solution.py:902
  335.5 3.7 product_sum.17
  341.1 4.1 product_sum.18
  351.8 22.5 %back_attend.3 = (f32[416,768]{1,0:T(8,128)}, bf16[416,768]{1,0:T(8,128)(2,1)}, bf16[416,1152]{1,0:T(8,128)(2,1)}, bf16[416,1152]{1,0:T(8,128)(2,1)}, f32[8,768]...) custom-call(f32[227,768]{1,0:T(8,128)} %fusion.4.vec.refs_1_.refs_2_.refs_0_, ...), custom_call_target="tpu_custom_call" | custom-call | flops 245366784 | bytes 65536 | tf_op jit(solution)/shard_map/back_attend/pallas_call | solution.py:918
  375.6 2.6 multiply_reduce_fusion.1
  393.1 4.0 product_sum.19
  397.3 5.3 collective-permute-done.51
  414.0 13.1 %collective-permute-done.59 = f16[400,768]{1,0:T(8,128)(2,1)S(1)} collective-permute-done((f16[400,768]{1,0:T(8,128)(2,1)S(1)}, f16[400,768]{1,0:T(8,128)(2,1)S(1)}, u32[]{:S(2)}, u32[]{:S(2)}) %collective-permute-start.59) | collective-permute-done | bytes 614432 | tf_op jit(solution)/shard_map/ppermute | solution.py:66
  427.1 6.1 %collective-permute-done.58 = f16[400,1152]{1,0:T(8,128)(2,1)S(1)} collective-permute-done((f16[400,1152]{1,0:T(8,128)(2,1)S(1)}, f16[400,1152]{1,0:T(8,128)(2,1)S(1)}, u32[]{:S(2)}, u32[]{:S(2)}) %collective-permute-start.58) | collective-permute-done | bytes 921632 | tf_op jit(solution)/shard_map/ppermute | solution.py:66
  450.0 4.7 collective-permute-done.65
  467.9 7.2 %collective-permute-done.67 = f32[32,768]{1,0:T(8,128)S(1)} collective-permute-done((f32[32,768]{1,0:T(8,128)S(1)}, f32[32,768]{1,0:T(8,128)S(1)}, u32[]{:S(2)}, u32[]{:S(2)}) %collective-permute-start.67) | collective-permute-done | bytes 98336 | tf_op jit(solution)/shard_map/ppermute | solution.py:66
  477.2 2.9 collective-permute-start.77
  485.7 12.5 %collective-permute-done.74 = f32[32,768]{1,0:T(8,128)S(1)} collective-permute-done((f32[32,768]{1,0:T(8,128)S(1)}, f32[32,768]{1,0:T(8,128)S(1)}, u32[]{:S(2)}, u32[]{:S(2)}) %collective-permute-start.74) | collective-permute-done | bytes 98336 | tf_op jit(solution)/shard_map/ppermute | solution.py:66
  507.5 2.6 collective-permute-done.72
  523.5 2.7 collective-permute-done.80
  527.6 2.8 collective-permute-done.81
  538.7 2.4 collective-permute-start.83
  546.6 20.2 %shampoo.1 = (f32[48,96,96]{2,1,0:T(8,128)}, f32[48,96,96]{2,1,0:T(8,128)}, f32[48,96,96]{2,1,0:T(8,128)}, f32[48,96,96]{2,1,0:T(8,128)}, f32[48,96,96]{2,1,0:T(8,128)}) custom-call(s32[5,48]{1,0:T(8,128)S(1)} %stack.34.refs_0_, bf16[4,48,9984]{2,1,0:T(8,128)(2,1)} %get-tuple-element.618.refs_1_, f32[64,4992]{1,0:T(8,128)} %copy-done.82, ...), custom_call_target="tpu_custom_call" | custom-call | flops 127401984 | bytes 65536 | tf_op jit(solution)/shard_map/shampoo/pallas_call | solution.py:591
  566.9 3.4 multiply_bitcast_fusion
  580.9 3.3 multiply_subtract_fusion
  (766 shorter events, 216.7 us)
Async XLA Ops:
  8.4 23.9 %collective-permute-start.2 = (bf16[48,3456]{1,0:T(8,128)(2,1)S(1)}, bf16[48,3456]{1,0:T(8,128)(2,1)}, u32[]{:S(2)}, u32[]{:S(2)}) collective-permute-start(bf16[48,3456]{1,0:T(8,128)(2,1)S(1)} %get-tuple-element.320), channel_id=1, source_target_pairs={{0,3},{1,2},{2,1},{3,0},{4,7},{5,6},{6,5},{7,4},{8,11},{9,10},{10,... | collective-permute-start | bytes 995336 | tf_op jit(solution)/shard_map/ppermute | solution.py:66
  13.4 28.4 %collective-permute-start.1 = (bf16[48,3456]{1,0:T(8,128)(2,1)S(1)}, bf16[48,3456]{1,0:T(8,128)(2,1)}, u32[]{:S(2)}, u32[]{:S(2)}) collective-permute-start(bf16[48,3456]{1,0:T(8,128)(2,1)S(1)} %get-tuple-element.320), channel_id=1, source_target_pairs={{0,2},{1,3},{2,0},{3,1},{4,6},{5,7},{6,4},{7,5},{8,10},{9,11},{10,... | collective-permute-start | bytes 995336 | tf_op jit(solution)/shard_map/ppermute | solution.py:66
  13.4 28.4 %collective-permute-start = (bf16[48,3456]{1,0:T(8,128)(2,1)S(1)}, bf16[48,3456]{1,0:T(8,128)(2,1)}, u32[]{:S(2)}, u32[]{:S(2)}) collective-permute-start(bf16[48,3456]{1,0:T(8,128)(2,1)S(1)} %get-tuple-element.320), channel_id=1, source_target_pairs={{0,1},{1,0},{2,3},{3,2},{4,5},{5,4},{6,7},{7,6},{8,9},{9,8},{10,11... | collective-permute-start | bytes 995336 | tf_op jit(solution)/shard_map/ppermute | solution.py:66
  43.1 25.3 %collective-permute-start.6 = (bf16[144,3456]{1,0:T(8,128)(2,1)S(1)}, bf16[144,3456]{1,0:T(8,128)(2,1)S(1)}, u32[]{:S(2)}, u32[]{:S(2)}) collective-permute-start(bf16[144,3456]{1,0:T(8,128)(2,1)S(1)} %pad_maximum_fusion.7.refs_1_), channel_id=1, source_target_pairs={{0,8},{8,0},{16,24},{24,16},{1,9},{9,1},{17,25},{25,17},{2,10},{10... | collective-permute-start | bytes 2985992 | tf_op jit(solution)/shard_map/ppermute | solution.py:66
  44.6 23.8 %collective-permute-start.7 = (bf16[144,3456]{1,0:T(8,128)(2,1)S(1)}, bf16[144,3456]{1,0:T(8,128)(2,1)S(1)}, u32[]{:S(2)}, u32[]{:S(2)}) collective-permute-start(bf16[144,3456]{1,0:T(8,128)(2,1)S(1)} %pad_maximum_fusion.7.refs_1_), channel_id=1, source_target_pairs={{0,16},{8,24},{16,0},{24,8},{1,17},{9,25},{17,1},{25,9},{2,18},{10... | collective-permute-start | bytes 2985992 | tf_op jit(solution)/shard_map/ppermute | solution.py:66
  48.6 19.7 %collective-permute-start.9 = (bf16[48,2688]{1,0:T(8,128)(2,1)S(1)}, bf16[48,2688]{1,0:T(8,128)(2,1)S(1)}, u32[]{:S(2)}, u32[]{:S(2)}) collective-permute-start(bf16[48,2688]{1,0:T(8,128)(2,1)S(1)} %get-tuple-element.327), channel_id=1, source_target_pairs={{0,2},{1,3},{2,0},{3,1},{4,6},{5,7},{6,4},{7,5},{8,10},{9,11},{10,... | collective-permute-start | bytes 774152 | tf_op jit(solution)/shard_map/ppermute | solution.py:66
  48.6 19.7 %collective-permute-start.8 = (bf16[48,2688]{1,0:T(8,128)(2,1)S(1)}, bf16[48,2688]{1,0:T(8,128)(2,1)S(1)}, u32[]{:S(2)}, u32[]{:S(2)}) collective-permute-start(bf16[48,2688]{1,0:T(8,128)(2,1)S(1)} %get-tuple-element.327), channel_id=1, source_target_pairs={{0,1},{1,0},{2,3},{3,2},{4,5},{5,4},{6,7},{7,6},{8,9},{9,8},{10,11... | collective-permute-start | bytes 774152 | tf_op jit(solution)/shard_map/ppermute | solution.py:66
  69.7 31.6 %collective-permute-start.12 = (bf16[144,4480]{1,0:T(8,128)(2,1)S(1)}, bf16[144,4480]{1,0:T(8,128)(2,1)S(1)}, u32[]{:S(2)}, u32[]{:S(2)}) collective-permute-start(bf16[144,4480]{1,0:T(8,128)(2,1)S(1)} %pad_maximum_fusion.3), channel_id=1, source_target_pairs={{0,8},{8,0},{16,24},{24,16},{1,9},{9,1},{17,25},{25,17},{2,10},{10... | collective-permute-start | bytes 3870728 | tf_op jit(solution)/shard_map/ppermute | solution.py:66
  70.3 30.9 %collective-permute-start.11 = (bf16[144,4352]{1,0:T(8,128)(2,1)S(1)}, bf16[144,4352]{1,0:T(8,128)(2,1)S(1)}, u32[]{:S(2)}, u32[]{:S(2)}) collective-permute-start(bf16[144,4352]{1,0:T(8,128)(2,1)S(1)} %pad_maximum_fusion.4), channel_id=1, source_target_pairs={{0,16},{8,24},{16,0},{24,8},{1,17},{9,25},{17,1},{25,9},{2,18},{10... | collective-permute-start | bytes 3760136 | tf_op jit(solution)/shard_map/ppermute | solution.py:66
  73.0 28.2 %collective-permute-start.14 = (bf16[48,3840]{1,0:T(8,128)(2,1)S(1)}, bf16[48,3840]{1,0:T(8,128)(2,1)S(1)}, u32[]{:S(2)}, u32[]{:S(2)}) collective-permute-start(bf16[48,3840]{1,0:T(8,128)(2,1)S(1)} %get-tuple-element.333), channel_id=1, source_target_pairs={{0,2},{1,3},{2,0},{3,1},{4,6},{5,7},{6,4},{7,5},{8,10},{9,11},{10,... | collective-permute-start | bytes 1105928 | tf_op jit(solution)/shard_map/ppermute | solution.py:66
  73.0 28.2 %collective-permute-start.13 = (bf16[48,3840]{1,0:T(8,128)(2,1)S(1)}, bf16[48,3840]{1,0:T(8,128)(2,1)S(1)}, u32[]{:S(2)}, u32[]{:S(2)}) collective-permute-start(bf16[48,3840]{1,0:T(8,128)(2,1)S(1)} %get-tuple-element.333), channel_id=1, source_target_pairs={{0,1},{1,0},{2,3},{3,2},{4,5},{5,4},{6,7},{7,6},{8,9},{9,8},{10,11... | collective-permute-start | bytes 1105928 | tf_op jit(solution)/shard_map/ppermute | solution.py:66
  108.2 22.4 %collective-permute-start.21 = (bf16[768,1536]{1,0:T(8,128)(2,1)}, bf16[768,1536]{1,0:T(8,128)(2,1)}, u32[]{:S(2)}, u32[]{:S(2)}) collective-permute-start(bf16[768,1536]{1,0:T(8,128)(2,1)} %get-tuple-element.356.refs_8_.refs_7_), channel_id=1, source_target_pairs={{0,4},{4,0},{1,5},{5,1},{2,6},{6,2},{3,7},{7,3},{8,12},{12,8},{9,1... | collective-permute-start | bytes 7077896 | tf_op jit(solution)/shard_map/ppermute | solution.py:66
  109.5 37.7 %collective-permute-start.17 = (bf16[144,5248]{1,0:T(8,128)(2,1)}, bf16[144,5248]{1,0:T(8,128)(2,1)}, u32[]{:S(2)}, u32[]{:S(2)}) collective-permute-start(bf16[144,5248]{1,0:T(8,128)(2,1)} %pad_maximum_fusion.1), channel_id=1, source_target_pairs={{0,8},{8,0},{16,24},{24,16},{1,9},{9,1},{17,25},{25,17},{2,10},{10... | collective-permute-start | bytes 4534280 | tf_op jit(solution)/shard_map/ppermute | solution.py:66
  112.5 34.8 %collective-permute-start.16 = (bf16[144,5120]{1,0:T(8,128)(2,1)}, bf16[144,5120]{1,0:T(8,128)(2,1)}, u32[]{:S(2)}, u32[]{:S(2)}) collective-permute-start(bf16[144,5120]{1,0:T(8,128)(2,1)} %pad_maximum_fusion.2), channel_id=1, source_target_pairs={{0,16},{8,24},{16,0},{24,8},{1,17},{9,25},{17,1},{25,9},{2,18},{10... | collective-permute-start | bytes 4423688 | tf_op jit(solution)/shard_map/ppermute | solution.py:66
  152.7 26.5 %collective-permute-start.25 = (bf16[416,2304]{1,0:T(8,128)(2,1)}, bf16[416,2304]{1,0:T(8,128)(2,1)S(1)}, u32[]{:S(2)}, u32[]{:S(2)}) collective-permute-start(bf16[416,2304]{1,0:T(8,128)(2,1)} %get-tuple-element.378), channel_id=1, source_target_pairs={{0,4},{4,0},{1,5},{5,1},{2,6},{6,2},{3,7},{7,3},{8,12},{12,8},{9,1... | collective-permute-start | bytes 5750792 | tf_op jit(solution)/shard_map/ppermute | solution.py:66
  152.7 26.4 %collective-permute-start.24 = (bf16[416,1152]{1,0:T(8,128)(2,1)S(1)}, bf16[416,1152]{1,0:T(8,128)(2,1)S(1)}, u32[]{:S(2)}, u32[]{:S(2)}) collective-permute-start(bf16[416,1152]{1,0:T(8,128)(2,1)S(1)} %copy-done.157), channel_id=1, source_target_pairs={{0,4},{4,0},{1,5},{5,1},{2,6},{6,2},{3,7},{7,3},{8,12},{12,8},{9,1... | collective-permute-start | bytes 2875400 | tf_op jit(solution)/shard_map/ppermute | solution.py:66
  154.3 24.8 %collective-permute-start.22 = (bf16[144,1920]{1,0:T(8,128)(2,1)S(1)}, bf16[144,1920]{1,0:T(8,128)(2,1)S(1)}, u32[]{:S(2)}, u32[]{:S(2)}) collective-permute-start(bf16[144,1920]{1,0:T(8,128)(2,1)S(1)} %slice.385), channel_id=1, source_target_pairs={{0,16},{8,24},{16,0},{24,8},{1,17},{9,25},{17,1},{25,9},{2,18},{10... | collective-permute-start | bytes 1658888 | tf_op jit(solution)/shard_map/ppermute | solution.py:66
  160.8 18.3 %collective-permute-start.23 = (bf16[144,1920]{1,0:T(8,128)(2,1)S(1)}, bf16[144,1920]{1,0:T(8,128)(2,1)S(1)}, u32[]{:S(2)}, u32[]{:S(2)}) collective-permute-start(bf16[144,1920]{1,0:T(8,128)(2,1)S(1)} %slice.386), channel_id=1, source_target_pairs={{0,8},{8,0},{16,24},{24,16},{1,9},{9,1},{17,25},{25,17},{2,10},{10... | collective-permute-start | bytes 1658888 | tf_op jit(solution)/shard_map/ppermute | solution.py:66
  184.8 19.1 %collective-permute-start.30 = (bf16[768,1536]{1,0:T(8,128)(2,1)}, bf16[768,1536]{1,0:T(8,128)(2,1)S(1)}, u32[]{:S(2)}, u32[]{:S(2)}) collective-permute-start(bf16[768,1536]{1,0:T(8,128)(2,1)} %get-tuple-element.407.refs_7_.refs_3_), channel_id=1, source_target_pairs={{0,4},{4,0},{1,5},{5,1},{2,6},{6,2},{3,7},{7,3},{8,12},{12,8},{9,1... | collective-permute-start | bytes 7077896 | tf_op jit(solution)/shard_map/ppermute | solution.py:66
  185.4 18.6 %collective-permute-start.31 = (bf16[768,384]{1,0:T(8,128)(2,1)}, bf16[768,384]{1,0:T(8,128)(2,1)S(1)}, u32[]{:S(2)}, u32[]{:S(2)}) collective-permute-start(bf16[768,384]{1,0:T(8,128)(2,1)} %get-tuple-element.408.refs_9_), channel_id=1, source_target_pairs={{0,4},{4,0},{1,5},{5,1},{2,6},{6,2},{3,7},{7,3},{8,12},{12,8},{9,1... | collective-permute-start | bytes 1769480 | tf_op jit(solution)/shard_map/ppermute | solution.py:66
  245.5 29.6 %collective-permute-start.35 = (f16[400,1536]{1,0:T(8,128)(2,1)}, f16[400,1536]{1,0:T(8,128)(2,1)}, u32[]{:S(2)}, u32[]{:S(2)}) collective-permute-start(f16[400,1536]{1,0:T(8,128)(2,1)} %convert_element_type.320), channel_id=1, source_target_pairs={{0,8},{8,0},{16,24},{24,16},{1,9},{9,1},{17,25},{25,17},{2,10},{10... | collective-permute-start | bytes 3686408 | tf_op jit(solution)/shard_map/ppermute | solution.py:66
  246.4 29.3 %collective-permute-start.36 = (f16[400,1536]{1,0:T(8,128)(2,1)}, f16[400,1536]{1,0:T(8,128)(2,1)}, u32[]{:S(2)}, u32[]{:S(2)}) collective-permute-start(f16[400,1536]{1,0:T(8,128)(2,1)} %convert_element_type.321), channel_id=1, source_target_pairs={{0,16},{8,24},{16,0},{24,8},{1,17},{9,25},{17,1},{25,9},{2,18},{10... | collective-permute-start | bytes 3686408 | tf_op jit(solution)/shard_map/ppermute | solution.py:66
  278.6 16.9 %collective-permute-start.38 = (f16[208,1536]{1,0:T(8,128)(2,1)S(1)}, f16[208,1536]{1,0:T(8,128)(2,1)S(1)}, u32[]{:S(2)}, u32[]{:S(2)}) collective-permute-start(f16[208,1536]{1,0:T(8,128)(2,1)S(1)} %pad_maximum_fusion.12), channel_id=1, source_target_pairs={{0,16},{8,24},{16,0},{24,8},{1,17},{9,25},{17,1},{25,9},{2,18},{10... | collective-permute-start | bytes 1916936 | tf_op jit(solution)/shard_map/ppermute | solution.py:66
  299.7 22.1 %collective-permute-start.43 = (f16[400,1152]{1,0:T(8,128)(2,1)}, f16[400,1152]{1,0:T(8,128)(2,1)}, u32[]{:S(2)}, u32[]{:S(2)}) collective-permute-start(f16[400,1152]{1,0:T(8,128)(2,1)} %pad_maximum_fusion.8), channel_id=1, source_target_pairs={{0,16},{8,24},{16,0},{24,8},{1,17},{9,25},{17,1},{25,9},{2,18},{10... | collective-permute-start | bytes 2764808 | tf_op jit(solution)/shard_map/ppermute | solution.py:66
  303.5 16.8 %collective-permute-start.41 = (f16[112,3072]{1,0:T(8,128)(2,1)}, f16[112,3072]{1,0:T(8,128)(2,1)}, u32[]{:S(2)}, u32[]{:S(2)}) collective-permute-start(f16[112,3072]{1,0:T(8,128)(2,1)} %pad_maximum_fusion.10), channel_id=1, source_target_pairs={{0,1},{1,0},{2,3},{3,2},{4,5},{5,4},{6,7},{7,6},{8,9},{9,8},{10,11... | collective-permute-start | bytes 2064392 | tf_op jit(solution)/shard_map/ppermute | solution.py:66
  321.9 18.5 %collective-permute-start.44 = (bf16[416,2304]{1,0:T(8,128)(2,1)}, bf16[416,2304]{1,0:T(8,128)(2,1)S(1)}, u32[]{:S(2)}, u32[]{:S(2)}) collective-permute-start(bf16[416,2304]{1,0:T(8,128)(2,1)} %get-tuple-element.490), channel_id=1, source_target_pairs={{0,4},{4,0},{1,5},{5,1},{2,6},{6,2},{3,7},{7,3},{8,12},{12,8},{9,1... | collective-permute-start | bytes 5750792 | tf_op jit(solution)/shard_map/ppermute | solution.py:66
  324.8 21.6 %collective-permute-start.45 = (f16[64,3072]{1,0:T(8,128)(2,1)S(1)}, f16[64,3072]{1,0:T(8,128)(2,1)S(1)}, u32[]{:S(2)}, u32[]{:S(2)}) collective-permute-start(f16[64,3072]{1,0:T(8,128)(2,1)S(1)} %pad_maximum_fusion.24), channel_id=1, source_target_pairs={{0,2},{1,3},{2,0},{3,1},{4,6},{5,7},{6,4},{7,5},{8,10},{9,11},{10,... | collective-permute-start | bytes 1179656 | tf_op jit(solution)/shard_map/ppermute | solution.py:66
  328.3 18.1 %collective-permute-start.47 = (f16[208,1152]{1,0:T(8,128)(2,1)S(1)}, f16[208,1152]{1,0:T(8,128)(2,1)S(1)}, u32[]{:S(2)}, u32[]{:S(2)}) collective-permute-start(f16[208,1152]{1,0:T(8,128)(2,1)S(1)} %pad_maximum_fusion.20), channel_id=1, source_target_pairs={{0,8},{8,0},{16,24},{24,16},{1,9},{9,1},{17,25},{25,17},{2,10},{10... | collective-permute-start | bytes 1437704 | tf_op jit(solution)/shard_map/ppermute | solution.py:66
  347.4 30.8 %collective-permute-start.48 = (f16[112,1920]{1,0:T(8,128)(2,1)S(1)}, f16[112,1920]{1,0:T(8,128)(2,1)S(1)}, u32[]{:S(2)}, u32[]{:S(2)}) collective-permute-start(f16[112,1920]{1,0:T(8,128)(2,1)S(1)} %pad_maximum_fusion.22), channel_id=1, source_target_pairs={{0,1},{1,0},{2,3},{3,2},{4,5},{5,4},{6,7},{7,6},{8,9},{9,8},{10,11... | collective-permute-start | bytes 1290248 | tf_op jit(solution)/shard_map/ppermute | solution.py:66
  348.1 30.0 %collective-permute-start.49 = (f16[400,1536]{1,0:T(8,128)(2,1)}, f16[400,1536]{1,0:T(8,128)(2,1)}, u32[]{:S(2)}, u32[]{:S(2)}) collective-permute-start(f16[400,1536]{1,0:T(8,128)(2,1)} %convert_element_type.341), channel_id=1, source_target_pairs={{0,8},{8,0},{16,24},{24,16},{1,9},{9,1},{17,25},{25,17},{2,10},{10... | collective-permute-start | bytes 3686408 | tf_op jit(solution)/shard_map/ppermute | solution.py:66
  349.0 29.2 %collective-permute-start.50 = (f16[400,1536]{1,0:T(8,128)(2,1)}, f16[400,1536]{1,0:T(8,128)(2,1)}, u32[]{:S(2)}, u32[]{:S(2)}) collective-permute-start(f16[400,1536]{1,0:T(8,128)(2,1)} %convert_element_type.342), channel_id=1, source_target_pairs={{0,16},{8,24},{16,0},{24,8},{1,17},{9,25},{17,1},{25,9},{2,18},{10... | collective-permute-start | bytes 3686408 | tf_op jit(solution)/shard_map/ppermute | solution.py:66
  383.0 19.6 %collective-permute-start.52 = (f16[208,1536]{1,0:T(8,128)(2,1)S(1)}, f16[208,1536]{1,0:T(8,128)(2,1)S(1)}, u32[]{:S(2)}, u32[]{:S(2)}) collective-permute-start(f16[208,1536]{1,0:T(8,128)(2,1)S(1)} %pad_maximum_fusion.14), channel_id=1, source_target_pairs={{0,16},{8,24},{16,0},{24,8},{1,17},{9,25},{17,1},{25,9},{2,18},{10... | collective-permute-start | bytes 1916936 | tf_op jit(solution)/shard_map/ppermute | solution.py:66
  386.4 16.8 %collective-permute-start.53 = (f16[208,1536]{1,0:T(8,128)(2,1)S(1)}, f16[208,1536]{1,0:T(8,128)(2,1)S(1)}, u32[]{:S(2)}, u32[]{:S(2)}) collective-permute-start(f16[208,1536]{1,0:T(8,128)(2,1)S(1)} %pad_maximum_fusion.15), channel_id=1, source_target_pairs={{0,8},{8,0},{16,24},{24,16},{1,9},{9,1},{17,25},{25,17},{2,10},{10... | collective-permute-start | bytes 1916936 | tf_op jit(solution)/shard_map/ppermute | solution.py:66
  408.8 18.3 %collective-permute-start.57 = (f16[112,3072]{1,0:T(8,128)(2,1)S(1)}, f16[112,3072]{1,0:T(8,128)(2,1)S(1)}, u32[]{:S(2)}, u32[]{:S(2)}) collective-permute-start(f16[112,3072]{1,0:T(8,128)(2,1)S(1)} %pad_maximum_fusion.11), channel_id=1, source_target_pairs={{0,1},{1,0},{2,3},{3,2},{4,5},{5,4},{6,7},{7,6},{8,9},{9,8},{10,11... | collective-permute-start | bytes 2064392 | tf_op jit(solution)/shard_map/ppermute | solution.py:66
  410.6 22.6 %collective-permute-start.58 = (f16[400,1152]{1,0:T(8,128)(2,1)S(1)}, f16[400,1152]{1,0:T(8,128)(2,1)S(1)}, u32[]{:S(2)}, u32[]{:S(2)}) collective-permute-start(f16[400,1152]{1,0:T(8,128)(2,1)S(1)} %convert_element_type.357), channel_id=1, source_target_pairs={{0,8},{8,0},{16,24},{24,16},{1,9},{9,1},{17,25},{25,17},{2,10},{10... | collective-permute-start | bytes 2764808 | tf_op jit(solution)/shard_map/ppermute | solution.py:66
  438.4 19.1 %collective-permute-start.63 = (f16[64,3072]{1,0:T(8,128)(2,1)}, f16[64,3072]{1,0:T(8,128)(2,1)}, u32[]{:S(2)}, u32[]{:S(2)}) collective-permute-start(f16[64,3072]{1,0:T(8,128)(2,1)} %pad_maximum_fusion.25), channel_id=1, source_target_pairs={{0,2},{1,3},{2,0},{3,1},{4,6},{5,7},{6,4},{7,5},{8,10},{9,11},{10,... | collective-permute-start | bytes 1179656 | tf_op jit(solution)/shard_map/ppermute | solution.py:66
  447.5 28.4 %collective-permute-start.68 = (f16[64,4992]{1,0:T(8,128)(2,1)}, f16[64,4992]{1,0:T(8,128)(2,1)S(1)}, u32[]{:S(2)}, u32[]{:S(2)}) collective-permute-start(f16[64,4992]{1,0:T(8,128)(2,1)} %pad_maximum_fusion.16), channel_id=1, source_target_pairs={{0,8},{8,0},{16,24},{24,16},{1,9},{9,1},{17,25},{25,17},{2,10},{10... | collective-permute-start | bytes 1916936 | tf_op jit(solution)/shard_map/ppermute | solution.py:66
  448.4 28.8 %collective-permute-start.69 = (f16[64,4992]{1,0:T(8,128)(2,1)}, f16[64,4992]{1,0:T(8,128)(2,1)S(1)}, u32[]{:S(2)}, u32[]{:S(2)}) collective-permute-start(f16[64,4992]{1,0:T(8,128)(2,1)} %pad_maximum_fusion.16), channel_id=1, source_target_pairs={{0,16},{8,24},{16,0},{24,8},{1,17},{9,25},{17,1},{25,9},{2,18},{10... | collective-permute-start | bytes 1916936 | tf_op jit(solution)/shard_map/ppermute | solution.py:66
  454.8 27.3 %collective-permute-start.70 = (f16[64,4992]{1,0:T(8,128)(2,1)}, f16[64,4992]{1,0:T(8,128)(2,1)S(1)}, u32[]{:S(2)}, u32[]{:S(2)}) collective-permute-start(f16[64,4992]{1,0:T(8,128)(2,1)} %pad_maximum_fusion.16), channel_id=1, source_target_pairs={{0,24},{8,16},{16,8},{24,0},{1,25},{9,17},{17,9},{25,1},{2,26},{10... | collective-permute-start | bytes 1916936 | tf_op jit(solution)/shard_map/ppermute | solution.py:66
  461.8 20.3 %collective-permute-start.71 = (f16[112,1920]{1,0:T(8,128)(2,1)S(1)}, f16[112,1920]{1,0:T(8,128)(2,1)S(1)}, u32[]{:S(2)}, u32[]{:S(2)}) collective-permute-start(f16[112,1920]{1,0:T(8,128)(2,1)S(1)} %pad_maximum_fusion.23), channel_id=1, source_target_pairs={{0,1},{1,0},{2,3},{3,2},{4,5},{5,4},{6,7},{7,6},{8,9},{9,8},{10,11... | collective-permute-start | bytes 1290248 | tf_op jit(solution)/shard_map/ppermute | solution.py:66
  475.1 36.8 %collective-permute-start.75 = (f16[64,3072]{1,0:T(8,128)(2,1)}, f16[64,3072]{1,0:T(8,128)(2,1)}, u32[]{:S(2)}, u32[]{:S(2)}) collective-permute-start(f16[64,3072]{1,0:T(8,128)(2,1)} %pad_maximum_fusion.27), channel_id=1, source_target_pairs={{0,8},{8,0},{16,24},{24,16},{1,9},{9,1},{17,25},{25,17},{2,10},{10... | collective-permute-start | bytes 1179656 | tf_op jit(solution)/shard_map/ppermute | solution.py:66
  475.9 35.9 %collective-permute-start.76 = (f16[64,3072]{1,0:T(8,128)(2,1)}, f16[64,3072]{1,0:T(8,128)(2,1)}, u32[]{:S(2)}, u32[]{:S(2)}) collective-permute-start(f16[64,3072]{1,0:T(8,128)(2,1)} %pad_maximum_fusion.27), channel_id=1, source_target_pairs={{0,16},{8,24},{16,0},{24,8},{1,17},{9,25},{17,1},{25,9},{2,18},{10... | collective-permute-start | bytes 1179656 | tf_op jit(solution)/shard_map/ppermute | solution.py:66
  477.2 34.6 %collective-permute-start.77 = (f16[64,3072]{1,0:T(8,128)(2,1)}, f16[64,3072]{1,0:T(8,128)(2,1)}, u32[]{:S(2)}, u32[]{:S(2)}) collective-permute-start(f16[64,3072]{1,0:T(8,128)(2,1)} %pad_maximum_fusion.27), channel_id=1, source_target_pairs={{0,24},{8,16},{16,8},{24,0},{1,25},{9,17},{17,9},{25,1},{2,26},{10... | collective-permute-start | bytes 1179656 | tf_op jit(solution)/shard_map/ppermute | solution.py:66
  484.1 21.3 %collective-permute-start.73 = (f32[32,768]{1,0:T(8,128)S(1)}, f32[32,768]{1,0:T(8,128)}, u32[]{:S(2)}, u32[]{:S(2)}) collective-permute-start(f32[32,768]{1,0:T(8,128)S(1)} %add.985), channel_id=1, source_target_pairs={{0,16},{8,24},{16,0},{24,8},{1,17},{9,25},{17,1},{25,9},{2,18},{10... | collective-permute-start | bytes 294920 | tf_op jit(solution)/shard_map/ppermute | solution.py:66
  513.9 30.6 %collective-permute-start.85 = (f16[64,1920]{1,0:T(8,128)(2,1)S(1)}, f16[64,1920]{1,0:T(8,128)(2,1)S(1)}, u32[]{:S(2)}, u32[]{:S(2)}) collective-permute-start(f16[64,1920]{1,0:T(8,128)(2,1)S(1)} %pad_maximum_fusion.34), channel_id=1, source_target_pairs={{0,8},{8,0},{16,24},{24,16},{1,9},{9,1},{17,25},{25,17},{2,10},{10... | collective-permute-start | bytes 737288 | tf_op jit(solution)/shard_map/ppermute | solution.py:66
  514.8 29.7 %collective-permute-start.86 = (f16[64,1920]{1,0:T(8,128)(2,1)S(1)}, f16[64,1920]{1,0:T(8,128)(2,1)}, u32[]{:S(2)}, u32[]{:S(2)}) collective-permute-start(f16[64,1920]{1,0:T(8,128)(2,1)S(1)} %pad_maximum_fusion.34), channel_id=1, source_target_pairs={{0,16},{8,24},{16,0},{24,8},{1,17},{9,25},{17,1},{25,9},{2,18},{10... | collective-permute-start | bytes 737288 | tf_op jit(solution)/shard_map/ppermute | solution.py:66
  515.4 29.1 %collective-permute-start.87 = (f16[64,1920]{1,0:T(8,128)(2,1)S(1)}, f16[64,1920]{1,0:T(8,128)(2,1)}, u32[]{:S(2)}, u32[]{:S(2)}) collective-permute-start(f16[64,1920]{1,0:T(8,128)(2,1)S(1)} %pad_maximum_fusion.34), channel_id=1, source_target_pairs={{0,24},{8,16},{16,8},{24,0},{1,25},{9,17},{17,9},{25,1},{2,26},{10... | collective-permute-start | bytes 737288 | tf_op jit(solution)/shard_map/ppermute | solution.py:66
  519.6 61.2 %collective-permute-start.84 = (f32[128,768]{1,0:T(8,128)}, f32[128,768]{1,0:T(8,128)}, u32[]{:S(2)}, u32[]{:S(2)}) collective-permute-start(f32[128,768]{1,0:T(8,128)} %pad_maximum_fusion.26), channel_id=1, source_target_pairs={{0,4},{4,0},{1,5},{5,1},{2,6},{6,2},{3,7},{7,3},{8,12},{12,8},{9,1... | collective-permute-start | bytes 1179656 | tf_op jit(solution)/shard_map/ppermute | solution.py:66
  (202 other events, 1855.1 us)
